TPU v7x, 32 devices: a whole 2x2x4 slice. The times are simulated.
32 devices in a mesh: section: 2 (over x), tensor: 2 (over y), ctx: 8 (over z, core).
Axes of the slice: x: 2, y: 2, z: 4, core: 2. Of those that a mesh axis runs over, the one named last changes fastest.
Arguments:
- block_input: bfloat16 [4, 1024, 1536], P(None, 'ctx'), may hold values from -6 to 6
- positions: int32 [4, 1024], P(None, 'ctx'), may hold values from 0 to 1023, as said below
- cotangent: bfloat16 [4, 1024, 1536], P(None, 'ctx'), may hold values from -6 to 6
- norm_attn: bfloat16 [2, 1536], P('section', 'ctx'), may hold values from 0.5 to 1.5
- w_qkv: bfloat16 [2, 1536, 2, 1024], P('section', 'ctx', 'tensor'), may hold values from -0.15625 to 0.15625
- b_qkv: bfloat16 [2, 2, 1024], P('section', 'tensor', 'ctx'), may hold values from -3 to 3
- w_out: bfloat16 [2, 2, 768, 1536], P('section', 'tensor', 'ctx'), may hold values from -3.5 to 3.5
- norm_mlp: bfloat16 [2, 1536], P('section', 'ctx'), may hold values from 0.5 to 1.5
- w_gate_up: bfloat16 [2, 1536, 2, 8960], P('section', 'ctx', None, 'tensor'), may hold values from -0.15625 to 0.15625
- w_down: bfloat16 [2, 8960, 1536], P('section', ('tensor', 'ctx')), may hold values from -0.125 to 0.125
Outputs:
- section_output: bfloat16 [2, 4, 1024, 1536], P('section', None, 'ctx')
- input_grad: bfloat16 [2, 4, 1024, 1536], P('section', None, 'ctx')
- grad_norm_attn: float32 [2, 1536], P('section', 'ctx')
- grad_w_qkv: float32 [2, 1536, 2, 1024], P('section', 'ctx', 'tensor')
- grad_b_qk: float32 [2, 2, 896], P('section', 'tensor', 'ctx')
- grad_b_v: float32 [2, 2, 128], P('section', 'tensor', 'ctx')
- grad_w_out: float32 [2, 2, 768, 1536], P('section', 'tensor', 'ctx')
- grad_norm_mlp: float32 [2, 1536], P('section', 'ctx')
- grad_w_gate_up: float32 [2, 1536, 2, 8960], P('section', 'ctx', None, 'tensor')
- grad_w_down: float32 [2, 8960, 1536], P('section', ('tensor', 'ctx'))
Inputs may be any that keep to these rules, and one draw needn't show every extreme that they name: In every micro-batch each position of 0 to 1023 appears once; the 128 tokens of one index of ctx are two runs of 64 consecutive positions in rising order, sequence blocks b and 15 - b of size 64, with b differing between devices.
All inputs are finite; a program needn't handle non-finite values.
Results may differ from a plain program's by a relative error of at most 0.04.
Values may be sent and summed in bfloat16 or wider, within the bound.
A program may use at most 320 MiB of HBM per device.

v0:
```python
import math

import jax
import jax.numpy as jnp
from jax import lax
from jax.sharding import PartitionSpec as P

HD = 128


EPSILON = 1e-06
ROPE_BASE = 1000000.0
CONTRACT_ROWS = (((0,), (0,)), ((), ()))
CONTRACT_LAST = (((1,), (1,)), ((), ()))


def from_behind(block, axis, distance):
    devices = range(lax.axis_size(axis))
    route = [(i - distance, i) for i in devices if i - distance in devices]
    return lax.ppermute(block, axis, route)


def angles(positions, head_dim):
    half_dim = head_dim // 2
    frequency = ROPE_BASE ** (-(jnp.arange(half_dim, dtype=jnp.float32) * 2.0) / head_dim)
    phases = positions.astype(jnp.float32)[:, None] * frequency[None, :]
    phases = jnp.concatenate([phases, phases], axis=-1)
    return (jnp.cos(phases), jnp.sin(phases))


def rotate(values, cosine_table, sine_table):
    half_dim = values.shape[-1] // 2
    turned = jnp.concatenate([-values[..., half_dim:], values[..., :half_dim]], axis=-1)
    return values * cosine_table + turned * sine_table


def unrotate(grads_in, cosine_table, sine_table):
    half_dim = grads_in.shape[-1] // 2
    twisted = grads_in * sine_table
    turned = jnp.concatenate([twisted[..., half_dim:], -twisted[..., :half_dim]], axis=-1)
    return grads_in * cosine_table + turned


def tensor_total(partial_value):
    return lax.psum(partial_value.astype(jnp.bfloat16), "tensor").astype(jnp.float32)


def unpack(gathered):
    gain_attn, qkv_full, bias_full, out_full, gain_mlp, expand_full, reduce_full = gathered
    return (
        gain_attn[0],
        qkv_full[0, :, 0, :],
        bias_full[0, 0],
        out_full[0, 0],
        gain_mlp[0],
        expand_full[0],
        reduce_full[0],
    )


def norm_backward(values, inv_root, gain_row, grad_normed):
    normal = values * inv_root
    gain_grad = jnp.sum(grad_normed * normal, axis=0)
    scaled = grad_normed * gain_row
    return (
        inv_root * (scaled - normal * jnp.mean(scaled * normal, axis=-1, keepdims=True)),
        gain_grad,
    )


def score_block(query_rows, query_pos, key_block, block_pos, factor):
    raw_scores = lax.dot_general(
        query_rows, key_block, CONTRACT_LAST, preferred_element_type=jnp.float32
    )
    return jnp.where(query_pos[:, None] >= block_pos[None, :], raw_scores * factor, -1e30)


def split_blocks(kv_all, pos_all, head_dim):
    key_count = kv_all.shape[0]
    block_size = min(512, key_count)
    kv_blocks = kv_all.reshape(key_count // block_size, block_size, 2 * head_dim)
    pos_blocks = pos_all.reshape(key_count // block_size, block_size)
    return (kv_blocks, pos_blocks)


def attention_forward(query_rows, query_pos, kv_all, pos_all):
    head_dim = query_rows.shape[1]
    row_count = query_rows.shape[0]
    factor = 1.0 / math.sqrt(head_dim)
    kv_blocks, pos_blocks = split_blocks(kv_all, pos_all, head_dim)

    def max_step(state_pair, inputs):
        running, summed = state_pair
        kv_block, block_pos = inputs
        scores = score_block(query_rows, query_pos, kv_block[:, :head_dim], block_pos, factor)
        newest = jnp.maximum(running, jnp.max(scores, axis=1))
        summed = summed * jnp.exp(running - newest) + jnp.sum(
            jnp.exp(scores - newest[:, None]), axis=1
        )
        return ((newest, summed), None)

    initial = (jnp.full((row_count,), -1e30, jnp.float32), jnp.zeros((row_count,), jnp.float32))
    (running, summed), unused = lax.scan(max_step, initial, (kv_blocks, pos_blocks))
    log_total = running + jnp.log(summed)

    def value_step(accumulated, inputs):
        kv_block, block_pos = inputs
        scores = score_block(query_rows, query_pos, kv_block[:, :head_dim], block_pos, factor)
        weights_low = jnp.exp(scores - log_total[:, None]).astype(jnp.bfloat16)
        return (
            accumulated
            + jnp.dot(weights_low, kv_block[:, head_dim:], preferred_element_type=jnp.float32),
            None,
        )

    accumulated, unused = lax.scan(
        value_step, jnp.zeros((row_count, head_dim), jnp.float32), (kv_blocks, pos_blocks)
    )
    return (accumulated, log_total)


def attention_backward(query_rows, query_pos, kv_all, pos_all, log_total, grad_rows, row_delta):
    head_dim = query_rows.shape[1]
    factor = 1.0 / math.sqrt(head_dim)
    kv_blocks, pos_blocks = split_blocks(kv_all, pos_all, head_dim)

    def grad_step(grad_query, inputs):
        kv_block, block_pos = inputs
        key_block = kv_block[:, :head_dim]
        value_block = kv_block[:, head_dim:]
        scores = score_block(query_rows, query_pos, key_block, block_pos, factor)
        weights_full = jnp.exp(scores - log_total[:, None])
        grad_probs = lax.dot_general(
            grad_rows, value_block, CONTRACT_LAST, preferred_element_type=jnp.float32
        )
        grad_scores = (weights_full * (grad_probs - row_delta[:, None]) * factor).astype(
            jnp.bfloat16
        )
        grad_query = grad_query + jnp.dot(
            grad_scores, key_block, preferred_element_type=jnp.float32
        )
        grad_keys = lax.dot_general(
            grad_scores, query_rows, CONTRACT_ROWS, preferred_element_type=jnp.float32
        )
        grad_values = lax.dot_general(
            weights_full.astype(jnp.bfloat16),
            grad_rows,
            CONTRACT_ROWS,
            preferred_element_type=jnp.float32,
        )
        return (grad_query, jnp.concatenate([grad_keys, grad_values], axis=1))

    grad_query, grad_pairs = lax.scan(
        grad_step, jnp.zeros(query_rows.shape, jnp.float32), (kv_blocks, pos_blocks)
    )
    return (grad_query, grad_pairs.reshape(kv_all.shape[0], 2 * head_dim))


def layer_forward(values, weights, pos_local, pos_all):
    gain_attn, w_mixed, bias_mixed, w_project, gain_mlp, w_expand, w_reduce = weights
    tok_count = values.shape[0]
    query_width = w_project.shape[0]
    head_dim = (w_mixed.shape[1] - query_width) // 2
    head_count = query_width // head_dim
    cosine_table, sine_table = angles(pos_local, head_dim)
    scale_attn = lax.rsqrt(jnp.mean(values * values, axis=-1, keepdims=True) + EPSILON)
    normed = (values * scale_attn * gain_attn).astype(jnp.bfloat16)
    mixed_proj = jnp.dot(normed, w_mixed, preferred_element_type=jnp.float32) + bias_mixed
    queries = rotate(
        mixed_proj[:, :query_width].reshape(tok_count, head_count, head_dim),
        cosine_table[:, None, :],
        sine_table[:, None, :],
    )
    query_rows = queries.astype(jnp.bfloat16).reshape(tok_count * head_count, head_dim)
    keys_local = rotate(
        mixed_proj[:, query_width : query_width + head_dim], cosine_table, sine_table
    )
    kv_local = jnp.concatenate(
        [keys_local, mixed_proj[:, query_width + head_dim :]], axis=1
    ).astype(jnp.bfloat16)
    kv_all = lax.all_gather(kv_local, "ctx", axis=0, tiled=True)
    query_pos = jnp.repeat(pos_local, head_count)
    accumulated, log_total = attention_forward(query_rows, query_pos, kv_all, pos_all)
    attended = accumulated.astype(jnp.bfloat16).reshape(tok_count, query_width)
    middle = values + tensor_total(jnp.dot(attended, w_project, preferred_element_type=jnp.float32))
    scale_mlp = lax.rsqrt(jnp.mean(middle * middle, axis=-1, keepdims=True) + EPSILON)
    normed_mlp = (middle * scale_mlp * gain_mlp).astype(jnp.bfloat16)
    gate_up = jnp.einsum("td,dcf->tcf", normed_mlp, w_expand, preferred_element_type=jnp.float32)
    hidden = (jax.nn.silu(gate_up[:, 0]) * gate_up[:, 1]).astype(jnp.bfloat16)
    result = middle + tensor_total(jnp.dot(hidden, w_reduce, preferred_element_type=jnp.float32))
    kept_values = (
        values,
        scale_attn,
        normed,
        query_rows,
        kv_local,
        accumulated,
        log_total,
        attended,
        middle,
        scale_mlp,
        normed_mlp,
        gate_up,
        hidden,
    )
    return (result, kept_values)


def layer_backward(grad_result, kept_values, weights, pos_local, pos_all):
    gain_attn, w_mixed, bias_mixed, w_project, gain_mlp, w_expand, w_reduce = weights
    (
        values,
        scale_attn,
        normed,
        query_rows,
        kv_store,
        accumulated,
        log_total,
        attended,
        middle,
        scale_mlp,
        normed_mlp,
        gate_up,
        hidden,
    ) = kept_values
    tok_count = values.shape[0]
    query_width = w_project.shape[0]
    head_dim = (w_mixed.shape[1] - query_width) // 2
    head_count = query_width // head_dim
    grad_mlp = grad_result.astype(jnp.bfloat16)
    grad_hidden = lax.dot_general(
        grad_mlp, w_reduce, CONTRACT_LAST, preferred_element_type=jnp.float32
    )
    gate_part = gate_up[:, 0]
    up_part = gate_up[:, 1]
    gate_sigmoid = jax.nn.sigmoid(gate_part)
    grad_gate = grad_hidden * up_part * gate_sigmoid * (1.0 + gate_part * (1.0 - gate_sigmoid))
    grad_up = grad_hidden * (gate_part * gate_sigmoid)
    grad_expand = jnp.stack([grad_gate, grad_up], axis=1).astype(jnp.bfloat16)
    grad_normed_mlp = tensor_total(
        jnp.einsum("tcf,dcf->td", grad_expand, w_expand, preferred_element_type=jnp.float32)
    )
    grad_middle, gain_mlp_grad = norm_backward(middle, scale_mlp, gain_mlp, grad_normed_mlp)
    grad_middle = grad_middle + grad_result
    grad_branch = grad_middle.astype(jnp.bfloat16)
    grad_attended = lax.dot_general(
        grad_branch, w_project, CONTRACT_LAST, preferred_element_type=jnp.float32
    ).astype(jnp.bfloat16)
    grad_rows = grad_attended.reshape(tok_count * head_count, head_dim)
    row_delta = jnp.sum(grad_rows.astype(jnp.float32) * accumulated, axis=1)
    kv_all = lax.all_gather(kv_store, "ctx", axis=0, tiled=True)
    query_pos = jnp.repeat(pos_local, head_count)
    grad_query, grad_pairs = attention_backward(
        query_rows, query_pos, kv_all, pos_all, log_total, grad_rows, row_delta
    )
    grad_kv = lax.psum_scatter(
        grad_pairs.astype(jnp.bfloat16), "ctx", scatter_dimension=0, tiled=True
    ).astype(jnp.float32)
    cosine_table, sine_table = angles(pos_local, head_dim)
    grad_query = unrotate(
        grad_query.reshape(tok_count, head_count, head_dim),
        cosine_table[:, None, :],
        sine_table[:, None, :],
    ).reshape(tok_count, query_width)
    grad_key = unrotate(grad_kv[:, :head_dim], cosine_table, sine_table)
    grad_mixed = jnp.concatenate([grad_query, grad_key, grad_kv[:, head_dim:]], axis=1).astype(
        jnp.bfloat16
    )
    grad_normed = tensor_total(
        lax.dot_general(grad_mixed, w_mixed, CONTRACT_LAST, preferred_element_type=jnp.float32)
    )
    grad_values, gain_attn_grad = norm_backward(values, scale_attn, gain_attn, grad_normed)
    grad_values = grad_values + grad_middle
    return (
        grad_values,
        (gain_attn_grad, gain_mlp_grad),
        (grad_mixed, grad_branch, grad_expand, grad_mlp),
    )


def local_grads(
    normed_rows,
    attended_rows,
    normed_mlp_rows,
    hidden_rows,
    grad_mixed_rows,
    grad_branch_rows,
    grad_expand_rows,
    grad_mlp_rows,
    gain_attn_term,
    gain_mlp_term,
):
    grad_qkv = lax.dot_general(
        normed_rows, grad_mixed_rows, CONTRACT_ROWS, preferred_element_type=jnp.float32
    )
    grad_bias = jnp.sum(grad_mixed_rows.astype(jnp.float32), axis=0)
    split_at = grad_bias.shape[0] - HD
    grad_project = lax.dot_general(
        attended_rows, grad_branch_rows, CONTRACT_ROWS, preferred_element_type=jnp.float32
    )
    grad_expand = jnp.einsum(
        "td,tcf->dcf", normed_mlp_rows, grad_expand_rows, preferred_element_type=jnp.float32
    )
    grad_reduce = lax.dot_general(
        hidden_rows, grad_mlp_rows, CONTRACT_ROWS, preferred_element_type=jnp.float32
    )
    return (
        gain_attn_term[None],
        grad_qkv[None, :, None, :],
        grad_bias[:split_at][None, None],
        grad_bias[split_at:][None, None],
        grad_project[None, None],
        gain_mlp_term[None],
        grad_expand[None],
        grad_reduce[None],
    )


def shards(
    block_input, positions, cotangent, norm_attn, w_qkv, b_qkv, w_out, norm_mlp, w_gate_up, w_down
):
    micro_count = block_input.shape[0]
    last_index = micro_count - 1
    first_section = lax.axis_index("section") == 0

    def by_section(earlier, later):
        return jax.tree.map(
            lambda first_leaf, second_leaf: jnp.where(first_section, first_leaf, second_leaf),
            earlier,
            later,
        )

    all_positions = lax.all_gather(positions, "ctx", axis=1, tiled=True)
    weights = unpack(
        (
            lax.all_gather(norm_attn, "ctx", axis=1, tiled=True),
            lax.all_gather(w_qkv, "ctx", axis=1, tiled=True),
            lax.all_gather(b_qkv, "ctx", axis=2, tiled=True),
            lax.all_gather(w_out, "ctx", axis=2, tiled=True),
            lax.all_gather(norm_mlp, "ctx", axis=1, tiled=True),
            lax.all_gather(w_gate_up, "ctx", axis=1, tiled=True),
            lax.all_gather(w_down, "ctx", axis=1, tiled=True),
        )
    )
    received = jnp.zeros(block_input.shape[1:], jnp.bfloat16)
    forward_out = []
    forward_kept = []
    for step_index in range(micro_count + 1):
        later_index = min(step_index, last_index)
        earlier_index = max(step_index - 1, 0)
        entering = jnp.where(first_section, block_input[later_index], received).astype(jnp.float32)
        pos_local = by_section(positions[later_index], positions[earlier_index])
        pos_all = by_section(all_positions[later_index], all_positions[earlier_index])
        result, kept_values = layer_forward(entering, weights, pos_local, pos_all)
        handed = result.astype(jnp.bfloat16)
        forward_out.append(handed)
        forward_kept.append(kept_values)
        if step_index < micro_count:
            received = from_behind(handed, "section", 1)
    stored = [
        by_section(forward_kept[micro_index], forward_kept[micro_index + 1])
        for micro_index in range(micro_count)
    ]
    section_output = jnp.stack(
        [
            by_section(forward_out[micro_index], forward_out[micro_index + 1])
            for micro_index in range(micro_count)
        ]
    )[None]
    back_weights = unpack(
        (
            lax.all_gather(norm_attn, "ctx", axis=1, tiled=True),
            lax.all_gather(w_qkv, "ctx", axis=1, tiled=True),
            lax.all_gather(b_qkv, "ctx", axis=2, tiled=True),
            lax.all_gather(w_out, "ctx", axis=2, tiled=True),
            lax.all_gather(norm_mlp, "ctx", axis=1, tiled=True),
            lax.all_gather(w_gate_up, "ctx", axis=1, tiled=True),
            lax.all_gather(w_down, "ctx", axis=1, tiled=True),
        )
    )
    width = block_input.shape[2]
    received = jnp.zeros(block_input.shape[1:], jnp.bfloat16)
    backward_out = []
    grad_lists = []
    gain_attn_sum = jnp.zeros((width,), jnp.float32)
    gain_mlp_sum = jnp.zeros((width,), jnp.float32)
    for step_index in range(micro_count + 1):
        later_index = min(step_index, last_index)
        earlier_index = max(step_index - 1, 0)
        seed_own = (
            cotangent[later_index].astype(jnp.float32)
            if step_index < micro_count
            else jnp.zeros(block_input.shape[1:], jnp.float32)
        )
        entering = jnp.where(first_section, received.astype(jnp.float32), seed_own)
        kept_values = by_section(stored[earlier_index], stored[later_index])
        pos_local = by_section(positions[earlier_index], positions[later_index])
        pos_all = by_section(all_positions[earlier_index], all_positions[later_index])
        grad_values, gain_grads, grad_pairs = layer_backward(
            entering, kept_values, back_weights, pos_local, pos_all
        )
        handed = grad_values.astype(jnp.bfloat16)
        backward_out.append(handed)
        gain_attn_sum = gain_attn_sum + gain_grads[0]
        gain_mlp_sum = gain_mlp_sum + gain_grads[1]
        grad_lists.append(grad_pairs)
        if step_index < micro_count:
            received = from_behind(handed, "section", -1)
    input_grad = jnp.stack(
        [
            by_section(backward_out[micro_index + 1], backward_out[micro_index])
            for micro_index in range(micro_count)
        ]
    )[None]
    grad_micro = [
        by_section(grad_lists[micro_index + 1], grad_lists[micro_index])
        for micro_index in range(micro_count)
    ]
    normed_all = jnp.concatenate(
        [stored[micro_index][2] for micro_index in range(micro_count)], axis=0
    )
    attended_all = jnp.concatenate(
        [stored[micro_index][7] for micro_index in range(micro_count)], axis=0
    )
    normed_mlp_all = jnp.concatenate(
        [stored[micro_index][10] for micro_index in range(micro_count)], axis=0
    )
    hidden_all = jnp.concatenate(
        [stored[micro_index][12] for micro_index in range(micro_count)], axis=0
    )
    grad_mixed_all = jnp.concatenate(
        [grad_micro[micro_index][0] for micro_index in range(micro_count)], axis=0
    )
    grad_branch_all = jnp.concatenate(
        [grad_micro[micro_index][1] for micro_index in range(micro_count)], axis=0
    )
    grad_expand_all = jnp.concatenate(
        [grad_micro[micro_index][2] for micro_index in range(micro_count)], axis=0
    )
    grad_mlp_all = jnp.concatenate(
        [grad_micro[micro_index][3] for micro_index in range(micro_count)], axis=0
    )
    all_terms = local_grads(
        normed_all,
        attended_all,
        normed_mlp_all,
        hidden_all,
        grad_mixed_all,
        grad_branch_all,
        grad_expand_all,
        grad_mlp_all,
        gain_attn_sum,
        gain_mlp_sum,
    )
    reduced = (
        lax.psum_scatter(
            all_terms[0].astype(jnp.bfloat16), "ctx", scatter_dimension=1, tiled=True
        ).astype(jnp.float32),
        lax.psum_scatter(
            all_terms[1].astype(jnp.bfloat16), "ctx", scatter_dimension=1, tiled=True
        ).astype(jnp.float32),
        lax.psum_scatter(
            all_terms[2].astype(jnp.bfloat16), "ctx", scatter_dimension=2, tiled=True
        ).astype(jnp.float32),
        lax.psum_scatter(
            all_terms[3].astype(jnp.bfloat16), "ctx", scatter_dimension=2, tiled=True
        ).astype(jnp.float32),
        lax.psum_scatter(
            all_terms[4].astype(jnp.bfloat16), "ctx", scatter_dimension=2, tiled=True
        ).astype(jnp.float32),
        lax.psum_scatter(
            all_terms[5].astype(jnp.bfloat16), "ctx", scatter_dimension=1, tiled=True
        ).astype(jnp.float32),
        lax.psum_scatter(
            all_terms[6].astype(jnp.bfloat16), "ctx", scatter_dimension=1, tiled=True
        ).astype(jnp.float32),
        lax.psum_scatter(
            all_terms[7].astype(jnp.bfloat16), "ctx", scatter_dimension=1, tiled=True
        ).astype(jnp.float32),
    )
    return (
        section_output,
        input_grad,
        reduced[0],
        reduced[1],
        reduced[2],
        reduced[3],
        reduced[4],
        reduced[5],
        reduced[6],
        reduced[7],
    )


def solution(mesh):
    in_specs = (
        P(None, "ctx", None),
        P(None, "ctx"),
        P(None, "ctx", None),
        P("section", "ctx"),
        P("section", "ctx", "tensor", None),
        P("section", "tensor", "ctx"),
        P("section", "tensor", "ctx", None),
        P("section", "ctx"),
        P("section", "ctx", None, "tensor"),
        P("section", ("tensor", "ctx"), None),
    )
    out_specs = (
        P("section", None, "ctx", None),
        P("section", None, "ctx", None),
        P("section", "ctx"),
        P("section", "ctx", "tensor", None),
        P("section", "tensor", "ctx"),
        P("section", "tensor", "ctx"),
        P("section", "tensor", "ctx", None),
        P("section", "ctx"),
        P("section", "ctx", None, "tensor"),
        P("section", ("tensor", "ctx"), None),
    )
    return jax.shard_map(shards, mesh=mesh, in_specs=in_specs, out_specs=out_specs, check_vma=False)
```

profile of v0, /device:TPU:9, one launch (start us, length us, event | category | flops | bytes accessed | tf_op | source)
XLA Modules:
  0.0 2622.8 jit_solution(9567779795752878618)
XLA Ops:
  104.3 21.3 all-reduce.24.cloned.1.call-done
  126.9 237.5 %all-gather.9.cloned.1.call-done = bf16[1,1536,2,4480]{3,1,2,0:T(8,128)(2,1)} async-done(((bf16[1,192,2,4480]{3,1,2,0:T(8,128)(2,1)}), bf16[1,1536,2,4480]{3,1,2,0:T(8,128)(2,1)}) %all-gather.9.cloned.1.call-update) | async-done | bytes 27525136 | tf_op jit(solution)/shard_map/all_gather | solution.py:341
  379.8 110.8 %all-gather.11.cloned.1.call-done = bf16[1,4480,1536]{2,1,0:T(8,128)(2,1)} async-done(((bf16[1,560,1536]{2,1,0:T(8,128)(2,1)}), bf16[1,4480,1536]{2,1,0:T(8,128)(2,1)}) %all-gather.11.cloned.1.call-update) | async-done | bytes 13762576 | tf_op jit(solution)/shard_map/all_gather | solution.py:342
  500.0 26.6 %all-reduce.26.cloned.1.call-done = bf16[128,1536]{1,0:T(8,128)(2,1)} async-done(((bf16[128,1536]{1,0:T(8,128)(2,1)}), bf16[128,1536]{1,0:T(8,128)(2,1)}) %all-reduce.26.cloned.1.call-update) | async-done | bytes 393232 | tf_op jit(solution)/shard_map/psum | solution.py:45
  587.3 25.5 while.187
  638.0 26.4 %all-reduce.28.cloned.1.call-done = bf16[128,1536]{1,0:T(8,128)(2,1)} async-done(((bf16[128,1536]{1,0:T(8,128)(2,1)}), bf16[128,1536]{1,0:T(8,128)(2,1)}) %all-reduce.28.cloned.1.call-update) | async-done | bytes 393232 | tf_op jit(solution)/shard_map/psum | solution.py:45
  723.0 33.7 %all-reduce.48.cloned.1.call-done = (bf16[128,1536]{1,0:T(8,128)(2,1)}, bf16[128,1536]{1,0:T(8,128)(2,1)}) async-done(((bf16[128,1536]{1,0:T(8,128)(2,1)}, bf16[128,1536]{1,0:T(8,128)(2,1)}), (bf16[128,1536]{1,0:T(8,128)(2,1)}, bf16[128,1536]{1,0:T(8,128)(2,1)})) %all-reduce.48.cloned.1.call-update) | async-done | bytes 786448 | tf_op jit(solution)/shard_map/psum | solution.py:45
  829.1 25.6 while.189
  873.0 25.1 while.195
  942.9 38.5 %all-reduce.46.cloned.1.call-done = (bf16[128,1536]{1,0:T(8,128)(2,1)}, bf16[128,1536]{1,0:T(8,128)(2,1)}) async-done(((bf16[128,1536]{1,0:T(8,128)(2,1)}, bf16[128,1536]{1,0:T(8,128)(2,1)}), (bf16[128,1536]{1,0:T(8,128)(2,1)}, bf16[128,1536]{1,0:T(8,128)(2,1)})) %all-reduce.46.cloned.1.call-update) | async-done | bytes 786448 | tf_op jit(solution)/shard_map/psum | solution.py:45
  990.2 19.2 broadcast_select_fusion.8
  1098.7 25.2 while.196
  1176.6 20.4 all_gather.71
  1199.7 25.7 while.191
  1254.4 35.1 %all-reduce.42.cloned.1.call-done = (bf16[128,1536]{1,0:T(8,128)(2,1)}, bf16[128,1536]{1,0:T(8,128)(2,1)}) async-done(((bf16[128,1536]{1,0:T(8,128)(2,1)}, bf16[128,1536]{1,0:T(8,128)(2,1)}), (bf16[128,1536]{1,0:T(8,128)(2,1)}, bf16[128,1536]{1,0:T(8,128)(2,1)})) %all-reduce.42.cloned.1.call-update) | async-done | bytes 786448 | tf_op jit(solution)/shard_map/psum | solution.py:45
  1300.7 19.1 broadcast_select_fusion.6
  1357.0 35.2 %all-reduce.40.cloned.1.call-done = (bf16[128,1536]{1,0:T(8,128)(2,1)}, bf16[128,1536]{1,0:T(8,128)(2,1)}) async-done(((bf16[128,1536]{1,0:T(8,128)(2,1)}, bf16[128,1536]{1,0:T(8,128)(2,1)}), (bf16[128,1536]{1,0:T(8,128)(2,1)}, bf16[128,1536]{1,0:T(8,128)(2,1)})) %all-reduce.40.cloned.1.call-update) | async-done | bytes 786448 | tf_op jit(solution)/shard_map/psum | solution.py:45
  1438.7 25.2 while.197
  1502.7 25.5 while.193
  1575.3 37.6 %all-reduce.38.cloned.1.call-done = (bf16[128,1536]{1,0:T(8,128)(2,1)}, bf16[128,1536]{1,0:T(8,128)(2,1)}) async-done(((bf16[128,1536]{1,0:T(8,128)(2,1)}, bf16[128,1536]{1,0:T(8,128)(2,1)}), (bf16[128,1536]{1,0:T(8,128)(2,1)}, bf16[128,1536]{1,0:T(8,128)(2,1)})) %all-reduce.38.cloned.1.call-update) | async-done | bytes 786448 | tf_op jit(solution)/shard_map/psum | solution.py:45
  1621.0 21.1 broadcast_select_fusion.4
  1709.0 25.3 while.198
  1740.1 20.6 reduce-scatter.28.cloned.1.call-done
  1780.8 30.8 %all-reduce.32.cloned.1.call-done = bf16[128,1536]{1,0:T(8,128)(2,1)} async-done(((bf16[128,1536]{1,0:T(8,128)(2,1)}), bf16[128,1536]{1,0:T(8,128)(2,1)}) %all-reduce.32.cloned.1.call-update) | async-done | bytes 393232 | tf_op jit(solution)/shard_map/psum | solution.py:45
  1894.7 25.0 while.199
  1963.6 29.2 %all-reduce.36.cloned.1.call-done = (bf16[128,1536]{1,0:T(8,128)(2,1)}, bf16[128,1536]{1,0:T(8,128)(2,1)}) async-done(((bf16[128,1536]{1,0:T(8,128)(2,1)}, bf16[128,1536]{1,0:T(8,128)(2,1)}), (bf16[128,1536]{1,0:T(8,128)(2,1)}, bf16[128,1536]{1,0:T(8,128)(2,1)})) %all-reduce.36.cloned.1.call-update) | async-done | bytes 786448 | tf_op jit(solution)/shard_map/psum | solution.py:45
  2038.5 21.4 convert_bitcast_fusion
  2084.6 26.7 %reduce-scatter.40.cloned.1.call-done = bf16[192,1]{1,0:T(8,128)(2,1)} async-done(((bf16[1536,1]{1,0:T(8,128)(2,1)}), bf16[192,1]{1,0:T(8,128)(2,1)}) %reduce-scatter.40.cloned.1.call-update) | async-done | bytes 400
  2112.8 37.2 %reduce-scatter.34.cloned.1.call-done = bf16[1,1,96,1536]{3,2,1,0:T(8,128)(2,1)} async-done(((bf16[1,1,768,1536]{3,2,1,0:T(8,128)(2,1)}), bf16[1,1,96,1536]{3,2,1,0:T(8,128)(2,1)}) %reduce-scatter.34.cloned.1.call-update) | async-done | bytes 294928 | tf_op jit(solution)/shard_map/reduce_scatter | solution.py:468
  2151.8 43.1 %reduce-scatter.32.cloned.1.call-done = bf16[1,192,1,1024]{3,1,2,0:T(8,128)(2,1)} async-done(((bf16[1,1536,1,1024]{3,1,2,0:T(8,128)(2,1)}), bf16[1,192,1,1024]{3,1,2,0:T(8,128)(2,1)}) %reduce-scatter.32.cloned.1.call-update) | async-done | bytes 393232 | tf_op jit(solution)/shard_map/reduce_scatter | solution.py:459
  2197.4 139.9 %reduce-scatter.38.cloned.1.call-done = bf16[1,560,1536]{2,1,0:T(8,128)(2,1)} async-done(((bf16[1,4480,1536]{2,1,0:T(8,128)(2,1)}), bf16[1,560,1536]{2,1,0:T(8,128)(2,1)}) %reduce-scatter.38.cloned.1.call-update) | async-done | bytes 1720336 | tf_op jit(solution)/shard_map/reduce_scatter | solution.py:477
  2341.0 266.4 %reduce-scatter.36.cloned.1.call-done = bf16[1,192,2,4480]{3,1,2,0:T(8,128)(2,1)} async-done(((bf16[1,1536,2,4480]{3,1,2,0:T(8,128)(2,1)}), bf16[1,192,2,4480]{3,1,2,0:T(8,128)(2,1)}) %reduce-scatter.36.cloned.1.call-update) | async-done | bytes 3440656 | tf_op jit(solution)/shard_map/reduce_scatter | solution.py:474
  (1152 shorter events, 1389.2 us)
Async XLA Ops:
  7.2 51.2 %all-gather.5.cloned.1.call-start = ((), (), s32[]{:S(2)}) async-start(), calls=%async_computation.13 | async-start | bytes 3538944 | tf_op jit(solution)/shard_map/all_gather | solution.py:337
  7.9 88.1 %all-gather.7.cloned.1.call-start = ((), (), s32[]{:S(2)}) async-start(), calls=%async_computation.14 | async-start | bytes 2654208 | tf_op jit(solution)/shard_map/all_gather | solution.py:339
  8.7 117.0 %all-reduce.24.cloned.1.call-start = ((), (), s32[]{:S(2)}) async-start(), calls=%async_computation.15 | async-start | bytes 786432 | tf_op jit(solution)/shard_map/psum | solution.py:45
  99.0 265.4 %all-gather.9.cloned.1.call-start = ((), (), s32[]{:S(2)}) async-start(), calls=%async_computation.16 | async-start | bytes 30965760 | tf_op jit(solution)/shard_map/all_gather | solution.py:341
  103.2 387.4 %all-gather.11.cloned.1.call-start = ((), (), s32[]{:S(2)}) async-start(), calls=%async_computation.17 | async-start | bytes 15482880 | tf_op jit(solution)/shard_map/all_gather | solution.py:342
  103.8 422.8 %all-reduce.26.cloned.1.call-start = ((), (), s32[]{:S(2)}) async-start(), calls=%async_computation.18 | async-start | bytes 786432 | tf_op jit(solution)/shard_map/psum | solution.py:45
  499.9 164.4 %all-reduce.28.cloned.1.call-start = ((), (), s32[]{:S(2)}) async-start(), calls=%async_computation.19 | async-start | bytes 786432 | tf_op jit(solution)/shard_map/psum | solution.py:45
  637.7 119.0 %all-reduce.48.cloned.1.call-start = ((), (), s32[]{:S(2)}) async-start(), calls=%async_computation.42 | async-start | bytes 1572864 | tf_op jit(solution)/shard_map/psum | solution.py:45
  723.0 212.6 %reduce-scatter.22.cloned.1.call-start = ((), (), s32[]{:S(2)}) async-start(), calls=%async_computation.20 | async-start | bytes 589824 | tf_op jit(solution)/shard_map/reduce_scatter | solution.py:256
  910.0 71.4 %all-reduce.46.cloned.1.call-start = ((), (), s32[]{:S(2)}) async-start(), calls=%async_computation.41 | async-start | bytes 1572864 | tf_op jit(solution)/shard_map/psum | solution.py:45
  942.3 138.0 %all-reduce.44.cloned.1.call-start = ((), (), s32[]{:S(2)}) async-start(), calls=%async_computation.40 | async-start | bytes 1572864 | tf_op jit(solution)/shard_map/psum | solution.py:45
  1046.4 107.0 %reduce-scatter.24.cloned.1.call-start = ((), (), s32[]{:S(2)}) async-start(), calls=%async_computation.21 | async-start | bytes 589824 | tf_op jit(solution)/shard_map/reduce_scatter | solution.py:256
  1094.3 35.4 %collective-permute-start.2 = (bf16[128,1536]{1,0:T(8,128)(2,1)}, bf16[128,1536]{1,0:T(8,128)(2,1)}, u32[]{:S(2)}, u32[]{:S(2)}) collective-permute-start(bf16[128,1536]{1,0:T(8,128)(2,1)} %get-tuple-element.1482), channel_id=1, source_target_pairs={{0,16},{1,17},{2,18},{3,19},{4,20},{5,21},{6,22},{7,23},{8,24},{9,... | collective-permute-start | bytes 1179656 | tf_op jit(solution)/shard_map/ppermute | solution.py:20
  1129.6 159.9 %all-reduce.42.cloned.1.call-start = ((), (), s32[]{:S(2)}) async-start(), calls=%async_computation.39 | async-start | bytes 1572864 | tf_op jit(solution)/shard_map/psum | solution.py:45
  1254.4 137.8 %all-reduce.40.cloned.1.call-start = ((), (), s32[]{:S(2)}) async-start(), calls=%async_computation.38 | async-start | bytes 1572864 | tf_op jit(solution)/shard_map/psum | solution.py:45
  1299.0 30.1 %collective-permute-start.5 = (bf16[128,1536]{1,0:T(8,128)(2,1)}, bf16[128,1536]{1,0:T(8,128)(2,1)}, u32[]{:S(2)}, u32[]{:S(2)}) collective-permute-start(bf16[128,1536]{1,0:T(8,128)(2,1)} %get-tuple-element.1474), channel_id=1, source_target_pairs={{16,0},{17,1},{18,2},{19,3},{20,4},{21,5},{22,6},{23,7},{24,8},{25... | collective-permute-start | bytes 1179656 | tf_op jit(solution)/shard_map/ppermute | solution.py:20
  1357.0 198.2 %reduce-scatter.26.cloned.1.call-start = ((), (), s32[]{:S(2)}) async-start(), calls=%async_computation.22 | async-start | bytes 589824 | tf_op jit(solution)/shard_map/reduce_scatter | solution.py:256
  1530.3 82.6 %all-reduce.38.cloned.1.call-start = ((), (), s32[]{:S(2)}) async-start(), calls=%async_computation.37 | async-start | bytes 1572864 | tf_op jit(solution)/shard_map/psum | solution.py:45
  1575.2 120.6 %all-reduce.30.cloned.1.call-start = ((), (), s32[]{:S(2)}) async-start(), calls=%async_computation.23 | async-start | bytes 786432 | tf_op jit(solution)/shard_map/psum | solution.py:45
  1670.0 90.6 %reduce-scatter.28.cloned.1.call-start = ((), (), s32[]{:S(2)}) async-start(), calls=%async_computation.24 | async-start | bytes 589824 | tf_op jit(solution)/shard_map/reduce_scatter | solution.py:256
  1736.4 75.3 %all-reduce.32.cloned.1.call-start = ((), (), s32[]{:S(2)}) async-start(), calls=%async_computation.25 | async-start | bytes 786432 | tf_op jit(solution)/shard_map/psum | solution.py:45
  1780.7 102.4 %all-reduce.34.cloned.1.call-start = ((), (), s32[]{:S(2)}) async-start(), calls=%async_computation.26 | async-start | bytes 786432 | tf_op jit(solution)/shard_map/psum | solution.py:45
  1857.3 89.1 %reduce-scatter.30.cloned.1.call-start = ((), (), s32[]{:S(2)}) async-start(), calls=%async_computation.27 | async-start | bytes 589824 | tf_op jit(solution)/shard_map/reduce_scatter | solution.py:256
  1921.8 71.0 %all-reduce.36.cloned.1.call-start = ((), (), s32[]{:S(2)}) async-start(), calls=%async_computation.36 | async-start | bytes 1572864 | tf_op jit(solution)/shard_map/psum | solution.py:45
  1953.3 106.6 %reduce-scatter.46.cloned.1.call-start = ((), (), s32[]{:S(2)}) async-start(), calls=%async_computation.35 | async-start | bytes 442368
  1957.9 103.7 %reduce-scatter.44.cloned.1.call-start = ((), (), s32[]{:S(2)}) async-start(), calls=%async_computation.34 | async-start | bytes 36864
  1959.7 120.5 %reduce-scatter.42.cloned.1.call-start = ((), (), s32[]{:S(2)}) async-start(), calls=%async_computation.33 | async-start | bytes 258048
  1963.5 147.8 %reduce-scatter.40.cloned.1.call-start = ((), (), s32[]{:S(2)}) async-start(), calls=%async_computation.32 | async-start | bytes 442368
  1995.3 154.7 %reduce-scatter.34.cloned.1.call-start = ((), (), s32[]{:S(2)}) async-start(), calls=%async_computation.29 | async-start | bytes 2654208 | tf_op jit(solution)/shard_map/reduce_scatter | solution.py:468
  1999.8 195.1 %reduce-scatter.32.cloned.1.call-start = ((), (), s32[]{:S(2)}) async-start(), calls=%async_computation.28 | async-start | bytes 3538944 | tf_op jit(solution)/shard_map/reduce_scatter | solution.py:459
  2004.8 332.5 %reduce-scatter.38.cloned.1.call-start = ((), (), s32[]{:S(2)}) async-start(), calls=%async_computation.31 | async-start | bytes 15482880 | tf_op jit(solution)/shard_map/reduce_scatter | solution.py:477
  2028.4 579.0 %reduce-scatter.36.cloned.1.call-start = ((), (), s32[]{:S(2)}) async-start(), calls=%async_computation.30 | async-start | bytes 30965760 | tf_op jit(solution)/shard_map/reduce_scatter | solution.py:474
  (225 other events, 2053.5 us)
Sparse Core Ops, SparseCore 0:
  9.7 39.4 all-gather.4
  50.8 35.1 all-gather.6
  99.1 26.4 all-reduce.23
  127.7 236.6 all-gather.8
  366.0 124.5 all-gather.10
  500.1 26.4 all-reduce.25
  637.9 26.4 all-reduce.27
  723.1 33.5 all-reduce.47
  910.1 24.7 reduce-scatter.21
  942.5 38.8 all-reduce.45
  1046.5 33.7 all-reduce.43
  1129.8 23.5 reduce-scatter.23
  1254.5 34.9 all-reduce.41
  1357.1 35.0 all-reduce.39
  1530.4 22.8 reduce-scatter.25
  1575.4 37.5 all-reduce.37
  1670.2 25.5 all-reduce.29
  1736.5 24.1 reduce-scatter.27
  1780.9 30.7 all-reduce.31
  1857.4 25.6 all-reduce.33
  1921.9 24.3 reduce-scatter.29
  1953.5 39.2 all-reduce.35
  1995.1 23.9 reduce-scatter.45
  2021.3 28.1 reduce-scatter.43
  2051.7 28.4 reduce-scatter.41
  2082.4 28.8 reduce-scatter.39
  2113.5 36.4 reduce-scatter.33
  2152.9 41.9 reduce-scatter.31
  2197.2 140.0 reduce-scatter.37
  2339.6 267.7 reduce-scatter.35
where the time goes:
time: 2640 us; the launch traced here: 2620 us
  waiting for transfers between devices  1270 us (48%)
  matrix products  461 us (17%)
  local copies, waits for them, and re-layouts  386 us (15%)
  other arithmetic  250 us (9%)
  blocking collectives  210 us (8%)
    psum x13, waiting for transfers between devices, tensor_total(): lax.psum(partial_value.astype(jnp.bfloat16), 'tensor').astype(jnp.float32)  346 us
    reduce_scatter x1, waiting for transfers between devices, shards(): lax.psum_scatter(all_terms[6].astype(jnp.bfloat16), 'ctx', scatter_dimens...  266 us
    all_gather x1, waiting for transfers between devices, shards(): lax.all_gather(w_gate_up, 'ctx', axis=1, tiled=True)  238 us
    reduce_scatter x1, waiting for transfers between devices, shards(): lax.psum_scatter(all_terms[7].astype(jnp.bfloat16), 'ctx', scatter_dimens...  140 us
    all_gather x1, waiting for transfers between devices, shards(): lax.all_gather(w_down, 'ctx', axis=1, tiled=True)  111 us
    dot_general x5, matrix products, layer_forward(): jnp.einsum('td,dcf->tcf', normed_mlp, w_expand, preferred_element_type=jn...  90.9 us
    all_gather x5, blocking collectives, layer_forward(): kv_all = lax.all_gather(kv_local, 'ctx', axis=0, tiled=True)  86.1 us
    all_gather x5, blocking collectives, layer_backward(): kv_all = lax.all_gather(kv_store, 'ctx', axis=0, tiled=True)  83.7 us
  transfers between devices with their start and end apart: 38, of which 27 were waited for; matrix products, arithmetic and copies ran while one was open for 14% of the time, Pallas kernels for 0%

commit v1 on v0

v1 whole, which is shorter than its diff:
```python
import functools
import math

import jax
import jax.numpy as jnp
from jax import lax
from jax.sharding import PartitionSpec as P

EPSILON = 1e-06
ROPE_BASE = 1000000.0
ROWS = (((0,), (0,)), ((), ()))
LAST = (((1,), (1,)), ((), ()))
F32 = jnp.float32
BF16 = jnp.bfloat16
SWAP = [(0, 1), (1, 0)]


def dot(a, b, dims=(((1,), (0,)), ((), ()))):
    return lax.dot_general(a, b, dims, preferred_element_type=F32)


def angles(positions, head_dim):
    half_dim = head_dim // 2
    frequency = ROPE_BASE ** (-(jnp.arange(half_dim, dtype=F32) * 2.0) / head_dim)
    phases = positions.astype(F32)[:, None] * frequency[None, :]
    phases = jnp.concatenate([phases, phases], axis=-1)
    return jnp.cos(phases), jnp.sin(phases)


def rotate(values, cosine, sine):
    half = values.shape[-1] // 2
    turned = jnp.concatenate([-values[..., half:], values[..., :half]], axis=-1)
    return values * cosine + turned * sine


def unrotate(grads, cosine, sine):
    half = grads.shape[-1] // 2
    twisted = grads * sine
    turned = jnp.concatenate([twisted[..., half:], -twisted[..., :half]], axis=-1)
    return grads * cosine + turned


def inverse_root(values):
    return lax.rsqrt(jnp.mean(values * values, axis=-1, keepdims=True) + EPSILON)


def norm_backward(values, root, gain, grad_normed):
    normal = values * root
    gain_grad = jnp.sum(grad_normed * normal, axis=0)
    scaled = grad_normed * gain
    mean = jnp.mean(scaled * normal, axis=-1, keepdims=True)
    return root * (scaled - normal * mean), gain_grad


def swap(value):
    return lax.ppermute(value, "section", SWAP)


def gather_ctx(value, axis):
    return lax.all_gather(value, "ctx", axis=axis, tiled=True)


def gather_tokens(rows):
    return lax.all_gather(rows, ("tensor", "ctx"), axis=0, tiled=True)


def scatter_tokens(rows):
    return lax.psum_scatter(rows, ("tensor", "ctx"), scatter_dimension=0, tiled=True).astype(F32)


def tensor_gather(rows):
    return lax.all_gather(rows, "tensor", axis=0, tiled=True)


def tensor_scatter(rows):
    return lax.psum_scatter(
        rows.astype(BF16), "tensor", scatter_dimension=0, tiled=True
    ).astype(F32)


def attend(queries, kv, query_pos, key_pos, head_dim):
    factor = 1.0 / math.sqrt(head_dim)
    keys, values = kv[..., :head_dim], kv[..., head_dim:]
    scores = jnp.einsum("bqhd,bkd->bhqk", queries, keys, preferred_element_type=F32)
    allowed = query_pos[:, None, :, None] >= key_pos[:, None, None, :]
    scores = jnp.where(allowed, scores * factor, -1e30)
    log_total = jax.nn.logsumexp(scores, axis=-1)
    probs = jnp.exp(scores - log_total[..., None]).astype(BF16)
    out = jnp.einsum("bhqk,bkd->bqhd", probs, values, preferred_element_type=F32)
    return out, log_total


def attend_backward(queries, kv, query_pos, key_pos, head_dim, log_total, grads, delta):
    factor = 1.0 / math.sqrt(head_dim)
    keys, values = kv[..., :head_dim], kv[..., head_dim:]
    scores = jnp.einsum("bqhd,bkd->bhqk", queries, keys, preferred_element_type=F32)
    allowed = query_pos[:, None, :, None] >= key_pos[:, None, None, :]
    scores = jnp.where(allowed, scores * factor, -1e30)
    probs = jnp.exp(scores - log_total[..., None])
    grad_probs = jnp.einsum("bqhd,bkd->bhqk", grads, values, preferred_element_type=F32)
    grad_scores = (probs * (grad_probs - delta[..., None]) * factor).astype(BF16)
    grad_q = jnp.einsum("bhqk,bkd->bqhd", grad_scores, keys, preferred_element_type=F32)
    grad_k = jnp.einsum("bhqk,bqhd->bkd", grad_scores, queries, preferred_element_type=F32)
    grad_v = jnp.einsum("bhqk,bqhd->bkd", probs.astype(BF16), grads, preferred_element_type=F32)
    return grad_q, jnp.concatenate([grad_k, grad_v], axis=-1)


def layer_forward(x_low, weights, tables):
    gain_attn, w_mixed, bias, w_project, gain_mlp, w_expand, w_reduce = weights
    cosine, sine, query_pos, key_pos, mine = tables
    count, width = x_low.shape
    query_width = w_project.shape[0]
    head_dim = (w_mixed.shape[1] - query_width) // 2
    heads = query_width // head_dim
    batch = query_pos.shape[0]
    tokens = count // batch
    x = x_low.astype(F32)
    root_attn = inverse_root(x)
    normed = (x * root_attn * gain_attn).astype(BF16)
    mixed = dot(normed, w_mixed) + bias
    queries = rotate(
        mixed[:, :query_width].reshape(count, heads, head_dim),
        cosine[:, None, :],
        sine[:, None, :],
    ).astype(BF16)
    queries = queries.reshape(batch, tokens, heads, head_dim)
    keys = rotate(mixed[:, query_width : query_width + head_dim], cosine, sine)
    kv = jnp.concatenate([keys, mixed[:, query_width + head_dim :]], axis=1).astype(BF16)
    kv = gather_ctx(kv.reshape(batch, tokens, 2 * head_dim), 1)
    attended_full, log_total = attend(queries, kv, query_pos, key_pos, head_dim)
    attended = attended_full.astype(BF16).reshape(count, query_width)
    x_mine = lax.dynamic_slice_in_dim(x, mine * tokens, tokens, 0)
    middle = x_mine + tensor_scatter(dot(attended, w_project))
    root_mlp = inverse_root(middle)
    normed_mlp = (middle * root_mlp * gain_mlp).astype(BF16)
    all_normed = gather_tokens(normed_mlp)
    gate = dot(all_normed, w_expand[0])
    up = dot(all_normed, w_expand[1])
    hidden = (jax.nn.silu(gate) * up).astype(BF16)
    result = middle + scatter_tokens(dot(hidden, w_reduce).astype(BF16))
    kept = (
        x_mine,
        lax.dynamic_slice_in_dim(root_attn, mine * tokens, tokens, 0),
        normed,
        queries,
        kv,
        attended_full,
        log_total,
        attended,
        middle,
        root_mlp,
        all_normed,
        gate,
        up,
        hidden,
    )
    return result.astype(BF16), kept


def layer_backward(grad_out, kept, weights, tables):
    gain_attn, w_mixed, bias, w_project, gain_mlp, w_expand, w_reduce = weights
    cosine, sine, query_pos, key_pos, mine = tables
    (
        x_mine,
        root_attn,
        normed,
        queries,
        kv,
        attended_full,
        log_total,
        attended,
        middle,
        root_mlp,
        all_normed,
        gate,
        up,
        hidden,
    ) = kept
    batch, tokens, heads, head_dim = queries.shape
    count = batch * tokens
    grad_mlp = gather_tokens(grad_out.astype(BF16))
    grad_hidden = dot(grad_mlp, w_reduce, LAST)
    sig = jax.nn.sigmoid(gate)
    grad_gate = (grad_hidden * up * sig * (1.0 + gate * (1.0 - sig))).astype(BF16)
    grad_up = (grad_hidden * (gate * sig)).astype(BF16)
    part = dot(grad_gate, w_expand[0], LAST) + dot(grad_up, w_expand[1], LAST)
    grad_normed_mlp = scatter_tokens(part.astype(BF16))
    d_reduce = dot(hidden, grad_mlp, ROWS)
    d_expand = jnp.stack([dot(all_normed, grad_gate, ROWS), dot(all_normed, grad_up, ROWS)])
    grad_middle, d_gain_mlp = norm_backward(middle, root_mlp, gain_mlp, grad_normed_mlp)
    grad_middle = grad_middle + grad_out
    grad_branch = tensor_gather(grad_middle.astype(BF16))
    d_project = dot(attended, grad_branch, ROWS)
    grad_attended = dot(grad_branch, w_project, LAST).astype(BF16)
    grad_attended = grad_attended.reshape(batch, tokens, heads, head_dim)
    delta = jnp.sum(grad_attended.astype(F32) * attended_full, axis=-1)
    grad_q, grad_kv = attend_backward(
        queries,
        kv,
        query_pos,
        key_pos,
        head_dim,
        log_total,
        grad_attended,
        jnp.swapaxes(delta, 1, 2),
    )
    grad_kv = lax.psum_scatter(
        grad_kv.astype(BF16), "ctx", scatter_dimension=1, tiled=True
    ).astype(F32)
    grad_kv = grad_kv.reshape(count, 2 * head_dim)
    grad_q = unrotate(
        grad_q.reshape(count, heads, head_dim), cosine[:, None, :], sine[:, None, :]
    )
    grad_k = unrotate(grad_kv[:, :head_dim], cosine, sine)
    grad_mixed = jnp.concatenate(
        [grad_q.reshape(count, heads * head_dim), grad_k, grad_kv[:, head_dim:]], axis=1
    ).astype(BF16)
    d_mixed = dot(normed, grad_mixed, ROWS)
    d_bias = jnp.sum(grad_mixed.astype(F32), axis=0)
    grad_normed = tensor_scatter(dot(grad_mixed, w_mixed, LAST))
    grad_x, d_gain_attn = norm_backward(x_mine, root_attn, gain_attn, grad_normed)
    grad_x = (grad_x + grad_middle).astype(BF16)
    return grad_x, (d_gain_attn, d_mixed, d_bias, d_project, d_gain_mlp, d_expand, d_reduce)


def shards(
    block_input, positions, cotangent, norm_attn, w_qkv, b_qkv, w_out, norm_mlp, w_gate_up, w_down
):
    section = lax.axis_index("section")
    tensor = lax.axis_index("tensor")
    ctx = lax.axis_index("ctx")
    ctx_size = lax.axis_size("ctx")
    first = section == 0
    micro, tokens, width = block_input.shape
    half = micro // 2
    head_dim = w_qkv.shape[3] - w_out.shape[2] * ctx_size
    head_dim = head_dim // 2
    slice_width = norm_attn.shape[1]
    slice_bias = b_qkv.shape[2]
    units = w_down.shape[1]

    def plane_part(value):
        return lax.dynamic_slice_in_dim(value, section * half, half, 0)

    def layers(own, other):
        return jnp.where(first, own, other), jnp.where(first, other, own)

    x = plane_part(block_input).reshape(half * tokens, width)
    pos_local = plane_part(positions)
    pos_all = gather_ctx(pos_local, 1)
    cosine, sine = angles(pos_local.reshape(-1), head_dim)
    tables = (cosine, sine, pos_local, pos_all, tensor)

    small = jnp.concatenate([norm_attn[0], norm_mlp[0], b_qkv[0, 0]])
    qkv, out = w_qkv[0, :, 0, :], w_out[0, 0]
    expand = jnp.transpose(
        w_gate_up[0].reshape(slice_width, 2, ctx_size, units), (2, 1, 0, 3)
    )
    expand = lax.all_to_all(expand, "ctx", split_axis=0, concat_axis=0, tiled=True)
    expand = jnp.transpose(expand, (1, 0, 2, 3)).reshape(2, width, units)
    small0, small1 = layers(small, swap(small))
    qkv0, qkv1 = layers(qkv, swap(qkv))
    out0, out1 = layers(out, swap(out))
    expand0, expand1 = layers(expand, swap(expand))
    down0, down1 = layers(w_down[0], swap(w_down[0]))

    def whole(small, qkv, out, expand, down):
        small = gather_ctx(small[None], 0)
        return (
            small[:, :slice_width].reshape(1, width),
            gather_ctx(qkv, 0),
            small[:, 2 * slice_width :].reshape(1, slice_bias * ctx_size),
            gather_ctx(out, 0),
            small[:, slice_width : 2 * slice_width].reshape(1, width),
            expand,
            down,
        )

    weights0 = whole(small0, qkv0, out0, expand0, down0)
    weights1 = whole(small1, qkv1, out1, expand1, down1)

    result0, kept0 = layer_forward(x, weights0, tables)
    x1 = tensor_gather(result0)
    result1, kept1 = layer_forward(x1, weights1, tables)
    out1_all = tensor_gather(result1)

    def exchange(layer0, layer1):
        kept_here = jnp.where(first, layer0, layer1)
        received = swap(jnp.where(first, layer1, layer0))
        low = jnp.where(first, kept_here, received)
        high = jnp.where(first, received, kept_here)
        both = jnp.concatenate([low, high], axis=0)
        return both.reshape(1, micro, tokens, width)

    section_output = exchange(x1, out1_all)

    seed = lax.dynamic_slice_in_dim(cotangent, section * half + tensor, 1, 0)[0].astype(F32)
    grad1, d1 = layer_backward(seed, kept1, weights1, tables)
    grad0, d0 = layer_backward(grad1.astype(F32), kept0, weights0, tables)
    input_grad = exchange(tensor_gather(grad0), tensor_gather(grad1))

    def to_owner(part0, part1):
        return jnp.where(first, part0, part1), jnp.where(first, part1, part0).astype(BF16)

    def over_section(part0, part1):
        own, other = to_owner(part0, part1)
        return own + swap(other).astype(F32)

    d_expand = over_section(d0[5], d1[5])
    d_expand = d_expand.astype(BF16).reshape(2, ctx_size, slice_width, units)
    d_expand = lax.all_to_all(
        jnp.transpose(d_expand, (1, 0, 2, 3)), "ctx", split_axis=0, concat_axis=0, tiled=True
    )
    d_expand = jnp.transpose(d_expand, (2, 1, 0, 3)).reshape(
        1, slice_width, 2, ctx_size * units
    ).astype(F32)
    d_reduce = over_section(d0[6], d1[6])

    def ctx_scatter(value):
        return lax.psum_scatter(
            value.astype(BF16), "ctx", scatter_dimension=0, tiled=True
        ).astype(F32)

    d_mixed = over_section(ctx_scatter(d0[1]), ctx_scatter(d1[1]))
    d_project = over_section(ctx_scatter(d0[3]), ctx_scatter(d1[3]))
    gains = jnp.stack([jnp.stack([d0[0], d0[4]]), jnp.stack([d1[0], d1[4]])])
    gains = lax.psum(gains, ("section", "tensor", "ctx"))
    gains = lax.dynamic_slice(
        gains, (section, 0, ctx * slice_width), (1, 2, slice_width)
    )
    biases = lax.psum(jnp.stack([d0[2], d1[2]]), ("section", "ctx"))
    biases = lax.dynamic_slice_in_dim(biases, section, 1, 0)
    split_at = biases.shape[1] - head_dim
    bias_qk = lax.dynamic_slice_in_dim(
        biases[:, :split_at], ctx * (split_at // ctx_size), split_at // ctx_size, 1
    )
    bias_v = lax.dynamic_slice_in_dim(
        biases[:, split_at:], ctx * (head_dim // ctx_size), head_dim // ctx_size, 1
    )
    return (
        section_output,
        input_grad,
        gains[:, 0],
        d_mixed[None, :, None, :],
        bias_qk[None],
        bias_v[None],
        d_project[None, None],
        gains[:, 1],
        d_expand,
        d_reduce[None],
    )


def solution(mesh):
    in_specs = (
        P(None, "ctx", None),
        P(None, "ctx"),
        P(None, "ctx", None),
        P("section", "ctx"),
        P("section", "ctx", "tensor", None),
        P("section", "tensor", "ctx"),
        P("section", "tensor", "ctx", None),
        P("section", "ctx"),
        P("section", "ctx", None, "tensor"),
        P("section", ("tensor", "ctx"), None),
    )
    out_specs = (
        P("section", None, "ctx", None),
        P("section", None, "ctx", None),
        P("section", "ctx"),
        P("section", "ctx", "tensor", None),
        P("section", "tensor", "ctx"),
        P("section", "tensor", "ctx"),
        P("section", "tensor", "ctx", None),
        P("section", "ctx"),
        P("section", "ctx", None, "tensor"),
        P("section", ("tensor", "ctx"), None),
    )
    return jax.shard_map(shards, mesh=mesh, in_specs=in_specs, out_specs=out_specs, check_vma=False)
```

time: 2640 us -> 1690 us (0.64)
  waiting for transfers between devices: 1270 us -> 936 us
  local copies, waits for them, and re-layouts: 386 us -> 99.4 us
  matrix products: 461 us -> 202 us
  other arithmetic: 250 us -> 90 us
  blocking collectives: 210 us -> 301 us
    psum x13 -> x0, waiting for transfers between devices: 346 us -> none  [tensor_total(): lax.psum(partial_value.astype(jnp.bfloat16), 'tensor').astype(jnp.float32)]
    dot_general x114 -> x42, matrix products: 461 us -> 202 us  [the longest x30 170 us: dot(): return lax.dot_general(a, b, dims, preferred_element_type=F32)]
    ppermute x8 -> x11, waiting for transfers between devices: 16.4 us -> 226 us  [swap(): return lax.ppermute(value, 'section', SWAP)]
    reduce_scatter x9 -> x12, waiting for transfers between devices: 517 us -> 368 us  [the longest x4 325 us: scatter_tokens(): lax.psum_scatter(rows, ('tensor', 'ctx'), scatter_dimension=0, tiled=True)]
    all_to_all x0 -> x1, blocking collectives: none -> 119 us  [shards(): lax.all_to_all(expand, 'ctx', split_axis=0, concat_axis=0, tiled=True)]
    all_gather x12 -> x9, blocking collectives: 197 us -> 101 us  [the longest x6 60.4 us: tensor_gather(): return lax.all_gather(rows, 'tensor', axis=0, tiled=True)]
    psum x0 -> x2, blocking collectives: none -> 81.2 us  [the longest x1 53.3 us: shards(): gains = lax.psum(gains, ('section', 'tensor', 'ctx'))]
    all_gather x4 -> x10, waiting for transfers between devices: 348 us -> 280 us  [the longest x4 178 us: gather_tokens(): return lax.all_gather(rows, ('tensor', 'ctx'), axis=0, tiled=True)]
  transfers between devices with their start and end apart: 38 -> 36, of which waited for: 27 -> 26; matrix products, arithmetic and copies ran while one was open for 14% -> 14% of each run, Pallas kernels for 0% -> 0%
where the time goes in v1:
time: 1690 us; the launch traced here: 1670 us
  waiting for transfers between devices  936 us (55%)
  blocking collectives  301 us (18%)
  matrix products  202 us (12%)
  local copies, waits for them, and re-layouts  99.4 us (6%)
  other arithmetic  90 us (5%)
  starting transfers between devices  25.8 us (2%)
    reduce_scatter x4, waiting for transfers between devices, scatter_tokens(): lax.psum_scatter(rows, ('tensor', 'ctx'), scatter_dimension=0, tiled=True)  325 us
    ppermute x11, waiting for transfers between devices, swap(): return lax.ppermute(value, 'section', SWAP)  226 us
    all_gather x4, waiting for transfers between devices, gather_tokens(): return lax.all_gather(rows, ('tensor', 'ctx'), axis=0, tiled=True)  178 us
    dot_general x30, matrix products, dot(): return lax.dot_general(a, b, dims, preferred_element_type=F32)  170 us
    all_to_all x1, blocking collectives, shards(): lax.all_to_all(expand, 'ctx', split_axis=0, concat_axis=0, tiled=True)  119 us
    all_gather x6, waiting for transfers between devices, gather_ctx(): return lax.all_gather(value, 'ctx', axis=axis, tiled=True)  102 us
    all_gather x6, blocking collectives, tensor_gather(): return lax.all_gather(rows, 'tensor', axis=0, tiled=True)  60.4 us
    psum x1, blocking collectives, shards(): gains = lax.psum(gains, ('section', 'tensor', 'ctx'))  53.3 us
  transfers between devices with their start and end apart: 36, of which 26 were waited for; matrix products, arithmetic and copies ran while one was open for 14% of the time, Pallas kernels for 0%

profile of v1, /device:TPU:9, one launch (start us, length us, event | category | flops | bytes accessed | tf_op | source)
XLA Modules:
  0.0 1670.8 jit_solution(7030658594013339818)
XLA Ops:
  27.1 14.7 all-gather.3
  42.2 17.2 %all-gather.16.cloned.1.call-done = bf16[1536,1024]{1,0:T(8,128)(2,1)} async-done(((bf16[192,1024]{1,0:T(8,128)(2,1)}), bf16[1536,1024]{1,0:T(8,128)(2,1)}) %all-gather.16.cloned.1.call-update) | async-done | bytes 3145744 | tf_op jit(solution)/shard_map/all_gather | solution.py:60
  102.3 16.8 %all-gather.20.cloned.1.call-done = bf16[768,1536]{1,0:T(8,128)(2,1)} async-done(((bf16[96,1536]{1,0:T(8,128)(2,1)}), bf16[768,1536]{1,0:T(8,128)(2,1)}) %all-gather.20.cloned.1.call-update) | async-done | bytes 2359312 | tf_op jit(solution)/shard_map/all_gather | solution.py:60
  122.8 16.5 reduce-scatter.19.cloned.1.call-done
  141.4 10.9 reshape.429
  155.3 119.2 %all_to_all.10 = bf16[8,2,192,560]{3,2,1,0:T(8,128)(2,1)S(1)} all-to-all(bf16[8,2,192,560]{3,2,1,0:T(8,128)(2,1)S(1)} %copy.194), channel_id=1, replica_groups=mesh['section'=2,'tensor'=2,'ctx'=8] {'ctx'}, dimensions={0} | all-to-all | bytes 6881280 | tf_op jit(solution)/shard_map/all_to_all | solution.py:259
  284.5 73.6 %collective-permute-done.3 = bf16[2,1536,560]{1,2,0:T(8,128)(2,1)S(1)} collective-permute-done((bf16[2,1536,560]{1,2,0:T(8,128)(2,1)}, bf16[2,1536,560]{1,2,0:T(8,128)(2,1)S(1)}, u32[]{:S(2)}, u32[]{:S(2)}) %collective-permute-start.3) | collective-permute-done | bytes 3440672 | tf_op jit(solution)/shard_map/ppermute | solution.py:56
  376.0 19.1 %collective-permute-done.4 = bf16[560,1536]{1,0:T(8,128)(2,1)} collective-permute-done((bf16[560,1536]{1,0:T(8,128)(2,1)S(1)}, bf16[560,1536]{1,0:T(8,128)(2,1)}, u32[]{:S(2)}, u32[]{:S(2)}) %collective-permute-start.4) | collective-permute-done | bytes 1720352 | tf_op jit(solution)/shard_map/ppermute | solution.py:56
  402.9 14.6 all-gather.4
  418.3 72.1 %reduce-scatter.21.cloned.1.call-done = bf16[128,1536]{1,0:T(8,128)(2,1)} async-done(((bf16[2048,1536]{1,0:T(8,128)(2,1)}), bf16[128,1536]{1,0:T(8,128)(2,1)}) %reduce-scatter.21.cloned.1.call-update) | async-done | bytes 393232 | tf_op jit(solution)/shard_map/reduce_scatter | solution.py:68
  502.1 28.5 %all-gather.24.cloned.1.call-done = bf16[1536,1024]{1,0:T(8,128)(2,1)} async-done(((bf16[192,1024]{1,0:T(8,128)(2,1)}), bf16[1536,1024]{1,0:T(8,128)(2,1)}) %all-gather.24.cloned.1.call-update) | async-done | bytes 3145744 | tf_op jit(solution)/shard_map/all_gather | solution.py:60
  543.4 13.9 all-gather.26.cloned.1.call-done
  564.4 25.1 %all-gather.28.cloned.1.call-done = bf16[768,1536]{1,0:T(8,128)(2,1)} async-done(((bf16[96,1536]{1,0:T(8,128)(2,1)}), bf16[768,1536]{1,0:T(8,128)(2,1)}) %all-gather.28.cloned.1.call-update) | async-done | bytes 2359312 | tf_op jit(solution)/shard_map/all_gather | solution.py:60
  595.0 14.6 reduce-scatter.23.cloned.1.call-done
  612.3 62.8 %all-gather.34.cloned.1.call-done = bf16[1,2048,1536]{2,1,0:T(8,128)(2,1)} async-done(((bf16[1,128,1536]{2,1,0:T(8,128)(2,1)}), bf16[1,2048,1536]{2,1,0:T(8,128)(2,1)}) %all-gather.34.cloned.1.call-update) | async-done | bytes 6291472 | tf_op jit(solution)/shard_map/all_gather | solution.py:64
  684.7 53.3 %all-gather.30.cloned.1.call-done = bf16[2048,1536]{1,0:T(8,128)(2,1)} async-done(((bf16[128,1536]{1,0:T(8,128)(2,1)}), bf16[2048,1536]{1,0:T(8,128)(2,1)}) %all-gather.30.cloned.1.call-update) | async-done | bytes 6291472 | tf_op jit(solution)/shard_map/all_gather | solution.py:64
  769.4 82.6 %reduce-scatter.27.cloned.1.call-done = bf16[128,1536]{1,0:T(8,128)(2,1)} async-done(((bf16[2048,1536]{1,0:T(8,128)(2,1)}), bf16[128,1536]{1,0:T(8,128)(2,1)}) %reduce-scatter.27.cloned.1.call-update) | async-done | bytes 393232 | tf_op jit(solution)/shard_map/reduce_scatter | solution.py:68
  888.8 23.4 %reduce-scatter.43.cloned.1.call-done = bf16[128,512]{1,0:T(8,128)(2,1)} async-done(((bf16[1024,512]{1,0:T(8,128)(2,1)}), bf16[128,512]{1,0:T(8,128)(2,1)}) %reduce-scatter.43.cloned.1.call-update) | async-done | bytes 131088
  932.3 12.3 reduce-scatter.29.cloned.1.call-done
  946.6 87.3 %reduce-scatter.25.cloned.1.call-done = bf16[128,1536]{1,0:T(8,128)(2,1)} async-done(((bf16[2048,1536]{1,0:T(8,128)(2,1)}), bf16[128,1536]{1,0:T(8,128)(2,1)}) %reduce-scatter.25.cloned.1.call-update) | async-done | bytes 393232 | tf_op jit(solution)/shard_map/reduce_scatter | solution.py:68
  1037.0 62.0 %all-gather.32.cloned.1.call-done = bf16[2048,1536]{1,0:T(8,128)(2,1)} async-done(((bf16[128,1536]{1,0:T(8,128)(2,1)}), bf16[2048,1536]{1,0:T(8,128)(2,1)}) %all-gather.32.cloned.1.call-update) | async-done | bytes 6291472 | tf_op jit(solution)/shard_map/all_gather | solution.py:64
  1099.0 10.9 multiply_convert_fusion.1
  1122.9 82.9 %reduce-scatter.31.cloned.1.call-done = bf16[128,1536]{1,0:T(8,128)(2,1)} async-done(((bf16[2048,1536]{1,0:T(8,128)(2,1)}), bf16[128,1536]{1,0:T(8,128)(2,1)}) %reduce-scatter.31.cloned.1.call-update) | async-done | bytes 393232 | tf_op jit(solution)/shard_map/reduce_scatter | solution.py:68
  1249.4 16.3 reduce-scatter.45.cloned.1.call-done
  1310.7 68.9 %collective-permute-done.9 = bf16[2,1536,560]{1,2,0:T(8,128)(2,1)} collective-permute-done((bf16[2,1536,560]{1,2,0:T(8,128)(2,1)}, bf16[2,1536,560]{1,2,0:T(8,128)(2,1)}, u32[]{:S(2)}, u32[]{:S(2)}) %collective-permute-start.9) | collective-permute-done | bytes 3440672 | tf_op jit(solution)/shard_map/ppermute | solution.py:56
  1398.6 12.5 all-to-all-start.1
  1411.0 11.5 all_gather.69
  1456.2 37.8 %collective-permute-done.5 = bf16[256,1536]{1,0:T(8,128)(2,1)} collective-permute-done((bf16[256,1536]{1,0:T(8,128)(2,1)}, bf16[256,1536]{1,0:T(8,128)(2,1)}, u32[]{:S(2)}, u32[]{:S(2)}) %collective-permute-start.5) | collective-permute-done | bytes 786464 | tf_op jit(solution)/shard_map/ppermute | solution.py:56
  1500.6 20.7 %all-to-all-done.1 = bf16[8,2,192,560]{3,2,1,0:T(8,128)(2,1)} async-done(((bf16[8,2,192,560]{3,2,1,0:T(8,128)(2,1)}), bf16[8,2,192,560]{3,2,1,0:T(8,128)(2,1)}, u32[]{:S(2)}, u32[]{:S(2)}) %all-to-all-start.1) | async-done | bytes 3440672 | tf_op jit(solution)/shard_map/all_to_all | solution.py:311
  1532.1 12.5 reshape.430
  1545.8 27.9 %psum.15 = f32[2,1024]{1,0:T(2,128)S(1)} all-reduce(f32[2,1024]{1,0:T(2,128)S(1)} %pad_maximum_fusion.15), channel_id=1, replica_groups=mesh['section'=2,'tensor'=2,'ctx'=8] {'section','ctx'}, use_global_device_ids=true, to_apply=%region_33.34 | all-reduce | flops 2048 | bytes 16384 | tf_op jit(solution)/shard_map/psum | solution.py:331
  1588.9 53.3 %psum.14 = f32[2,2,1536]{2,1,0:T(2,128)S(1)} all-reduce(f32[2,2,1536]{2,1,0:T(2,128)S(1)} %pad_maximum_fusion.14), channel_id=1, replica_groups=mesh['section'=2,'tensor'=2,'ctx'=8] {'section','tensor','ctx'}, use_global_device_ids=true, to_apply=%region_28.29 | all-reduce | flops 6144 | bytes 49152 | tf_op jit(solution)/shard_map/psum | solution.py:327
  (506 shorter events, 459.0 us)
Async XLA Ops:
  7.2 52.3 %all-gather.16.cloned.1.call-start = ((), (), s32[]{:S(2)}) async-start(), calls=%async_computation.16 | async-start | bytes 3538944 | tf_op jit(solution)/shard_map/all_gather | solution.py:60
  19.4 75.6 %all-gather.18.cloned.1.call-start = ((), (), s32[]{:S(2)}) async-start(), calls=%async_computation.17 | async-start | bytes 1179648 | tf_op jit(solution)/shard_map/all_gather | solution.py:60
  64.0 55.1 %all-gather.20.cloned.1.call-start = ((), (), s32[]{:S(2)}) async-start(), calls=%async_computation.18 | async-start | bytes 2654208 | tf_op jit(solution)/shard_map/all_gather | solution.py:60
  74.6 64.7 %reduce-scatter.19.cloned.1.call-start = ((), (), s32[]{:S(2)}) async-start(), calls=%async_computation.19 | async-start | bytes 1179648 | tf_op jit(solution)/shard_map/reduce_scatter | solution.py:76
  122.5 241.3 %all-gather.22.cloned.1.call-start = ((), (), s32[]{:S(2)}) async-start(), calls=%async_computation.20 | async-start | bytes 6684672 | tf_op jit(solution)/shard_map/all_gather | solution.py:64
  141.4 349.0 %reduce-scatter.21.cloned.1.call-start = ((), (), s32[]{:S(2)}) async-start(), calls=%async_computation.21 | async-start | bytes 6684672 | tf_op jit(solution)/shard_map/reduce_scatter | solution.py:68
  283.0 75.0 %collective-permute-start.3 = (bf16[2,1536,560]{1,2,0:T(8,128)(2,1)}, bf16[2,1536,560]{1,2,0:T(8,128)(2,1)S(1)}, u32[]{:S(2)}, u32[]{:S(2)}) collective-permute-start(bf16[2,1536,560]{1,2,0:T(8,128)(2,1)} %copy.197), channel_id=1, source_target_pairs={{0,16},{16,0},{1,17},{17,1},{2,18},{18,2},{3,19},{19,3},{4,20},{20... | collective-permute-start | bytes 10321928 | tf_op jit(solution)/shard_map/ppermute | solution.py:56
  284.3 110.7 %collective-permute-start.4 = (bf16[560,1536]{1,0:T(8,128)(2,1)S(1)}, bf16[560,1536]{1,0:T(8,128)(2,1)}, u32[]{:S(2)}, u32[]{:S(2)}) collective-permute-start(bf16[560,1536]{1,0:T(8,128)(2,1)S(1)} %bitcast.413), channel_id=1, source_target_pairs={{0,16},{16,0},{1,17},{17,1},{2,18},{18,2},{3,19},{19,3},{4,20},{20... | collective-permute-start | bytes 5160968 | tf_op jit(solution)/shard_map/ppermute | solution.py:56
  402.1 128.5 %all-gather.24.cloned.1.call-start = ((), (), s32[]{:S(2)}) async-start(), calls=%async_computation.22 | async-start | bytes 3538944 | tf_op jit(solution)/shard_map/all_gather | solution.py:60
  402.8 154.4 %all-gather.26.cloned.1.call-start = ((), (), s32[]{:S(2)}) async-start(), calls=%async_computation.23 | async-start | bytes 1179648 | tf_op jit(solution)/shard_map/all_gather | solution.py:60
  534.9 54.5 %all-gather.28.cloned.1.call-start = ((), (), s32[]{:S(2)}) async-start(), calls=%async_computation.24 | async-start | bytes 2654208 | tf_op jit(solution)/shard_map/all_gather | solution.py:60
  535.7 73.9 %reduce-scatter.23.cloned.1.call-start = ((), (), s32[]{:S(2)}) async-start(), calls=%async_computation.25 | async-start | bytes 1179648 | tf_op jit(solution)/shard_map/reduce_scatter | solution.py:76
  592.8 82.3 %all-gather.34.cloned.1.call-start = ((), (), s32[]{:S(2)}) async-start(), calls=%async_computation.37 | async-start | bytes 6684672 | tf_op jit(solution)/shard_map/all_gather | solution.py:64
  594.7 143.3 %all-gather.30.cloned.1.call-start = ((), (), s32[]{:S(2)}) async-start(), calls=%async_computation.26 | async-start | bytes 6684672 | tf_op jit(solution)/shard_map/all_gather | solution.py:64
  612.3 239.8 %reduce-scatter.27.cloned.1.call-start = ((), (), s32[]{:S(2)}) async-start(), calls=%async_computation.28 | async-start | bytes 6684672 | tf_op jit(solution)/shard_map/reduce_scatter | solution.py:68
  769.4 142.8 %reduce-scatter.43.cloned.1.call-start = ((), (), s32[]{:S(2)}) async-start(), calls=%async_computation.38 | async-start | bytes 1179648
  884.8 59.9 %reduce-scatter.29.cloned.1.call-start = ((), (), s32[]{:S(2)}) async-start(), calls=%async_computation.29 | async-start | bytes 1179648 | tf_op jit(solution)/shard_map/reduce_scatter | solution.py:76
  922.5 111.3 %reduce-scatter.25.cloned.1.call-start = ((), (), s32[]{:S(2)}) async-start(), calls=%async_computation.27 | async-start | bytes 6684672 | tf_op jit(solution)/shard_map/reduce_scatter | solution.py:68
  931.6 167.3 %all-gather.32.cloned.1.call-start = ((), (), s32[]{:S(2)}) async-start(), calls=%async_computation.30 | async-start | bytes 6684672 | tf_op jit(solution)/shard_map/all_gather | solution.py:64
  1036.6 169.2 %reduce-scatter.31.cloned.1.call-start = ((), (), s32[]{:S(2)}) async-start(), calls=%async_computation.31 | async-start | bytes 6684672 | tf_op jit(solution)/shard_map/reduce_scatter | solution.py:68
  1122.7 143.1 %reduce-scatter.45.cloned.1.call-start = ((), (), s32[]{:S(2)}) async-start(), calls=%async_computation.39 | async-start | bytes 1179648
  1238.3 335.5 %reduce-scatter.33.cloned.1.call-start = ((), (), s32[]{:S(2)}) async-start(), calls=%async_computation.32 | async-start | bytes 1179648 | tf_op jit(solution)/shard_map/reduce_scatter | solution.py:76
  1272.0 372.1 %reduce-scatter.41.cloned.1.call-start = ((), (), s32[]{:S(2)}) async-start(), calls=%async_computation.36 | async-start | bytes 2654208 | tf_op jit(solution)/shard_map/reduce_scatter | solution.py:320
  1274.3 369.8 %reduce-scatter.39.cloned.1.call-start = ((), (), s32[]{:S(2)}) async-start(), calls=%async_computation.35 | async-start | bytes 2654208 | tf_op jit(solution)/shard_map/reduce_scatter | solution.py:320
  1286.0 361.8 %reduce-scatter.37.cloned.1.call-start = ((), (), s32[]{:S(2)}) async-start(), calls=%async_computation.34 | async-start | bytes 3538944 | tf_op jit(solution)/shard_map/reduce_scatter | solution.py:320
  1306.6 73.0 %collective-permute-start.9 = (bf16[2,1536,560]{1,2,0:T(8,128)(2,1)}, bf16[2,1536,560]{1,2,0:T(8,128)(2,1)}, u32[]{:S(2)}, u32[]{:S(2)}) collective-permute-start(bf16[2,1536,560]{1,2,0:T(8,128)(2,1)} %select_convert_fusion), channel_id=1, source_target_pairs={{0,16},{16,0},{1,17},{17,1},{2,18},{18,2},{3,19},{19,3},{4,20},{20... | collective-permute-start | bytes 10321928 | tf_op jit(solution)/shard_map/ppermute | solution.py:56
  1398.6 122.8 %all-to-all-start.1 = ((bf16[8,2,192,560]{3,2,1,0:T(8,128)(2,1)}), bf16[8,2,192,560]{3,2,1,0:T(8,128)(2,1)}, u32[]{:S(2)}, u32[]{:S(2)}) async-start(bf16[8,2,192,560]{3,2,1,0:T(8,128)(2,1)} %copy.235), calls=%async_computation.13 | async-start | bytes 7864320 | tf_op jit(solution)/shard_map/all_to_all | solution.py:311
  1411.0 236.8 %reduce-scatter.35.cloned.1.call-start = ((), (), s32[]{:S(2)}) async-start(), calls=%async_computation.33 | async-start | bytes 3538944 | tf_op jit(solution)/shard_map/reduce_scatter | solution.py:320
  1438.9 57.6 %collective-permute-start.10 = (bf16[560,1536]{1,0:T(8,128)(2,1)}, bf16[560,1536]{1,0:T(8,128)(2,1)}, u32[]{:S(2)}, u32[]{:S(2)}) collective-permute-start(bf16[560,1536]{1,0:T(8,128)(2,1)} %get-tuple-element.132), channel_id=1, source_target_pairs={{0,16},{16,0},{1,17},{17,1},{2,18},{18,2},{3,19},{19,3},{4,20},{20... | collective-permute-start | bytes 5160968 | tf_op jit(solution)/shard_map/ppermute | solution.py:56
  1441.3 52.7 %collective-permute-start.5 = (bf16[256,1536]{1,0:T(8,128)(2,1)}, bf16[256,1536]{1,0:T(8,128)(2,1)}, u32[]{:S(2)}, u32[]{:S(2)}) collective-permute-start(bf16[256,1536]{1,0:T(8,128)(2,1)} %broadcast_select_fusion.10), channel_id=1, source_target_pairs={{0,16},{16,0},{1,17},{17,1},{2,18},{18,2},{3,19},{19,3},{4,20},{20... | collective-permute-start | bytes 2359304 | tf_op jit(solution)/shard_map/ppermute | solution.py:56
  1586.0 56.8 %collective-permute-start.6 = (bf16[256,1536]{1,0:T(8,128)(2,1)S(1)}, bf16[256,1536]{1,0:T(8,128)(2,1)}, u32[]{:S(2)}, u32[]{:S(2)}) collective-permute-start(bf16[256,1536]{1,0:T(8,128)(2,1)S(1)} %broadcast_select_fusion.6), channel_id=1, source_target_pairs={{0,16},{16,0},{1,17},{17,1},{2,18},{18,2},{3,19},{19,3},{4,20},{20... | collective-permute-start | bytes 2359304 | tf_op jit(solution)/shard_map/ppermute | solution.py:56
  1649.1 11.6 collective-permute-start.7
  (115 other events, 3415.2 us)
Sparse Core Ops, SparseCore 0:
  19.6 39.8 all-gather.15
  64.1 22.1 all-gather.17
  88.6 30.5 all-gather.19
  122.6 16.6 reduce-scatter.18
  142.2 99.3 all-gather.21
  402.2 88.1 reduce-scatter.20
  492.6 37.9 all-gather.23
  535.0 22.1 all-gather.25
  558.9 30.5 all-gather.27
  592.9 16.6 reduce-scatter.22
  612.8 62.2 all-gather.33
  677.5 60.4 all-gather.29
  769.5 82.4 reduce-scatter.26
  884.9 27.2 reduce-scatter.42
  922.6 21.9 reduce-scatter.28
  949.5 84.2 reduce-scatter.24
  1036.7 62.2 all-gather.31
  1122.8 82.9 reduce-scatter.30
  1238.4 27.3 reduce-scatter.44
  1272.1 22.1 reduce-scatter.32
  1296.6 31.8 reduce-scatter.40
  1330.8 35.1 reduce-scatter.38
  1368.3 42.2 reduce-scatter.36
  1446.6 83.1 reduce-scatter.34

commit v2 on v1

v2 whole, which is shorter than its diff:
```python
import functools
import functools
import math

import jax
import jax.numpy as jnp
from jax import lax
from jax.experimental import pallas as pl
from jax.experimental.pallas import tpu as pltpu
from jax.sharding import PartitionSpec as P

EPSILON = 1e-06
ROPE_BASE = 1000000.0
ROWS = (((0,), (0,)), ((), ()))
LAST = (((1,), (1,)), ((), ()))
F32 = jnp.float32
BF16 = jnp.bfloat16
SWAP = [(0, 1), (1, 0)]
MESH = pl.DeviceIdType.MESH
VMEM = pl.BlockSpec(memory_space=pltpu.VMEM)
HBM = pl.BlockSpec(memory_space=pl.ANY)


def dot(a, b, dims=(((1,), (0,)), ((), ()))):
    return lax.dot_general(a, b, dims, preferred_element_type=F32)


def angles(positions, head_dim):
    half_dim = head_dim // 2
    frequency = ROPE_BASE ** (-(jnp.arange(half_dim, dtype=F32) * 2.0) / head_dim)
    phases = positions.astype(F32)[:, None] * frequency[None, :]
    phases = jnp.concatenate([phases, phases], axis=-1)
    return jnp.cos(phases), jnp.sin(phases)


def rotate(values, cosine, sine):
    half = values.shape[-1] // 2
    turned = jnp.concatenate([-values[..., half:], values[..., :half]], axis=-1)
    return values * cosine + turned * sine


def unrotate(grads, cosine, sine):
    half = grads.shape[-1] // 2
    twisted = grads * sine
    turned = jnp.concatenate([twisted[..., half:], -twisted[..., :half]], axis=-1)
    return grads * cosine + turned


def inverse_root(values):
    return lax.rsqrt(jnp.mean(values * values, axis=-1, keepdims=True) + EPSILON)


def norm_backward(values, root, gain, grad_normed):
    normal = values * root
    gain_grad = jnp.sum(grad_normed * normal, axis=0)
    scaled = grad_normed * gain
    mean = jnp.mean(scaled * normal, axis=-1, keepdims=True)
    return root * (scaled - normal * mean), gain_grad


def swap(value):
    return lax.ppermute(value, "section", SWAP)


def gather_ctx(value, axis):
    return lax.all_gather(value, "ctx", axis=axis, tiled=True)


def gather_tokens(rows):
    return lax.all_gather(rows, ("ctx", "tensor"), axis=0, tiled=True)


def scatter_tokens(rows):
    return lax.psum_scatter(rows, ("ctx", "tensor"), scatter_dimension=0, tiled=True).astype(F32)


def tensor_gather(rows):
    return lax.all_gather(rows, "tensor", axis=0, tiled=True)


def tensor_scatter(rows):
    mine = lax.axis_index("tensor")
    tokens = rows.shape[0] // 2
    own = lax.dynamic_slice_in_dim(rows, mine * tokens, tokens, 0)
    other = lax.dynamic_slice_in_dim(rows, (1 - mine) * tokens, tokens, 0)
    return own + lax.ppermute(other.astype(BF16), "tensor", SWAP).astype(F32)


def greet_all(size, me):
    barrier = pltpu.get_barrier_semaphore()
    for step in range(1, size):
        pl.semaphore_signal(
            barrier, inc=1, device_id={"ctx": (me + step) % size}, device_id_type=MESH
        )
    there = 1 - lax.axis_index("section")
    pl.semaphore_signal(barrier, inc=1, device_id={"section": there}, device_id_type=MESH)
    pl.semaphore_wait(barrier, size)


def by_distance(size):
    return sorted(range(size), key=lambda step: min(step, size - step))


def share_kernel(size, from_ref, all_ref, send, recv, over_send, over_recv, local):
    me = lax.axis_index("ctx")
    section = lax.axis_index("section")
    greet_all(size, me)

    def copy(there, source):
        return remote(
            from_ref.at[:, there],
            all_ref.at[section, :, source],
            send.at[there],
            recv.at[source],
            {"ctx": there},
        )

    def over(block, source):
        return remote(
            block,
            all_ref.at[section, :, source],
            over_send.at[source],
            over_recv.at[source],
            {"section": 1 - section},
        )

    own = pltpu.make_async_copy(from_ref.at[:, me], all_ref.at[section, :, me], local)
    own.start()
    over(from_ref.at[:, me], me).start()
    order = by_distance(size)[1:]

    def pass_on(step):
        source = (me + size - step) % size
        copy(source, source).wait_recv()
        over(all_ref.at[section, :, source], source).start()
        copy((me + step) % size, me).wait_send()

    for index, step in enumerate(order):
        copy((me + step) % size, me).start()
        if index > 0:
            pass_on(order[index - 1])
    pass_on(order[-1])
    own.wait()
    for step in range(size):
        source = (me + step) % size
        over(all_ref.at[section, :, source], source).wait()


def share(blocks):
    size = blocks.shape[1]
    if size != 8:
        moved = lax.all_to_all(blocks, "ctx", split_axis=1, concat_axis=1, tiled=True)
        return lax.all_gather(moved, "section")
    dma = pltpu.SemaphoreType.DMA
    return pl.pallas_call(
        functools.partial(share_kernel, size),
        out_shape=jax.ShapeDtypeStruct((2,) + blocks.shape, blocks.dtype),
        in_specs=[HBM],
        out_specs=HBM,
        scratch_shapes=[dma((size,)), dma((size,)), dma((size,)), dma((size,)), dma],
        compiler_params=pltpu.CompilerParams(collective_id=5, has_side_effects=True),
        cost_estimate=pl.CostEstimate(flops=blocks.size, bytes_accessed=1024, transcendentals=0),
        name="share",
    )(blocks)


def collect_kernel(
    size, first_ref, second_ref, to_ref, own, other, send, recv, over_send, over_recv, local, store
):
    me = lax.axis_index("ctx")
    section = lax.axis_index("section")
    greet_all(size, me)
    order = by_distance(size)[::-1]

    def over(source_ref, at):
        return remote(
            source_ref.at[:, at], other.at[at], over_send.at[at], over_recv.at[at],
            {"section": 1 - section},
        )

    def load(source_ref, at):
        return pltpu.make_async_copy(source_ref.at[:, at], own.at[at], local.at[at])

    def copy(there, source):
        return remote(
            own.at[there], to_ref.at[:, source], send.at[there], recv.at[source], {"ctx": there}
        )

    def start(at):
        @pl.when(section == 0)
        def _():
            over(second_ref, at).start()
            load(first_ref, at).start()

        @pl.when(section == 1)
        def _():
            over(first_ref, at).start()
            load(second_ref, at).start()

    for index, step in enumerate(order):
        at = (me + step) % size
        if index == 0:
            start(at)
        if index + 1 < size:
            start((me + order[index + 1]) % size)
        over(first_ref, at).wait()
        load(first_ref, at).wait()
        own[at] = (own[at].astype(F32) + other[at].astype(F32)).astype(own.dtype)
        if step > 0:
            copy(at, me).start()
        else:
            mine = pltpu.make_async_copy(own.at[at], to_ref.at[:, me], store)
            mine.start()
            mine.wait()
    for step in order:
        at = (me + step) % size
        if step > 0:
            copy(at, at).wait_recv()
            copy(at, me).wait_send()


def collect(first, second, is_first):
    parts, size, rows, columns = first.shape
    if size != 8:
        received = lax.ppermute(jnp.where(is_first, second, first), "section", SWAP)
        total = jnp.where(is_first, first, second).astype(F32) + received.astype(F32)
        return lax.all_to_all(
            total.astype(BF16), "ctx", split_axis=1, concat_axis=1, tiled=True
        )
    dma = pltpu.SemaphoreType.DMA
    block = pltpu.VMEM((size, parts, rows, columns), first.dtype)
    return pl.pallas_call(
        functools.partial(collect_kernel, size),
        out_shape=jax.ShapeDtypeStruct(first.shape, first.dtype),
        in_specs=[HBM, HBM],
        out_specs=HBM,
        scratch_shapes=[block, block]
        + [dma((size,)), dma((size,)), dma((size,)), dma((size,)), dma((size,)), dma],
        compiler_params=pltpu.CompilerParams(
            collective_id=6, has_side_effects=True, vmem_limit_bytes=24 << 20
        ),
        cost_estimate=pl.CostEstimate(flops=first.size, bytes_accessed=1024, transcendentals=0),
        name="collect",
    )(first, second)


def remote(src, dst, send, recv, device):
    return pltpu.make_async_remote_copy(
        src_ref=src, dst_ref=dst, send_sem=send, recv_sem=recv, device_id=device, device_id_type=MESH
    )


def spread_kernel(chunk, piece, layer, planes, ins, outs, extra, own_ref, *refs):
    in_refs, refs = refs[:ins], refs[ins:]
    all_ref, sum_ref = refs[:2]
    out_refs, refs = refs[2 : 2 + outs], refs[2 + outs :]
    work_refs, refs = refs[:extra], refs[extra:]
    (expand_w, load_sem), refs = refs[:2], refs[2:]
    load = pltpu.make_async_copy(in_refs[0].at[layer], expand_w, load_sem)
    load.start()
    in_refs = (expand_w,) + in_refs[1:]
    (land, core_out, core_in, y_out, y_in, z_out, z_in, both, kept,
     zs, zr, ys, yr, cs, cr, rcs, rcr, rys, ryr, rzs, rzr, local) = refs
    tensor = lax.axis_index("tensor")
    ctx = lax.axis_index("ctx")
    plane, core = ctx // 2, ctx % 2
    rows = own_ref.shape[0]
    y_peer = {"tensor": 1 - tensor}
    core_peer = {"ctx": plane * 2 + 1 - core}

    barrier = pltpu.get_barrier_semaphore()
    pl.semaphore_signal(barrier, inc=1, device_id=y_peer, device_id_type=MESH)
    pl.semaphore_signal(barrier, inc=1, device_id=core_peer, device_id_type=MESH)
    for step in range(1, planes):
        there = (plane + step) % planes
        pl.semaphore_signal(barrier, inc=1, device_id={"ctx": there * 2 + core}, device_id_type=MESH)
    pl.semaphore_wait(barrier, planes + 1)

    def block(at, which_core, which_tensor):
        start = pl.multiple_of(((at * 2 + which_core) * 2 + which_tensor) * rows, rows)
        return land.at[pl.ds(start, rows)]

    def along(at, target, direction):
        ref = block(at, core, tensor)
        return remote(ref, ref, zs.at[at, direction], zr.at[at], {"ctx": target * 2 + core})

    def across(at, which_tensor):
        ref = block(at, core, which_tensor)
        return remote(ref, ref, ys.at[at], yr.at[at], y_peer)

    def beside(at, which_core, which_tensor, slot):
        ref = block(at, which_core, which_tensor)
        return remote(ref, ref, cs.at[at, slot], cr.at[at, slot], core_peer)

    start = pl.multiple_of(((plane * 2 + core) * 2 + tensor) * rows, rows)
    land[pl.ds(start, rows)] = own_ref[...]

    @pl.when(plane < planes - 1)
    def _():
        along(plane, plane + 1, 0).start()

    @pl.when(plane > 0)
    def _():
        along(plane, plane - 1, 1).start()

    across(plane, tensor).start()
    beside(plane, core, tensor, 0).start()

    def reduce_core(at):
        return remote(core_out.at[at], core_in.at[at], rcs.at[at], rcr.at[at], core_peer)

    def reduce_y(at):
        return remote(y_out.at[at], y_in.at[at], rys.at[at], ryr.at[at], y_peer)

    def reduce_z(at):
        return remote(z_out.at[at], z_in.at[plane], rzs.at[at], rzr.at[plane], {"ctx": at * 2 + core})

    def reduced_z(at):
        return remote(z_out.at[at], z_in.at[at], rzs.at[at], rzr.at[at], {"ctx": at * 2 + core})

    def save(at):
        span = pl.ds(pl.multiple_of(at * 4 * rows, 4 * rows), 4 * rows)
        return pltpu.make_async_copy(land.at[span], all_ref.at[span], local.at[at])

    def side_plane(distance, side):
        return plane + distance * (2 * side - 1)

    def inside(at):
        return jnp.logical_and(at >= 0, at < planes)

    def pass_on(distance, side):
        at = side_plane(distance, side)
        target = plane + 1 - 2 * side

        @pl.when(inside(at))
        def _():
            along(at, plane, 0).wait_recv()

            @pl.when(inside(target))
            def _():
                along(at, target, side).start()

            across(at, tensor).start()
            beside(at, core, tensor, 0).start()

    def pass_beside(distance, side):
        at = side_plane(distance, side)

        @pl.when(inside(at))
        def _():
            across(at, 1 - tensor).wait_recv()
            beside(at, core, 1 - tensor, 1).start()

    def step(index, carry):
        distance = (index + 1) // 2
        at = side_plane(distance, 1 - index % 2)

        @pl.when(jnp.logical_or(index == 0, index % 2 == 1))
        def _():
            pass_on(distance + 1, 0)
            pass_on(distance + 1, 1)

            @pl.when(distance > 0)
            def _():
                pass_beside(distance, 0)

            pass_beside(distance, 1)

        @pl.when(inside(at))
        def _():
            beside(at, 1 - core, tensor, 0).wait_recv()
            beside(at, 1 - core, 1 - tensor, 1).wait_recv()
            if piece is None:
                save(at).start()
            theirs = pl.multiple_of((at * 2 + 1 - core) * 2 * rows, 2 * rows)
            core_out[at] = chunk(land, theirs, 2 * rows, in_refs, out_refs, work_refs).astype(BF16)
            reduce_core(at).start()
            mine = pl.multiple_of((at * 2 + core) * 2 * rows, 2 * rows)
            both[...] = chunk(land, mine, 2 * rows, in_refs, out_refs, work_refs)
            reduce_core(at).wait_recv()
            both[...] += core_in[at].astype(F32)
            other = pl.multiple_of((1 - tensor) * rows, rows)
            own = pl.multiple_of(tensor * rows, rows)
            y_out[at] = both[pl.ds(other, rows)].astype(BF16)

            @pl.when(index > 0)
            def _():
                reduce_y(at).start()

            kept[at] = both[pl.ds(own, rows)]

        return carry

    load.wait()
    lax.fori_loop(0, 2 * planes - 1, step, 0)

    reduce_y(plane).start()

    def collect(index, count):
        at = side_plane((index + 2) // 2, index % 2)

        @pl.when(inside(at))
        def _():
            if piece is not None:
                piece(land, count, planes, in_refs, out_refs, work_refs)
            reduce_y(at).wait_recv()
            z_out[at] = (kept[at] + y_in[at].astype(F32)).astype(BF16)
            reduce_z(at).start()

        return count + inside(at).astype(jnp.int32)

    count = lax.fori_loop(0, 2 * planes - 2, collect, 0)
    if piece is not None:
        piece(land, count, planes, in_refs, out_refs, work_refs)
    reduce_y(plane).wait_recv()
    sum_ref[...] = kept[plane] + y_in[plane].astype(F32)

    def finish(index, carry):
        at = (plane + 1 + index) % planes
        reduced_z(at).wait_recv()
        sum_ref[...] += z_in[at].astype(F32)
        return carry

    lax.fori_loop(0, planes - 1, finish, 0)

    @pl.when(plane < planes - 1)
    def _():
        along(plane, plane + 1, 0).wait_send()

    @pl.when(plane > 0)
    def _():
        along(plane, plane - 1, 1).wait_send()

    def drain(index, carry):
        distance = (index + 1) // 2
        side = 1 - index % 2
        at = side_plane(distance, side)
        target = plane + 1 - 2 * side

        @pl.when(inside(at))
        def _():
            @pl.when(jnp.logical_and(index > 0, inside(target)))
            def _():
                along(at, target, side).wait_send()

            across(at, tensor).wait_send()
            beside(at, core, tensor, 0).wait_send()
            beside(at, core, 1 - tensor, 1).wait_send()
            if piece is None:
                save(at).wait()
            reduce_core(at).wait_send()
            reduce_y(at).wait_send()

            @pl.when(index > 0)
            def _():
                reduce_z(at).wait_send()

        return carry

    lax.fori_loop(0, 2 * planes - 1, drain, 0)


def spread(chunk, piece, own, inputs, layer, outputs, work, planes, ident, name):
    rows, width = own.shape
    count = planes * 4 * rows
    dma = pltpu.SemaphoreType.DMA
    shape = jax.ShapeDtypeStruct
    saved = (count, width) if piece is None else (16, width)
    outs = [shape(saved, BF16), shape((rows, width), F32)] + list(outputs)
    return pl.pallas_call(
        functools.partial(
            spread_kernel, chunk, piece, layer, planes, len(inputs), len(outputs), len(work)
        ),
        out_shape=outs,
        in_specs=[VMEM, HBM] + [VMEM] * (len(inputs) - 1),
        out_specs=[HBM, VMEM] + [VMEM] * len(outputs),
        scratch_shapes=list(work)
        + [
            pltpu.VMEM(inputs[0].shape[1:], BF16),
            pltpu.SemaphoreType.DMA,
            pltpu.VMEM((count, width), BF16),
            pltpu.VMEM((planes, 2 * rows, width), BF16),
            pltpu.VMEM((planes, 2 * rows, width), BF16),
            pltpu.VMEM((planes, rows, width), BF16),
            pltpu.VMEM((planes, rows, width), BF16),
            pltpu.VMEM((planes, rows, width), BF16),
            pltpu.VMEM((planes, rows, width), BF16),
            pltpu.VMEM((2 * rows, width), F32),
            pltpu.VMEM((planes, rows, width), F32),
            dma((planes, 2)), dma((planes,)), dma((planes,)), dma((planes,)), dma((planes, 2)), dma((planes, 2)),
            dma((planes,)), dma((planes,)), dma((planes,)), dma((planes,)), dma((planes,)), dma((planes,)), dma((planes,)),
        ],
        compiler_params=pltpu.CompilerParams(collective_id=ident + 10 * layer, has_side_effects=True, vmem_limit_bytes=62 << 20),
        cost_estimate=pl.CostEstimate(
            flops=count * width, bytes_accessed=count, transcendentals=0
        ),
        name=name,
    )(own, *inputs)


def mlp_chunk(land, start, rows, in_refs, out_refs, work_refs):
    expand_w, down_w = in_refs
    gate_slope, up_slope, hidden_ref = out_refs
    span = pl.ds(start, rows)
    x = land[span]
    gate = dot(x, expand_w[0])
    up = dot(x, expand_w[1])
    sig = jax.nn.sigmoid(gate)
    silu = gate * sig
    hidden = (silu * up).astype(BF16)
    gate_slope[span] = (up * sig * (1.0 + gate * (1.0 - sig))).astype(BF16)
    up_slope[span] = silu.astype(BF16)
    hidden_ref[span] = hidden
    return dot(hidden, down_w[...])


def mlp_back_chunk(land, start, rows, in_refs, out_refs, work_refs):
    expand_w, down_w, gate_slope, up_slope = in_refs[:4]
    gate_ref, up_ref = work_refs
    span = pl.ds(start, rows)
    grad_hidden = dot(land[span], down_w[...], LAST)
    grad_gate = (grad_hidden * gate_slope[span].astype(F32)).astype(BF16)
    grad_up = (grad_hidden * up_slope[span].astype(F32)).astype(BF16)
    gate_ref[span] = grad_gate
    up_ref[span] = grad_up
    return dot(grad_gate, expand_w[0], LAST) + dot(grad_up, expand_w[1], LAST)


def mlp_back_piece(land, index, pieces, in_refs, out_refs, work_refs):
    normed, hidden = in_refs[4:]
    gate_ref, up_ref = work_refs
    d_expand, d_down = out_refs
    size = d_expand.shape[1] // pieces
    span = pl.ds(pl.multiple_of(index * size, size), size)
    rows = normed[:, span]
    d_expand[0, span] = dot(rows, gate_ref[...], ROWS).astype(BF16)
    d_expand[1, span] = dot(rows, up_ref[...], ROWS).astype(BF16)
    d_down[:, span] = dot(hidden[...], land[:, span], ROWS).astype(BF16)


def mlp_forward(own, expand, layer, down_w, planes):
    count = planes * 4 * own.shape[0]
    shape = jax.ShapeDtypeStruct((count, down_w.shape[0]), BF16)
    return spread(
        mlp_chunk,
        None,
        own,
        (expand, down_w),
        layer,
        (shape,) * 3,
        (),
        planes,
        1,
        "mlp_forward",
    )


def mlp_backward(own, expand, layer, down_w, gate_slope, up_slope, normed, hidden, planes):
    d_expand = jax.ShapeDtypeStruct(expand.shape[1:], BF16)
    reduce = jax.ShapeDtypeStruct(down_w.shape, BF16)
    work = pltpu.VMEM(gate_slope.shape, BF16)
    return spread(
        mlp_back_chunk,
        mlp_back_piece,
        own,
        (expand, down_w, gate_slope, up_slope, normed, hidden),
        layer,
        (d_expand, reduce),
        (work, work),
        planes,
        2,
        "mlp_backward",
    )[1:]


def feed_forward(own, expand_layer, down_w):
    planes = lax.axis_size("ctx") // 2
    if planes == 4:
        return mlp_forward(own, *expand_layer, down_w, planes)
    expand = expand_layer[0][expand_layer[1]]
    rows = gather_tokens(own)
    gate, up = dot(rows, expand[0]), dot(rows, expand[1])
    sig = jax.nn.sigmoid(gate)
    silu = gate * sig
    hidden = (silu * up).astype(BF16)
    gate_slope = (up * sig * (1.0 + gate * (1.0 - sig))).astype(BF16)
    total = scatter_tokens(dot(hidden, down_w).astype(BF16))
    return rows, total, gate_slope, silu.astype(BF16), hidden


def feed_backward(own, expand_layer, down_w, gate_slope, up_slope, normed, hidden):
    planes = lax.axis_size("ctx") // 2
    if planes == 4:
        return mlp_backward(
            own, *expand_layer, down_w, gate_slope, up_slope, normed, hidden, planes
        )
    expand = expand_layer[0][expand_layer[1]]
    rows = gather_tokens(own)
    grad_hidden = dot(rows, down_w, LAST)
    grad_gate = (grad_hidden * gate_slope.astype(F32)).astype(BF16)
    grad_up = (grad_hidden * up_slope.astype(F32)).astype(BF16)
    part = dot(grad_gate, expand[0], LAST) + dot(grad_up, expand[1], LAST)
    return (
        scatter_tokens(part.astype(BF16)),
        jnp.stack([dot(normed, grad_gate, ROWS), dot(normed, grad_up, ROWS)]).astype(BF16),
        dot(hidden, rows, ROWS).astype(BF16),
    )


def greet_line(planes, plane, core):
    barrier = pltpu.get_barrier_semaphore()
    pl.semaphore_signal(
        barrier, inc=1, device_id={"ctx": plane * 2 + 1 - core}, device_id_type=MESH
    )
    for step in range(1, planes):
        there = (plane + step) % planes
        pl.semaphore_signal(
            barrier, inc=1, device_id={"ctx": there * 2 + core}, device_id_type=MESH
        )
    pl.semaphore_wait(barrier, planes)


def attend_kernel(
    planes, heads, q_ref, kv_ref, qpos_ref, kpos_ref, out_ref, low_ref, log_ref, all_ref,
    zs, zr, cs, cr,
):
    ctx = lax.axis_index("ctx")
    plane, core = ctx // 2, ctx % 2
    batch, tokens, pair = kv_ref.shape
    head_dim = pair // 2
    factor = 1.0 / math.sqrt(head_dim)
    greet_line(planes, plane, core)
    core_peer = {"ctx": plane * 2 + 1 - core}

    def block(at):
        return all_ref.at[:, pl.ds(pl.multiple_of(at * tokens, tokens), tokens)]

    def along(there, source):
        ref = block(source * 2 + core)
        return remote(ref, ref, zs.at[there], zr.at[source], {"ctx": there * 2 + core})

    def beside(source, which):
        ref = block(source * 2 + which)
        return remote(ref, ref, cs.at[source], cr.at[source], core_peer)

    all_ref[:, pl.ds(pl.multiple_of(ctx * tokens, tokens), tokens)] = kv_ref[...]
    for step in range(1, planes):
        along((plane + step) % planes, plane).start()
    beside(plane, core).start()
    for step in range(1, planes):
        source = (plane + step) % planes
        along(source, source).wait_recv()
        beside(source, core).start()
    for step in range(planes):
        beside((plane + step) % planes, 1 - core).wait_recv()

    def one(index, carry):
        rows = pl.ds(pl.multiple_of(index * tokens, tokens), tokens)
        keys = all_ref[index, :, :head_dim]
        values = all_ref[index, :, head_dim:]
        allowed = qpos_ref[index] >= kpos_ref[index]
        lane = lax.broadcasted_iota(jnp.int32, (tokens, head_dim), 1)
        logs = jnp.zeros((tokens, head_dim), F32)
        for head in range(heads):
            span = slice(head * head_dim, (head + 1) * head_dim)
            scores = dot(q_ref[rows, span], keys, LAST)
            scores = jnp.where(allowed, scores * factor, -1e30)
            top = jnp.max(scores, axis=1, keepdims=True)
            weights = jnp.exp(scores - top)
            total = jnp.sum(weights, axis=1, keepdims=True)
            logs = jnp.where(lane == head, top + jnp.log(total), logs)
            out = dot((weights * (1.0 / total)).astype(BF16), values)
            out_ref[rows, span] = out
            low_ref[rows, span] = out.astype(BF16)
        log_ref[rows] = logs
        return carry

    lax.fori_loop(0, batch, one, 0)
    for step in range(1, planes):
        along((plane + step) % planes, plane).wait_send()
        beside((plane + step) % planes, core).wait_send()
    beside(plane, core).wait_send()


def attend_back_kernel(
    planes, heads, q_ref, kv_ref, qpos_ref, kpos_ref, grad_ref, out_ref, log_ref, dq_ref, dkv_ref,
    whole, core_out, core_in, z_out, z_in, cs, cr, zs, zr,
):
    ctx = lax.axis_index("ctx")
    plane, core = ctx // 2, ctx % 2
    batch = qpos_ref.shape[0]
    tokens = q_ref.shape[0] // batch
    head_dim = kv_ref.shape[2] // 2
    factor = 1.0 / math.sqrt(head_dim)
    greet_line(planes, plane, core)
    core_peer = {"ctx": plane * 2 + 1 - core}

    def to_core(index):
        return remote(core_out.at[index], core_in.at[index], cs.at[index], cr.at[index], core_peer)

    def to_plane(index, there, source):
        return remote(
            z_out.at[index, there],
            z_in.at[index, source],
            zs.at[index, there],
            zr.at[index, source],
            {"ctx": there * 2 + core},
        )

    def one(index, carry):
        rows = pl.ds(pl.multiple_of(index * tokens, tokens), tokens)
        keys = kv_ref[index, :, :head_dim]
        values = kv_ref[index, :, head_dim:]
        allowed = qpos_ref[index] >= kpos_ref[index]
        logs = log_ref[rows]
        for head in range(heads):
            span = slice(head * head_dim, (head + 1) * head_dim)
            queries = q_ref[rows, span]
            grads = grad_ref[rows, span]
            delta = jnp.sum(grads.astype(F32) * out_ref[rows, span], axis=1, keepdims=True)
            scores = jnp.where(allowed, dot(queries, keys, LAST) * factor, -1e30)
            weights = jnp.exp(scores - logs[:, head : head + 1])
            grad_scores = (weights * (dot(grads, values, LAST) - delta) * factor).astype(BF16)
            dq_ref[rows, span] = dot(grad_scores, keys)
            grad_keys = dot(grad_scores, queries, ROWS)
            grad_values = dot(weights.astype(BF16), grads, ROWS)
            if head == 0:
                whole[index, :, :head_dim] = grad_keys
                whole[index, :, head_dim:] = grad_values
            else:
                whole[index, :, :head_dim] += grad_keys
                whole[index, :, head_dim:] += grad_values

        for at in range(planes):
            theirs = pl.multiple_of((at * 2 + 1 - core) * tokens, tokens)
            core_out[index, at] = whole[index, pl.ds(theirs, tokens)].astype(BF16)
        to_core(index).start()
        return carry

    lax.fori_loop(0, batch, one, 0)

    def mine(index, at):
        start = pl.multiple_of((at * 2 + core) * tokens, tokens)
        return whole[index, pl.ds(start, tokens)] + core_in[index, at].astype(F32)

    for index in range(batch):
        to_core(index).wait_recv()
        for step in range(1, planes):
            there = (plane + step) % planes
            z_out[index, there] = mine(index, there).astype(BF16)
            to_plane(index, there, plane).start()
        dkv_ref[index] = mine(index, plane)
    for index in range(batch):
        for step in range(1, planes):
            source = (plane + step) % planes
            to_plane(index, source, source).wait_recv()
            dkv_ref[index] += z_in[index, source].astype(F32)
    for index in range(batch):
        to_core(index).wait_send()
        for step in range(1, planes):
            to_plane(index, (plane + step) % planes, plane).wait_send()


def attend(queries, kv, query_pos, key_pos):
    batch, tokens, pair = kv.shape
    head_dim = pair // 2
    heads = queries.shape[1] // head_dim
    planes = lax.axis_size("ctx") // 2
    keys = key_pos.shape[1]
    if planes != 4:
        kv_all = gather_ctx(kv, 1)
        split = queries.reshape(batch, tokens, heads, head_dim)
        scores = jnp.einsum(
            "bqhd,bkd->bqhk", split, kv_all[..., :head_dim], preferred_element_type=F32
        )
        allowed = query_pos[:, :, None, None] >= key_pos[:, None, None, :]
        scores = jnp.where(allowed, scores / math.sqrt(head_dim), -1e30)
        logs = jax.nn.logsumexp(scores, axis=-1)
        probs = jnp.exp(scores - logs[..., None]).astype(BF16)
        out = jnp.einsum(
            "bqhk,bkd->bqhd", probs, kv_all[..., head_dim:], preferred_element_type=F32
        ).reshape(queries.shape)
        return out, out.astype(BF16), logs, kv_all
    shape = jax.ShapeDtypeStruct
    dma = pltpu.SemaphoreType.DMA
    rows = batch * tokens
    return pl.pallas_call(
        functools.partial(attend_kernel, planes, heads),
        out_shape=[
            shape(queries.shape, F32),
            shape(queries.shape, BF16),
            shape((rows, head_dim), F32),
            shape((batch, keys, pair), BF16),
        ],
        in_specs=[VMEM] * 4,
        out_specs=[VMEM] * 4,
        scratch_shapes=[dma((planes,)), dma((planes,)), dma((planes,)), dma((planes,))],
        compiler_params=pltpu.CompilerParams(
            collective_id=3, has_side_effects=True, vmem_limit_bytes=48 << 20
        ),
        cost_estimate=pl.CostEstimate(
            flops=rows * keys, bytes_accessed=rows, transcendentals=0
        ),
        name="attend",
    )(queries, kv, query_pos[:, :, None], key_pos[:, None, :])


def attend_backward(queries, kv_all, query_pos, key_pos, grads, out, logs):
    batch, keys, pair = kv_all.shape
    head_dim = pair // 2
    heads = queries.shape[1] // head_dim
    rows = queries.shape[0]
    tokens = rows // batch
    planes = lax.axis_size("ctx") // 2
    if planes != 4:
        factor = 1.0 / math.sqrt(head_dim)
        k_all, v_all = kv_all[..., :head_dim], kv_all[..., head_dim:]
        split = queries.reshape(batch, tokens, heads, head_dim)
        grad_split = grads.reshape(split.shape)
        delta = jnp.sum(grad_split.astype(F32) * out.reshape(split.shape), axis=-1)
        scores = jnp.einsum("bqhd,bkd->bqhk", split, k_all, preferred_element_type=F32)
        allowed = query_pos[:, :, None, None] >= key_pos[:, None, None, :]
        scores = jnp.where(allowed, scores * factor, -1e30)
        probs = jnp.exp(scores - logs[..., None])
        grad_probs = jnp.einsum("bqhd,bkd->bqhk", grad_split, v_all, preferred_element_type=F32)
        grad_scores = (probs * (grad_probs - delta[..., None]) * factor).astype(BF16)
        dq = jnp.einsum("bqhk,bkd->bqhd", grad_scores, k_all, preferred_element_type=F32)
        dk = jnp.einsum("bqhk,bqhd->bkd", grad_scores, split, preferred_element_type=F32)
        dv = jnp.einsum(
            "bqhk,bqhd->bkd", probs.astype(BF16), grad_split, preferred_element_type=F32
        )
        dkv = lax.psum_scatter(
            jnp.concatenate([dk, dv], axis=-1).astype(BF16), "ctx", scatter_dimension=1, tiled=True
        )
        return dq.reshape(queries.shape), dkv.astype(F32)
    shape = jax.ShapeDtypeStruct
    dma = pltpu.SemaphoreType.DMA
    return pl.pallas_call(
        functools.partial(attend_back_kernel, planes, heads),
        out_shape=[shape(queries.shape, F32), shape((batch, tokens, pair), F32)],
        in_specs=[VMEM] * 7,
        out_specs=[VMEM] * 2,
        scratch_shapes=[
            pltpu.VMEM((batch, keys, pair), F32),
            pltpu.VMEM((batch, planes, tokens, pair), BF16),
            pltpu.VMEM((batch, planes, tokens, pair), BF16),
            pltpu.VMEM((batch, planes, tokens, pair), BF16),
            pltpu.VMEM((batch, planes, tokens, pair), BF16),
            dma((batch,)), dma((batch,)), dma((batch, planes)), dma((batch, planes)),
        ],
        compiler_params=pltpu.CompilerParams(
            collective_id=4, has_side_effects=True, vmem_limit_bytes=48 << 20
        ),
        cost_estimate=pl.CostEstimate(
            flops=rows * keys, bytes_accessed=rows, transcendentals=0
        ),
        name="attend_backward",
    )(queries, kv_all, query_pos[:, :, None], key_pos[:, None, :], grads, out, logs)


def layer_forward(x_low, weights, tables):
    gain_attn, w_mixed, bias, w_project, gain_mlp, w_expand, w_reduce = weights
    cosine, sine, query_pos, key_pos, mine = tables
    count, width = x_low.shape
    query_width = w_project.shape[0]
    head_dim = (w_mixed.shape[1] - query_width) // 2
    heads = query_width // head_dim
    batch = query_pos.shape[0]
    tokens = count // batch
    x = x_low.astype(F32)
    root_attn = inverse_root(x)
    normed = (x * root_attn * gain_attn).astype(BF16)
    mixed = dot(normed, w_mixed) + bias
    queries = rotate(
        mixed[:, :query_width].reshape(count, heads, head_dim),
        cosine[:, None, :],
        sine[:, None, :],
    ).astype(BF16).reshape(count, query_width)
    keys = rotate(mixed[:, query_width : query_width + head_dim], cosine, sine)
    kv = jnp.concatenate([keys, mixed[:, query_width + head_dim :]], axis=1).astype(BF16)
    attended_full, attended, log_total, kv = attend(
        queries, kv.reshape(batch, tokens, 2 * head_dim), query_pos, key_pos
    )
    x_mine = lax.dynamic_slice_in_dim(x, mine * tokens, tokens, 0)
    middle = x_mine + tensor_scatter(dot(attended, w_project))
    root_mlp = inverse_root(middle)
    normed_mlp = (middle * root_mlp * gain_mlp).astype(BF16)
    all_normed, branch, gate_slope, up_slope, hidden = feed_forward(
        normed_mlp, w_expand, w_reduce
    )
    result = middle + branch
    kept = (
        x_mine,
        lax.dynamic_slice_in_dim(root_attn, mine * tokens, tokens, 0),
        normed,
        queries,
        kv,
        attended_full,
        log_total,
        attended,
        middle,
        root_mlp,
        all_normed,
        gate_slope,
        up_slope,
        hidden,
    )
    return result.astype(BF16), kept


def layer_backward(grad_out, kept, weights, tables, route, earlier):
    gain_attn, w_mixed, bias, w_project, gain_mlp, w_expand, w_reduce = weights
    cosine, sine, query_pos, key_pos, mine = tables
    (
        x_mine,
        root_attn,
        normed,
        queries,
        kv,
        attended_full,
        log_total,
        attended,
        middle,
        root_mlp,
        all_normed,
        gate_slope,
        up_slope,
        hidden,
    ) = kept
    count, query_width = queries.shape
    head_dim = (w_mixed.shape[1] - query_width) // 2
    heads = query_width // head_dim
    grad_normed_mlp, d_expand, d_reduce = feed_backward(
        grad_out.astype(BF16),
        w_expand,
        w_reduce,
        gate_slope,
        up_slope,
        all_normed,
        hidden,
    )
    moved_reduce = lax.ppermute(d_reduce, "section", route)
    grad_middle, d_gain_mlp = norm_backward(middle, root_mlp, gain_mlp, grad_normed_mlp)
    grad_middle = grad_middle + grad_out
    grad_low, earlier = lax.optimization_barrier((grad_middle.astype(BF16), earlier))
    grad_branch = tensor_gather(grad_low)
    d_project = dot(attended, grad_branch, ROWS)
    grad_attended = dot(grad_branch, w_project, LAST).astype(BF16)
    grad_q, grad_kv = attend_backward(
        queries, kv, query_pos, key_pos, grad_attended, attended_full, log_total
    )
    grad_q, grad_kv, moved_reduce = lax.optimization_barrier((grad_q, grad_kv, moved_reduce))
    grad_kv = grad_kv.reshape(count, 2 * head_dim)
    grad_q = unrotate(
        grad_q.reshape(count, heads, head_dim), cosine[:, None, :], sine[:, None, :]
    )
    grad_k = unrotate(grad_kv[:, :head_dim], cosine, sine)
    grad_mixed = jnp.concatenate(
        [grad_q.reshape(count, heads * head_dim), grad_k, grad_kv[:, head_dim:]], axis=1
    ).astype(BF16)
    d_mixed = dot(normed, grad_mixed, ROWS)
    d_bias = jnp.sum(grad_mixed.astype(F32), axis=0)
    grad_normed = tensor_scatter(dot(grad_mixed, w_mixed, LAST))
    grad_x, d_gain_attn = norm_backward(x_mine, root_attn, gain_attn, grad_normed)
    grad_x = (grad_x + grad_middle).astype(BF16)
    vectors = (d_gain_attn, d_mixed, d_bias, d_project, d_gain_mlp)
    return grad_x, vectors, d_expand, (d_reduce, moved_reduce), earlier


def shards(
    block_input, positions, cotangent, norm_attn, w_qkv, b_qkv, w_out, norm_mlp, w_gate_up, w_down
):
    section = lax.axis_index("section")
    tensor = lax.axis_index("tensor")
    ctx = lax.axis_index("ctx")
    ctx_size = lax.axis_size("ctx")
    first = section == 0
    micro, tokens, width = block_input.shape
    half = micro // 2
    head_dim = w_qkv.shape[3] - w_out.shape[2] * ctx_size
    head_dim = head_dim // 2
    slice_width = norm_attn.shape[1]
    slice_bias = b_qkv.shape[2]
    units = w_down.shape[1]

    def plane_part(value):
        return lax.dynamic_slice_in_dim(value, section * half, half, 0)

    def layers(own, other):
        return jnp.where(first, own, other), jnp.where(first, other, own)

    x = plane_part(block_input).reshape(half * tokens, width)
    pos_local = plane_part(positions)
    cosine, sine = angles(pos_local.reshape(-1), head_dim)

    small = jnp.concatenate([norm_attn[0], norm_mlp[0], b_qkv[0, 0]])
    qkv, out = w_qkv[0, :, 0, :], w_out[0, 0]
    vectors = jnp.concatenate(layers(small, swap(small)))
    places = jnp.concatenate([pos_local // 64, pos_local % 64]).reshape(-1).astype(BF16)
    packed = gather_ctx(jnp.concatenate([vectors, places])[None], 0)
    places = packed[:, vectors.shape[0] :].astype(jnp.int32).reshape(ctx_size, 2, half, tokens)
    pos_all = jnp.swapaxes(places[:, 0] * 64 + places[:, 1], 0, 1).reshape(half, -1)
    tables = (cosine, sine, pos_local, pos_all, tensor)
    small_size = 2 * slice_width + slice_bias
    small0, small1 = packed[:, :small_size], packed[:, small_size : 2 * small_size]
    qkv0, qkv1 = layers(qkv, swap(qkv))
    out0, out1 = layers(out, swap(out))
    down0, down1 = layers(w_down[0], swap(w_down[0]))
    expand = w_gate_up[0].reshape(slice_width, 2, ctx_size, units)
    expand = share(jnp.transpose(expand, (1, 2, 0, 3))).reshape(2, 2, width, units)
    x, expand = lax.optimization_barrier((x, expand))
    expand0, expand1 = (expand, 0), (expand, 1)

    def whole(small, qkv, out, expand, down):
        return (
            small[:, :slice_width].reshape(1, width),
            gather_ctx(qkv, 0),
            small[:, 2 * slice_width :].reshape(1, slice_bias * ctx_size),
            gather_ctx(out, 0),
            small[:, slice_width : 2 * slice_width].reshape(1, width),
            expand,
            down,
        )

    weights0 = whole(small0, qkv0, out0, expand0, down0)
    weights1 = whole(small1, qkv1, out1, expand1, down1)

    result0, kept0 = layer_forward(x, weights0, tables)
    x1 = tensor_gather(result0)
    result1, kept1 = layer_forward(x1, weights1, tables)
    out1_all = tensor_gather(result1)

    def exchange(layer0, layer1):
        kept_here = jnp.where(first, layer0, layer1)
        received = swap(jnp.where(first, layer1, layer0))
        low = jnp.where(first, kept_here, received)
        high = jnp.where(first, received, kept_here)
        both = jnp.concatenate([low, high], axis=0)
        return both.reshape(1, micro, tokens, width)

    section_output = exchange(x1, out1_all)

    seed = lax.dynamic_slice_in_dim(cotangent, section * half + tensor, 1, 0)[0].astype(F32)
    def ctx_scatter(value):
        return lax.psum_scatter(
            value.astype(BF16), "ctx", scatter_dimension=0, tiled=True
        )

    group = w_qkv.shape[3]
    split_at = group - head_dim

    def with_vectors(grads):
        gain_attn, mixed, bias, project, gain_mlp = grads[:5]
        rows = jnp.concatenate(
            [
                bias[:split_at].reshape(ctx_size, -1),
                bias[split_at:].reshape(ctx_size, -1),
                gain_attn.reshape(ctx_size, slice_width),
                gain_mlp.reshape(ctx_size, slice_width),
            ],
            axis=1,
        )
        rows = jnp.pad(rows[:, None, :], ((0, 0), (0, 15), (0, group - rows.shape[1])))
        mixed = mixed.reshape(ctx_size, slice_width, group)
        both = jnp.concatenate([mixed.astype(BF16), rows.astype(BF16)], axis=1)
        return both.reshape(ctx_size * (slice_width + 16), group)

    grad1, d1, d_expand1, d_reduce1, _ = layer_backward(
        seed, kept1, weights1, tables, [(0, 1)], ()
    )
    slices1 = (ctx_scatter(with_vectors(d1)), ctx_scatter(d1[3]))
    grad1_all = tensor_gather(grad1)
    grad1, grad1_all = lax.optimization_barrier((grad1, grad1_all))
    grad0, d0, d_expand0, d_reduce0, earlier = layer_backward(
        grad1.astype(F32), kept0, weights0, tables, [(1, 0)], slices1 + (section_output,)
    )
    slices1, section_output = earlier[:2], earlier[2]

    def to_owner(part0, part1):
        received0 = lax.ppermute(part0.astype(BF16), "section", [(1, 0)])
        received1 = lax.ppermute(part1.astype(BF16), "section", [(0, 1)])
        own = jnp.where(first, part0, part1).astype(F32)
        return own + jnp.where(first, received0, received1).astype(F32)

    def of_owner(pair0, pair1):
        own, received = (jnp.where(first, low, high).astype(F32) for low, high in zip(pair0, pair1))
        return own + received

    blocks = (2, ctx_size, slice_width, units)
    grad0_all = tensor_gather(grad0)
    grad0_all, d_expand0 = lax.optimization_barrier((grad0_all, d_expand0))
    input_grad = exchange(grad0_all, grad1_all)
    total = collect(d_expand0.reshape(blocks), d_expand1.reshape(blocks), first)
    d_expand = jnp.transpose(total, (2, 0, 1, 3)).reshape(1, slice_width, 2, ctx_size * units)
    d_expand = d_expand.astype(F32)
    d_reduce = of_owner(d_reduce0, d_reduce1)

    d_mixed = to_owner(ctx_scatter(with_vectors(d0)), slices1[0])
    d_project = to_owner(ctx_scatter(d0[3]), slices1[1])
    vectors = d_mixed[slice_width]
    d_mixed = d_mixed[:slice_width]
    count_qk, count_v = split_at // ctx_size, head_dim // ctx_size
    bias_qk = vectors[:count_qk][None]
    bias_v = vectors[count_qk : count_qk + count_v][None]
    start = count_qk + count_v
    gains = vectors[start : start + 2 * slice_width].reshape(1, 2 * slice_width)
    gains = gains + lax.ppermute(gains, "tensor", SWAP)
    return (
        section_output,
        input_grad,
        gains[:, :slice_width],
        d_mixed[None, :, None, :],
        bias_qk[None],
        bias_v[None],
        d_project[None, None],
        gains[:, slice_width:],
        d_expand,
        d_reduce[None],
    )


def solution(mesh):
    in_specs = (
        P(None, "ctx", None),
        P(None, "ctx"),
        P(None, "ctx", None),
        P("section", "ctx"),
        P("section", "ctx", "tensor", None),
        P("section", "tensor", "ctx"),
        P("section", "tensor", "ctx", None),
        P("section", "ctx"),
        P("section", "ctx", None, "tensor"),
        P("section", ("tensor", "ctx"), None),
    )
    out_specs = (
        P("section", None, "ctx", None),
        P("section", None, "ctx", None),
        P("section", "ctx"),
        P("section", "ctx", "tensor", None),
        P("section", "tensor", "ctx"),
        P("section", "tensor", "ctx"),
        P("section", "tensor", "ctx", None),
        P("section", "ctx"),
        P("section", "ctx", None, "tensor"),
        P("section", ("tensor", "ctx"), None),
    )
    return jax.shard_map(shards, mesh=mesh, in_specs=in_specs, out_specs=out_specs, check_vma=False)
```

time: 1690 us -> 1120 us (0.66)
  waiting for transfers between devices: 936 us -> 59.7 us
  Pallas kernels: 0 us -> 738 us
  blocking collectives: 301 us -> 101 us
  matrix products: 202 us -> 30.4 us
  other arithmetic: 90 us -> 63.5 us
  local copies, waits for them, and re-layouts: 99.4 us -> 81.1 us
    pallas_call x0 -> x10, Pallas kernels: none -> 738 us  [the longest x4 394 us: spread(): pl.pallas_call(functools.partial(spread_kernel, chunk, piece, layer, plan...]
    reduce_scatter x8 -> x0, waiting for transfers between devices: 368 us -> none  [the longest x4 325 us: scatter_tokens(): lax.psum_scatter(rows, ('tensor', 'ctx'), scatter_dimension=0, tiled=True)]
    ppermute x11 -> x6, waiting for transfers between devices: 226 us -> 29.5 us  [swap(): return lax.ppermute(value, 'section', SWAP)]
    all_gather x4 -> x0, waiting for transfers between devices: 178 us -> none  [gather_tokens(): return lax.all_gather(rows, ('tensor', 'ctx'), axis=0, tiled=True)]
    dot_general x30 -> x12, matrix products: 170 us -> 30.4 us  [dot(): return lax.dot_general(a, b, dims, preferred_element_type=F32)]
    all_to_all x1 -> x0, blocking collectives: 119 us -> none  [shards(): lax.all_to_all(expand, 'ctx', split_axis=0, concat_axis=0, tiled=True)]
    all_gather x6 -> x4, waiting for transfers between devices: 102 us -> 0.04 us  [gather_ctx(): return lax.all_gather(value, 'ctx', axis=axis, tiled=True)]
    psum x2 -> x0, blocking collectives: 81.2 us -> none  [the longest x1 53.3 us: shards(): gains = lax.psum(gains, ('section', 'tensor', 'ctx'))]
  transfers between devices with their start and end apart: 36 -> 25, of which waited for: 26 -> 10; matrix products, arithmetic and copies ran while one was open for 14% -> 13% of each run, Pallas kernels for 0% -> 49%
where the time goes in v2:
time: 1120 us; the launch traced here: 1110 us
  Pallas kernels  738 us (66%)
  blocking collectives  101 us (9%)
  local copies, waits for them, and re-layouts  81.1 us (7%)
  other arithmetic  63.5 us (6%)
  waiting for transfers between devices  59.7 us (5%)
  matrix products  30.4 us (3%)
  starting transfers between devices  23.8 us (2%)
  between operations  16 us (1%)
    pallas_call x4, Pallas kernels, spread(): pl.pallas_call(functools.partial(spread_kernel, chunk, piece, layer, plan...  394 us
    pallas_call x1, Pallas kernels, share(): pl.pallas_call(functools.partial(share_kernel, size), out_shape=jax.Shape...  118 us
    pallas_call x1, Pallas kernels, collect(): pl.pallas_call(functools.partial(collect_kernel, size), out_shape=jax.Sha...  109 us
    pallas_call x2, Pallas kernels, attend_backward(): pl.pallas_call(functools.partial(attend_back_kernel, planes, heads), out_...  61.8 us
    all_gather x6, blocking collectives, tensor_gather(): return lax.all_gather(rows, 'tensor', axis=0, tiled=True)  56.5 us
    pallas_call x2, Pallas kernels, attend(): pl.pallas_call(functools.partial(attend_kernel, planes, heads), out_shape...  55.6 us
    all_gather x1, blocking collectives, gather_ctx(): return lax.all_gather(value, 'ctx', axis=axis, tiled=True)  44.2 us
    unnamed x159, local copies, waits for them, and re-layouts  39 us
  transfers between devices with their start and end apart: 25, of which 10 were waited for; matrix products, arithmetic and copies ran while one was open for 13% of the time, Pallas kernels for 49%

profile of v2, /device:TPU:9, one launch (start us, length us, event | category | flops | bytes accessed | tf_op | source)
XLA Modules:
  0.0 1113.2 jit_solution(6766646814813028062)
XLA Ops:
  8.5 9.0 collective-permute-done.1
  20.8 6.0 collective-permute-done.2
  31.1 10.9 reshape.412
  42.0 5.0 copy.78
  47.0 117.9 %share.1 = bf16[2,2,8,192,560]{4,3,2,1,0:T(8,128)(2,1)} custom-call(bf16[2,8,192,560]{3,2,1,0:T(8,128)(2,1)} %bitcast.122), custom_call_target="tpu_custom_call" | custom-call | flops 1720320 | bytes 1024 | tf_op jit(solution)/shard_map/share/pallas_call | solution.py:155
  166.3 44.2 %all-gather.1 = bf16[8,1,1536]{2,1,0:T(2,128)(2,1)S(1)} all-gather(bf16[1,1,1536]{2,1,0:T(2,128)(2,1)S(1)} %reshape.409), channel_id=2, replica_groups=mesh['section'=2,'tensor'=2,'ctx'=8] {'ctx'}, dimensions={0}, use_global_device_ids=true | all-gather | bytes 27648 | tf_op jit(solution)/shard_map/all_gather | solution.py:66
  227.6 31.2 %attend.2 = (f32[256,768]{1,0:T(8,128)S(1)}, bf16[256,768]{1,0:T(8,128)(2,1)S(1)}, f32[256,128]{1,0:T(8,128)S(1)}, bf16[2,1024,256]{2,1,0:T(8,128)(2,1)S(1)}) custom-call(bf16[256,768]{1,0:T(8,128)(2,1)S(1)} %add_convert_fusion.7.q_ref, bf16[2,128,256]{2,1,0:T(8,128)(2,1)S(1)} %pad_maximum_fusion.7.kv_ref, s32[2,128,1]{2,1,0:T(8,128)S(1)} %copy.51.qpos_ref, ...), custom_call_target="tpu_custom_call" | custom-call | flops 262144 | bytes 256 | tf_op jit(solution)/shard_map/attend/pallas_call | solution.py:787
  269.0 5.5 collective-permute-done.3
  276.6 93.4 %mlp_forward.2 = (bf16[2048,1536]{1,0:T(8,128)(2,1)}, f32[128,1536]{1,0:T(8,128)}, bf16[2048,560]{1,0:T(8,128)(2,1)}, bf16[2048,560]{1,0:T(8,128)(2,1)}, bf16[2048,560]{1,0:T(8,128)(2,1)}) custom-call(bf16[128,1536]{1,0:T(8,128)(2,1)} %multiply_convert_fusion.3.own_ref, bf16[2,2,1536,560]{3,2,1,0:T(8,128)(2,1)} %bitcast.118, ...), custom_call_target="tpu_custom_call" | custom-call | flops 3145728 | bytes 2048 | tf_op jit(solution)/shard_map/mlp_forward/pallas_call | solution.py:470
  371.5 10.3 all_gather.36
  395.8 24.3 %attend.3 = (f32[256,768]{1,0:T(8,128)S(1)}, bf16[256,768]{1,0:T(8,128)(2,1)S(1)}, f32[256,128]{1,0:T(8,128)S(1)}, bf16[2,1024,256]{2,1,0:T(8,128)(2,1)S(1)}) custom-call(bf16[256,768]{1,0:T(8,128)(2,1)S(1)} %add_convert_fusion.5.q_ref, bf16[2,128,256]{2,1,0:T(8,128)(2,1)S(1)} %pad_maximum_fusion.8.kv_ref, s32[2,128,1]{2,1,0:T(8,128)S(1)} %copy.51.qpos_ref, ...), custom_call_target="tpu_custom_call" | custom-call | flops 262144 | bytes 256 | tf_op jit(solution)/shard_map/attend/pallas_call | solution.py:787
  429.0 7.7 collective-permute-done.5
  438.7 94.6 %mlp_forward.3 = (bf16[2048,1536]{1,0:T(8,128)(2,1)}, f32[128,1536]{1,0:T(8,128)}, bf16[2048,560]{1,0:T(8,128)(2,1)}, bf16[2048,560]{1,0:T(8,128)(2,1)}, bf16[2048,560]{1,0:T(8,128)(2,1)}) custom-call(bf16[128,1536]{1,0:T(8,128)(2,1)} %multiply_convert_fusion.2.own_ref, bf16[2,2,1536,560]{3,2,1,0:T(8,128)(2,1)} %bitcast.119, ...), custom_call_target="tpu_custom_call" | custom-call | flops 3145728 | bytes 2048 | tf_op jit(solution)/shard_map/mlp_forward/pallas_call | solution.py:470
  533.3 100.8 %mlp_backward.2 = (bf16[16,1536]{1,0:T(8,128)(2,1)}, f32[128,1536]{1,0:T(8,128)}, bf16[2,1536,560]{2,1,0:T(8,128)(2,1)}, bf16[560,1536]{1,0:T(8,128)(2,1)}) custom-call(bf16[128,1536]{1,0:T(8,128)(2,1)} %dynamic-slice_bitcast_fusion.own_ref, bf16[2,2,1536,560]{3,2,1,0:T(8,128)(2,1)} %bitcast.120, bf16[560,1536]{1,0:T(8,128)(2,1)} %get-tuple-element.130.refs_1_, ...), custom_call_target="tpu_custom_call" | custom-call | flops 3145728 | bytes 2048 | tf_op jit(solution)/shard_map/mlp_backward/pallas_call | solution.py:470
  638.6 11.7 %all_gather.39 = bf16[256,1536]{1,0:T(8,128)(2,1)S(1)} all-gather(bf16[128,1536]{1,0:T(8,128)(2,1)S(1)} %get-tuple-element.143), channel_id=1, replica_groups=mesh['section'=2,'tensor'=2,'ctx'=8] {'tensor'}, dimensions={0}, use_global_device_ids=true | all-gather | bytes 1179648 | tf_op jit(solution)/shard_map/all_gather | solution.py:78
  659.3 31.0 %attend_backward.2 = (f32[256,768]{1,0:T(8,128)S(1)}, f32[2,128,256]{2,1,0:T(8,128)S(1)}) custom-call(bf16[256,768]{1,0:T(8,128)(2,1)S(1)} %add_convert_fusion.5.q_ref, bf16[2,1024,256]{2,1,0:T(8,128)(2,1)S(1)} %copy-done.7, s32[2,128,1]{2,1,0:T(8,128)S(1)} %copy.51.qpos_ref, s32[2,1,1024]{2,1,0:T(1,128)S(1)} %bitcast.116, ...), custom_call_target="tpu_custom_call" | custom-call | flops 262144 | bytes 256 | tf_op jit(solution)/shard_map/attend_backward/pallas_call | solution.py:838
  707.7 4.1 fusion.2
  712.8 8.1 all_gather.41
  721.5 14.5 %collective-permute-done.8 = bf16[256,1536]{1,0:T(8,128)(2,1)S(1)} collective-permute-done((bf16[256,1536]{1,0:T(8,128)(2,1)S(1)}, bf16[256,1536]{1,0:T(8,128)(2,1)S(1)}, u32[]{:S(2)}, u32[]{:S(2)}) %collective-permute-start.8) | collective-permute-done | bytes 786464 | tf_op jit(solution)/shard_map/ppermute | solution.py:62
  740.5 7.7 all_gather.40
  748.1 105.0 %mlp_backward.3 = (bf16[16,1536]{1,0:T(8,128)(2,1)}, f32[128,1536]{1,0:T(8,128)}, bf16[2,1536,560]{2,1,0:T(8,128)(2,1)}, bf16[560,1536]{1,0:T(8,128)(2,1)}) custom-call(bf16[128,1536]{1,0:T(8,128)(2,1)} %copy-done.29, bf16[2,2,1536,560]{3,2,1,0:T(8,128)(2,1)} %bitcast.121, bf16[560,1536]{1,0:T(8,128)(2,1)} %get-tuple-element.131.refs_1_, ...), custom_call_target="tpu_custom_call" | custom-call | flops 3145728 | bytes 2048 | tf_op jit(solution)/shard_map/mlp_backward/pallas_call | solution.py:470
  858.5 10.8 all_gather.42
  876.2 30.8 %attend_backward.3 = (f32[256,768]{1,0:T(8,128)S(1)}, f32[2,128,256]{2,1,0:T(8,128)S(1)}) custom-call(bf16[256,768]{1,0:T(8,128)(2,1)S(1)} %add_convert_fusion.7.q_ref, bf16[2,1024,256]{2,1,0:T(8,128)(2,1)S(1)} %copy-done.5, s32[2,128,1]{2,1,0:T(8,128)S(1)} %copy.51.qpos_ref, s32[2,1,1024]{2,1,0:T(1,128)S(1)} %bitcast.117, ...), custom_call_target="tpu_custom_call" | custom-call | flops 262144 | bytes 256 | tf_op jit(solution)/shard_map/attend_backward/pallas_call | solution.py:838
  925.3 4.1 fusion.3
  930.4 5.0 collective-permute-start.16
  939.4 8.0 all_gather.43
  947.6 4.2 add_bitcast_fusion
  952.5 109.0 %collect.1 = bf16[2,8,192,560]{3,2,1,0:T(8,128)(2,1)S(1)} custom-call(bf16[2,8,192,560]{3,2,1,0:T(8,128)(2,1)S(1)} %bitcast.107, bf16[2,8,192,560]{3,2,1,0:T(8,128)(2,1)S(1)} %bitcast.106), custom_call_target="tpu_custom_call" | custom-call | flops 1720320 | bytes 1024 | tf_op jit(solution)/shard_map/collect/pallas_call | solution.py:232
  1062.3 7.7 copy.71
  1070.0 12.4 %reshape.413 = f32[1,192,2,4480]{3,2,1,0:T(2,128)} reshape(f32[192,2,8,560]{3,2,1,0:T(8,128)} %copy.71) | data formatting | bytes 13762560
  1086.4 7.3 collective-permute-done.15
  1095.8 5.1 collective-permute-done.12
  (347 shorter events, 150.0 us)
Async XLA Ops:
  7.2 157.7 %copy-start = (bf16[4,128,1536]{2,1,0:T(8,128)(2,1)S(1)}, bf16[4,128,1536]{2,1,0:T(8,128)(2,1)}, u32[]{:S(2)}) copy-start(bf16[4,128,1536]{2,1,0:T(8,128)(2,1)} %param.10) | copy-start | bytes 4718596
  7.2 204.1 %all-gather.7.cloned.1.call-start = ((), (), s32[]{:S(2)}) async-start(), calls=%async_computation.4 | async-start | bytes 3538944 | tf_op jit(solution)/shard_map/all_gather | solution.py:66
  7.3 10.3 collective-permute-start.1
  19.5 241.8 %all-gather.9.cloned.1.call-start = ((), (), s32[]{:S(2)}) async-start(), calls=%async_computation.5 | async-start | bytes 2654208 | tf_op jit(solution)/shard_map/all_gather | solution.py:66
  19.5 7.2 collective-permute-start.2
  28.7 353.4 %all-gather.11.cloned.1.call-start = ((), (), s32[]{:S(2)}) async-start(), calls=%async_computation.6 | async-start | bytes 3538944 | tf_op jit(solution)/shard_map/all_gather | solution.py:66
  29.4 392.6 %all-gather.13.cloned.1.call-start = ((), (), s32[]{:S(2)}) async-start(), calls=%async_computation.7 | async-start | bytes 2654208 | tf_op jit(solution)/shard_map/all_gather | solution.py:66
  29.6 136.5 %collective-permute-start = (bf16[512]{0:T(512)(128)(2,1)S(1)}, bf16[512]{0:T(512)(128)(2,1)S(1)}, u32[]{:S(2)}, u32[]{:S(2)}) collective-permute-start(bf16[512]{0:T(512)(128)(2,1)S(1)} %pad_maximum_fusion.10), channel_id=1, source_target_pairs={{0,16},{16,0},{1,17},{17,1},{2,18},{18,2},{3,19},{19,3},{4,20},{20... | collective-permute-start | bytes 3080 | tf_op jit(solution)/shard_map/ppermute | solution.py:62
  30.8 234.2 %collective-permute-start.4 = (bf16[560,1536]{1,0:T(8,128)(2,1)}, bf16[560,1536]{1,0:T(8,128)(2,1)}, u32[]{:S(2)}, u32[]{:S(2)}) collective-permute-start(bf16[560,1536]{1,0:T(8,128)(2,1)} %bitcast.20), channel_id=1, source_target_pairs={{0,16},{16,0},{1,17},{17,1},{2,18},{18,2},{3,19},{19,3},{4,20},{20... | collective-permute-start | bytes 5160968 | tf_op jit(solution)/shard_map/ppermute | solution.py:62
  47.0 118.0 %copy-start.73 = (s32[4,128]{1,0:T(4,128)S(1)}, s32[4,128]{1,0:T(4,128)}, u32[]{:S(2)}) copy-start(s32[4,128]{1,0:T(4,128)} %param.11) | copy-start | bytes 6148
  165.2 49.3 %copy-start.71 = (f32[256]{0:T(256)}, f32[256]{0:T(256)S(1)}, u32[]{:S(2)}) copy-start(f32[256]{0:T(256)S(1)} %add_rsqrt_fusion.1) | copy-start | bytes 3076
  165.3 227.4 %copy-start.36 = (f32[256,64]{1,0:T(8,128)}, f32[256,64]{1,0:T(8,128)S(1)}, u32[]{:S(2)}) copy-start(f32[256,64]{1,0:T(8,128)S(1)} %broadcast_multiply_fusion.2) | copy-start | bytes 196612
  166.0 108.6 %copy-start.24 = (f32[256,1536]{1,0:T(8,128)}, f32[256,1536]{1,0:T(8,128)S(1)}, u32[]{:S(2)}) copy-start(f32[256,1536]{1,0:T(8,128)S(1)} %convert_element_type.237) | copy-start | bytes 4718596
  210.8 647.7 %reduce-scatter.7.cloned.1.call-start = ((), (), s32[]{:S(2)}) async-start(), calls=%async_computation.9 | async-start | bytes 2654208 | tf_op jit(solution)/shard_map/reduce_scatter | solution.py:1045
  219.0 169.4 %copy-start.43 = (f32[256,128]{0,1:T(8,128)}, f32[256,128]{0,1:T(8,128)S(1)}, u32[]{:S(2)}) copy-start(f32[256,128]{0,1:T(8,128)S(1)} %copy.49) | copy-start | bytes 393220
  263.8 10.8 collective-permute-start.3
  274.8 581.9 %copy-start.62 = (f32[128]{0:T(128)}, f32[128]{0:T(128)S(1)}, u32[]{:S(2)}) copy-start(f32[128]{0:T(128)S(1)} %add_rsqrt_fusion.3) | copy-start | bytes 1540
  426.3 10.3 collective-permute-start.5
  650.3 40.1 %collective-permute-start.6 = (bf16[560,1536]{1,0:T(8,128)(2,1)}, bf16[560,1536]{1,0:T(8,128)(2,1)}, u32[]{:S(2)}, u32[]{:S(2)}) collective-permute-start(bf16[560,1536]{1,0:T(8,128)(2,1)} %get-tuple-element.69), channel_id=1, source_target_pairs={{0,16},{1,17},{2,18},{3,19},{4,20},{5,21},{6,22},{7,23},{8,24},{9,... | collective-permute-start | bytes 5160968 | tf_op jit(solution)/shard_map/ppermute | solution.py:942
  656.6 202.0 %reduce-scatter.5.cloned.1.call-start = ((), (), s32[]{:S(2)}) async-start(), calls=%async_computation.8 | async-start | bytes 3833856 | tf_op jit(solution)/shard_map/reduce_scatter | solution.py:1045
  698.8 8.4 collective-permute-start.7
  711.8 370.6 %reduce-scatter.11.cloned.1.call-start = ((), (), s32[]{:S(2)}) async-start(), calls=%async_computation.11 | async-start | bytes 2654208 | tf_op jit(solution)/shard_map/reduce_scatter | solution.py:1045
  720.9 15.1 %collective-permute-start.8 = (bf16[256,1536]{1,0:T(8,128)(2,1)S(1)}, bf16[256,1536]{1,0:T(8,128)(2,1)S(1)}, u32[]{:S(2)}, u32[]{:S(2)}) collective-permute-start(bf16[256,1536]{1,0:T(8,128)(2,1)S(1)} %broadcast_select_fusion.8), channel_id=1, source_target_pairs={{0,16},{16,0},{1,17},{17,1},{2,18},{18,2},{3,19},{19,3},{4,20},{20... | collective-permute-start | bytes 2359304 | tf_op jit(solution)/shard_map/ppermute | solution.py:62
  853.2 53.8 %collective-permute-start.9 = (bf16[560,1536]{1,0:T(8,128)(2,1)}, bf16[560,1536]{1,0:T(8,128)(2,1)}, u32[]{:S(2)}, u32[]{:S(2)}) collective-permute-start(bf16[560,1536]{1,0:T(8,128)(2,1)} %get-tuple-element.86), channel_id=1, source_target_pairs={{16,0},{17,1},{18,2},{19,3},{20,4},{21,5},{22,6},{23,7},{24,8},{25... | collective-permute-start | bytes 5160968 | tf_op jit(solution)/shard_map/ppermute | solution.py:942
  872.5 212.6 %reduce-scatter.9.cloned.1.call-start = ((), (), s32[]{:S(2)}) async-start(), calls=%async_computation.10 | async-start | bytes 3833856 | tf_op jit(solution)/shard_map/reduce_scatter | solution.py:1045
  915.5 8.6 collective-permute-start.10
  930.4 156.1 %collective-permute-start.16 = (bf16[96,1536]{1,0:T(8,128)(2,1)S(1)}, bf16[96,1536]{1,0:T(8,128)(2,1)}, u32[]{:S(2)}, u32[]{:S(2)}) collective-permute-start(bf16[96,1536]{1,0:T(8,128)(2,1)S(1)} %copy-done.57), channel_id=1, source_target_pairs={{0,16},{1,17},{2,18},{3,19},{4,20},{5,21},{6,22},{7,23},{8,24},{9,... | collective-permute-start | bytes 884744 | tf_op jit(solution)/shard_map/ppermute | solution.py:1081
  935.4 160.4 %collective-permute-start.13 = (bf16[208,1024]{1,0:T(8,128)(2,1)}, bf16[208,1024]{1,0:T(8,128)(2,1)}, u32[]{:S(2)}, u32[]{:S(2)}) collective-permute-start(bf16[208,1024]{1,0:T(8,128)(2,1)} %reduce-scatter.5.cloned.1.call-done), channel_id=1, source_target_pairs={{0,16},{1,17},{2,18},{3,19},{4,20},{5,21},{6,22},{7,23},{8,24},{9,... | collective-permute-start | bytes 1277960 | tf_op jit(solution)/shard_map/ppermute | solution.py:1081
  947.5 136.2 %collective-permute-start.11 = (bf16[256,1536]{1,0:T(8,128)(2,1)S(1)}, bf16[256,1536]{1,0:T(8,128)(2,1)S(1)}, u32[]{:S(2)}, u32[]{:S(2)}) collective-permute-start(bf16[256,1536]{1,0:T(8,128)(2,1)S(1)} %broadcast_select_fusion.4), channel_id=1, source_target_pairs={{0,16},{16,0},{1,17},{17,1},{2,18},{18,2},{3,19},{19,3},{4,20},{20... | collective-permute-start | bytes 2359304 | tf_op jit(solution)/shard_map/ppermute | solution.py:62
  1082.4 11.3 %collective-permute-start.15 = (bf16[96,1536]{1,0:T(8,128)(2,1)}, bf16[96,1536]{1,0:T(8,128)(2,1)}, u32[]{:S(2)}, u32[]{:S(2)}) collective-permute-start(bf16[96,1536]{1,0:T(8,128)(2,1)} %reduce-scatter.11.cloned.1.call-done), channel_id=1, source_target_pairs={{16,0},{17,1},{18,2},{19,3},{20,4},{21,5},{22,6},{23,7},{24,8},{25... | collective-permute-start | bytes 884744 | tf_op jit(solution)/shard_map/ppermute | solution.py:1080
  1085.1 15.7 %collective-permute-start.12 = (bf16[208,1024]{1,0:T(8,128)(2,1)}, bf16[208,1024]{1,0:T(8,128)(2,1)S(1)}, u32[]{:S(2)}, u32[]{:S(2)}) collective-permute-start(bf16[208,1024]{1,0:T(8,128)(2,1)} %reduce-scatter.9.cloned.1.call-done), channel_id=1, source_target_pairs={{16,0},{17,1},{18,2},{19,3},{20,4},{21,5},{22,6},{23,7},{24,8},{25... | collective-permute-start | bytes 1277960 | tf_op jit(solution)/shard_map/ppermute | solution.py:1080
  1102.8 2.4 collective-permute-start.14
  (69 other events, 467.1 us)
Sparse Core Ops, SparseCore 0:
  19.6 43.0 all-gather.6
  64.3 56.9 all-gather.8
  123.6 59.5 all-gather.10
  210.9 39.4 all-gather.12
  656.7 46.8 reduce-scatter.6
  711.9 45.4 reduce-scatter.4
  872.6 48.3 reduce-scatter.10
  929.6 44.9 reduce-scatter.8

commit v3 on v2

--- a/solution.py
+++ b/solution.py
@@ -78,6 +78,12 @@
     return lax.all_gather(rows, "tensor", axis=0, tiled=True)
 
 
+def tensor_pair(rows):
+    received = lax.ppermute(rows, "tensor", SWAP)
+    mine = lax.axis_index("tensor") == 0
+    return jnp.concatenate([jnp.where(mine, rows, received), jnp.where(mine, received, rows)])
+
+
 def tensor_scatter(rows):
     mine = lax.axis_index("tensor")
     tokens = rows.shape[0] // 2
@@ -101,10 +107,10 @@
     return sorted(range(size), key=lambda step: min(step, size - step))
 
 
-def share_kernel(size, from_ref, all_ref, send, recv, over_send, over_recv, local):
+def share_job(size, from_ref, all_ref, send, recv, over_send, over_recv, local):
     me = lax.axis_index("ctx")
     section = lax.axis_index("section")
-    greet_all(size, me)
+    order = by_distance(size)[1:]
 
     def copy(there, source):
         return remote(
@@ -124,44 +130,36 @@
             {"section": 1 - section},
         )
 
-    own = pltpu.make_async_copy(from_ref.at[:, me], all_ref.at[section, :, me], local)
-    own.start()
-    over(from_ref.at[:, me], me).start()
-    order = by_distance(size)[1:]
-
-    def pass_on(step):
+    def own():
+        return pltpu.make_async_copy(from_ref.at[:, me], all_ref.at[section, :, me], local)
+
+    def start():
+        own().start()
+        over(from_ref.at[:, me], me).start()
+        for step in order[:2]:
+            copy((me + step) % size, me).start()
+
+    def stage(index):
+        step = order[index]
         source = (me + size - step) % size
         copy(source, source).wait_recv()
         over(all_ref.at[section, :, source], source).start()
         copy((me + step) % size, me).wait_send()
-
-    for index, step in enumerate(order):
-        copy((me + step) % size, me).start()
-        if index > 0:
-            pass_on(order[index - 1])
-    pass_on(order[-1])
-    own.wait()
-    for step in range(size):
-        source = (me + step) % size
-        over(all_ref.at[section, :, source], source).wait()
+        if index + 2 < len(order):
+            copy((me + order[index + 2]) % size, me).start()
+
+    def finish():
+        own().wait()
+        for step in range(size):
+            source = (me + step) % size
+            over(all_ref.at[section, :, source], source).wait()
+
+    return start, stage, finish
 
 
 def share(blocks):
-    size = blocks.shape[1]
-    if size != 8:
-        moved = lax.all_to_all(blocks, "ctx", split_axis=1, concat_axis=1, tiled=True)
-        return lax.all_gather(moved, "section")
-    dma = pltpu.SemaphoreType.DMA
-    return pl.pallas_call(
-        functools.partial(share_kernel, size),
-        out_shape=jax.ShapeDtypeStruct((2,) + blocks.shape, blocks.dtype),
-        in_specs=[HBM],
-        out_specs=HBM,
-        scratch_shapes=[dma((size,)), dma((size,)), dma((size,)), dma((size,)), dma],
-        compiler_params=pltpu.CompilerParams(collective_id=5, has_side_effects=True),
-        cost_estimate=pl.CostEstimate(flops=blocks.size, bytes_accessed=1024, transcendentals=0),
-        name="share",
-    )(blocks)
+    moved = lax.all_to_all(blocks, "ctx", split_axis=1, concat_axis=1, tiled=True)
+    return lax.all_gather(moved, "section")
 
 
 def collect_kernel(
@@ -250,7 +248,7 @@
     )
 
 
-def spread_kernel(chunk, piece, layer, planes, ins, outs, extra, own_ref, *refs):
+def spread_kernel(chunk, piece, layer, planes, gathered, ins, outs, extra, own_ref, *refs):
     in_refs, refs = refs[:ins], refs[ins:]
     all_ref, sum_ref = refs[:2]
     out_refs, refs = refs[2 : 2 + outs], refs[2 + outs :]
@@ -264,7 +262,7 @@
     tensor = lax.axis_index("tensor")
     ctx = lax.axis_index("ctx")
     plane, core = ctx // 2, ctx % 2
-    rows = own_ref.shape[0]
+    rows = own_ref.shape[0] // (4 * planes if gathered else 1)
     y_peer = {"tensor": 1 - tensor}
     core_peer = {"ctx": plane * 2 + 1 - core}
 
@@ -292,19 +290,20 @@
         ref = block(at, which_core, which_tensor)
         return remote(ref, ref, cs.at[at, slot], cr.at[at, slot], core_peer)
 
-    start = pl.multiple_of(((plane * 2 + core) * 2 + tensor) * rows, rows)
-    land[pl.ds(start, rows)] = own_ref[...]
-
-    @pl.when(plane < planes - 1)
-    def _():
-        along(plane, plane + 1, 0).start()
-
-    @pl.when(plane > 0)
-    def _():
-        along(plane, plane - 1, 1).start()
-
-    across(plane, tensor).start()
-    beside(plane, core, tensor, 0).start()
+    if not gathered:
+        start = pl.multiple_of(((plane * 2 + core) * 2 + tensor) * rows, rows)
+        land[pl.ds(start, rows)] = own_ref[...]
+
+        @pl.when(plane < planes - 1)
+        def _():
+            along(plane, plane + 1, 0).start()
+
+        @pl.when(plane > 0)
+        def _():
+            along(plane, plane - 1, 1).start()
+
+        across(plane, tensor).start()
+        beside(plane, core, tensor, 0).start()
 
     def reduce_core(at):
         return remote(core_out.at[at], core_in.at[at], rcs.at[at], rcr.at[at], core_peer)
@@ -351,25 +350,40 @@
             across(at, 1 - tensor).wait_recv()
             beside(at, core, 1 - tensor, 1).start()
 
+    def fetch(at):
+        span = pl.ds(pl.multiple_of(at * 4 * rows, 4 * rows), 4 * rows)
+        return pltpu.make_async_copy(own_ref.at[span], land.at[span], local.at[at])
+
+    if gathered:
+        for at in range(planes):
+            fetch(at).start()
+
     def step(index, carry):
+        if gathered:
+            index = 2 * planes - 2 - index
         distance = (index + 1) // 2
         at = side_plane(distance, 1 - index % 2)
 
-        @pl.when(jnp.logical_or(index == 0, index % 2 == 1))
-        def _():
-            pass_on(distance + 1, 0)
-            pass_on(distance + 1, 1)
-
-            @pl.when(distance > 0)
+        if not gathered:
+
+            @pl.when(jnp.logical_or(index == 0, index % 2 == 1))
             def _():
-                pass_beside(distance, 0)
-
-            pass_beside(distance, 1)
+                pass_on(distance + 1, 0)
+                pass_on(distance + 1, 1)
+
+                @pl.when(distance > 0)
+                def _():
+                    pass_beside(distance, 0)
+
+                pass_beside(distance, 1)
 
         @pl.when(inside(at))
         def _():
-            beside(at, 1 - core, tensor, 0).wait_recv()
-            beside(at, 1 - core, 1 - tensor, 1).wait_recv()
+            if gathered:
+                fetch(at).wait()
+            else:
+                beside(at, 1 - core, tensor, 0).wait_recv()
+                beside(at, 1 - core, 1 - tensor, 1).wait_recv()
             if piece is None:
                 save(at).start()
             theirs = pl.multiple_of((at * 2 + 1 - core) * 2 * rows, 2 * rows)
@@ -397,6 +411,8 @@
     reduce_y(plane).start()
 
     def collect(index, count):
+        if gathered:
+            index = 2 * planes - 3 - index
         at = side_plane((index + 2) // 2, index % 2)
 
         @pl.when(inside(at))
@@ -423,13 +439,14 @@
 
     lax.fori_loop(0, planes - 1, finish, 0)
 
-    @pl.when(plane < planes - 1)
-    def _():
-        along(plane, plane + 1, 0).wait_send()
-
-    @pl.when(plane > 0)
-    def _():
-        along(plane, plane - 1, 1).wait_send()
+    if not gathered:
+        @pl.when(plane < planes - 1)
+        def _():
+            along(plane, plane + 1, 0).wait_send()
+
+        @pl.when(plane > 0)
+        def _():
+            along(plane, plane - 1, 1).wait_send()
 
     def drain(index, carry):
         distance = (index + 1) // 2
@@ -439,13 +456,15 @@
 
         @pl.when(inside(at))
         def _():
-            @pl.when(jnp.logical_and(index > 0, inside(target)))
-            def _():
-                along(at, target, side).wait_send()
-
-            across(at, tensor).wait_send()
-            beside(at, core, tensor, 0).wait_send()
-            beside(at, core, 1 - tensor, 1).wait_send()
+            if not gathered:
+
+                @pl.when(jnp.logical_and(index > 0, inside(target)))
+                def _():
+                    along(at, target, side).wait_send()
+
+                across(at, tensor).wait_send()
+                beside(at, core, tensor, 0).wait_send()
+                beside(at, core, 1 - tensor, 1).wait_send()
             if piece is None:
                 save(at).wait()
             reduce_core(at).wait_send()
@@ -462,6 +481,9 @@
 
 def spread(chunk, piece, own, inputs, layer, outputs, work, planes, ident, name):
     rows, width = own.shape
+    gathered = rows == inputs[2].shape[0] if len(inputs) > 2 else False
+    if gathered:
+        rows //= 4 * planes
     count = planes * 4 * rows
     dma = pltpu.SemaphoreType.DMA
     shape = jax.ShapeDtypeStruct
@@ -469,10 +491,10 @@
     outs = [shape(saved, BF16), shape((rows, width), F32)] + list(outputs)
     return pl.pallas_call(
         functools.partial(
-            spread_kernel, chunk, piece, layer, planes, len(inputs), len(outputs), len(work)
+            spread_kernel, chunk, piece, layer, planes, gathered, len(inputs), len(outputs), len(work)
         ),
         out_shape=outs,
-        in_specs=[VMEM, HBM] + [VMEM] * (len(inputs) - 1),
+        in_specs=[HBM if gathered else VMEM, HBM] + [VMEM] * (len(inputs) - 1),
         out_specs=[HBM, VMEM] + [VMEM] * len(outputs),
         scratch_shapes=list(work)
         + [
@@ -595,7 +617,7 @@
             own, *expand_layer, down_w, gate_slope, up_slope, normed, hidden, planes
         )
     expand = expand_layer[0][expand_layer[1]]
-    rows = gather_tokens(own)
+    rows = own if own.shape[0] == normed.shape[0] else gather_tokens(own)
     grad_hidden = dot(rows, down_w, LAST)
     grad_gate = (grad_hidden * gate_slope.astype(F32)).astype(BF16)
     grad_up = (grad_hidden * up_slope.astype(F32)).astype(BF16)
@@ -620,16 +642,23 @@
     pl.semaphore_wait(barrier, planes)
 
 
-def attend_kernel(
-    planes, heads, q_ref, kv_ref, qpos_ref, kpos_ref, out_ref, low_ref, log_ref, all_ref,
-    zs, zr, cs, cr,
-):
+def attend_kernel(planes, heads, with_job, *refs):
+    q_ref, kv_ref, qpos_ref, kpos_ref = refs[:4]
+    if with_job:
+        out_ref, low_ref, log_ref, all_ref = refs[5:9]
+        zs, zr, cs, cr = refs[10:14]
+        start, stage, finish = share_job(2 * planes, refs[4], refs[9], *refs[14:])
+    else:
+        out_ref, low_ref, log_ref, all_ref, zs, zr, cs, cr = refs[4:]
     ctx = lax.axis_index("ctx")
     plane, core = ctx // 2, ctx % 2
     batch, tokens, pair = kv_ref.shape
     head_dim = pair // 2
     factor = 1.0 / math.sqrt(head_dim)
-    greet_line(planes, plane, core)
+    if with_job:
+        greet_all(2 * planes, ctx)
+    else:
+        greet_line(planes, plane, core)
     core_peer = {"ctx": plane * 2 + 1 - core}
 
     def block(at):
@@ -647,6 +676,8 @@
     for step in range(1, planes):
         along((plane + step) % planes, plane).start()
     beside(plane, core).start()
+    if with_job:
+        start()
     for step in range(1, planes):
         source = (plane + step) % planes
         along(source, source).wait_recv()
@@ -675,7 +706,16 @@
         log_ref[rows] = logs
         return carry
 
-    lax.fori_loop(0, batch, one, 0)
+    if with_job:
+        stages = 2 * planes - 1
+        for index in range(batch):
+            stage(index)
+            one(index, 0)
+        for index in range(batch, stages):
+            stage(index)
+        finish()
+    else:
+        lax.fori_loop(0, batch, one, 0)
     for step in range(1, planes):
         along((plane + step) % planes, plane).wait_send()
         beside((plane + step) % planes, core).wait_send()
@@ -761,7 +801,7 @@
             to_plane(index, (plane + step) % planes, plane).wait_send()
 
 
-def attend(queries, kv, query_pos, key_pos):
+def attend(queries, kv, query_pos, key_pos, blocks):
     batch, tokens, pair = kv.shape
     head_dim = pair // 2
     heads = queries.shape[1] // head_dim
@@ -780,29 +820,33 @@
         out = jnp.einsum(
             "bqhk,bkd->bqhd", probs, kv_all[..., head_dim:], preferred_element_type=F32
         ).reshape(queries.shape)
-        return out, out.astype(BF16), logs, kv_all
+        shared = [share(part) for part in blocks]
+        return out, out.astype(BF16), logs, kv_all, *shared
+    size = 2 * planes
     shape = jax.ShapeDtypeStruct
     dma = pltpu.SemaphoreType.DMA
     rows = batch * tokens
     return pl.pallas_call(
-        functools.partial(attend_kernel, planes, heads),
+        functools.partial(attend_kernel, planes, heads, len(blocks) > 0),
         out_shape=[
             shape(queries.shape, F32),
             shape(queries.shape, BF16),
             shape((rows, head_dim), F32),
             shape((batch, keys, pair), BF16),
-        ],
-        in_specs=[VMEM] * 4,
-        out_specs=[VMEM] * 4,
-        scratch_shapes=[dma((planes,)), dma((planes,)), dma((planes,)), dma((planes,))],
+        ]
+        + [shape((2,) + part.shape, part.dtype) for part in blocks],
+        in_specs=[VMEM] * 4 + [HBM] * len(blocks),
+        out_specs=[VMEM] * 4 + [HBM] * len(blocks),
+        scratch_shapes=[dma((planes,)), dma((planes,)), dma((planes,)), dma((planes,))]
+        + ([dma((size,))] * 4 + [dma]) * len(blocks),
         compiler_params=pltpu.CompilerParams(
-            collective_id=3, has_side_effects=True, vmem_limit_bytes=48 << 20
+            collective_id=3 + 2 * len(blocks), has_side_effects=True, vmem_limit_bytes=48 << 20
         ),
         cost_estimate=pl.CostEstimate(
             flops=rows * keys, bytes_accessed=rows, transcendentals=0
         ),
         name="attend",
-    )(queries, kv, query_pos[:, :, None], key_pos[:, None, :])
+    )(queries, kv, query_pos[:, :, None], key_pos[:, None, :], *blocks)
 
 
 def attend_backward(queries, kv_all, query_pos, key_pos, grads, out, logs):
@@ -858,7 +902,7 @@
     )(queries, kv_all, query_pos[:, :, None], key_pos[:, None, :], grads, out, logs)
 
 
-def layer_forward(x_low, weights, tables):
+def layer_forward(x_low, weights, tables, blocks, sooner, later):
     gain_attn, w_mixed, bias, w_project, gain_mlp, w_expand, w_reduce = weights
     cosine, sine, query_pos, key_pos, mine = tables
     count, width = x_low.shape
@@ -878,13 +922,17 @@
     ).astype(BF16).reshape(count, query_width)
     keys = rotate(mixed[:, query_width : query_width + head_dim], cosine, sine)
     kv = jnp.concatenate([keys, mixed[:, query_width + head_dim :]], axis=1).astype(BF16)
-    attended_full, attended, log_total, kv = attend(
-        queries, kv.reshape(batch, tokens, 2 * head_dim), query_pos, key_pos
-    )
+    kv, sooner = lax.optimization_barrier((kv, sooner))
+    attended_full, attended, log_total, kv, *shared = attend(
+        queries, kv.reshape(batch, tokens, 2 * head_dim), query_pos, key_pos, blocks
+    )
+    if shared:
+        w_expand = (shared[0].reshape((2, 2, width, -1)), 0)
     x_mine = lax.dynamic_slice_in_dim(x, mine * tokens, tokens, 0)
     middle = x_mine + tensor_scatter(dot(attended, w_project))
     root_mlp = inverse_root(middle)
     normed_mlp = (middle * root_mlp * gain_mlp).astype(BF16)
+    normed_mlp, later = lax.optimization_barrier((normed_mlp, later))
     all_normed, branch, gate_slope, up_slope, hidden = feed_forward(
         normed_mlp, w_expand, w_reduce
     )
@@ -905,10 +953,10 @@
         up_slope,
         hidden,
     )
-    return result.astype(BF16), kept
-
-
-def layer_backward(grad_out, kept, weights, tables, route, earlier):
+    return result.astype(BF16), kept, w_expand, sooner, later
+
+
+def layer_backward(grad_out, grad_rows, kept, weights, tables, route, earlier, pinned):
     gain_attn, w_mixed, bias, w_project, gain_mlp, w_expand, w_reduce = weights
     cosine, sine, query_pos, key_pos, mine = tables
     (
@@ -931,7 +979,7 @@
     head_dim = (w_mixed.shape[1] - query_width) // 2
     heads = query_width // head_dim
     grad_normed_mlp, d_expand, d_reduce = feed_backward(
-        grad_out.astype(BF16),
+        grad_rows,
         w_expand,
         w_reduce,
         gate_slope,
@@ -939,17 +987,19 @@
         all_normed,
         hidden,
     )
+    grad_normed_mlp, earlier = lax.optimization_barrier((grad_normed_mlp, earlier))
     moved_reduce = lax.ppermute(d_reduce, "section", route)
     grad_middle, d_gain_mlp = norm_backward(middle, root_mlp, gain_mlp, grad_normed_mlp)
     grad_middle = grad_middle + grad_out
-    grad_low, earlier = lax.optimization_barrier((grad_middle.astype(BF16), earlier))
-    grad_branch = tensor_gather(grad_low)
+    grad_branch = tensor_gather(grad_middle.astype(BF16))
     d_project = dot(attended, grad_branch, ROWS)
     grad_attended = dot(grad_branch, w_project, LAST).astype(BF16)
     grad_q, grad_kv = attend_backward(
         queries, kv, query_pos, key_pos, grad_attended, attended_full, log_total
     )
-    grad_q, grad_kv, moved_reduce = lax.optimization_barrier((grad_q, grad_kv, moved_reduce))
+    grad_q, grad_kv, moved_reduce, pinned = lax.optimization_barrier(
+        (grad_q, grad_kv, moved_reduce, pinned)
+    )
     grad_kv = grad_kv.reshape(count, 2 * head_dim)
     grad_q = unrotate(
         grad_q.reshape(count, heads, head_dim), cosine[:, None, :], sine[:, None, :]
@@ -964,7 +1014,7 @@
     grad_x, d_gain_attn = norm_backward(x_mine, root_attn, gain_attn, grad_normed)
     grad_x = (grad_x + grad_middle).astype(BF16)
     vectors = (d_gain_attn, d_mixed, d_bias, d_project, d_gain_mlp)
-    return grad_x, vectors, d_expand, (d_reduce, moved_reduce), earlier
+    return grad_x, vectors, d_expand, (d_reduce, moved_reduce), earlier, pinned
 
 
 def shards(
@@ -1005,11 +1055,10 @@
     small0, small1 = packed[:, :small_size], packed[:, small_size : 2 * small_size]
     qkv0, qkv1 = layers(qkv, swap(qkv))
     out0, out1 = layers(out, swap(out))
-    down0, down1 = layers(w_down[0], swap(w_down[0]))
+    down_moved = swap(w_down[0])
+    down0, down1 = layers(w_down[0], down_moved)
     expand = w_gate_up[0].reshape(slice_width, 2, ctx_size, units)
-    expand = share(jnp.transpose(expand, (1, 2, 0, 3))).reshape(2, 2, width, units)
-    x, expand = lax.optimization_barrier((x, expand))
-    expand0, expand1 = (expand, 0), (expand, 1)
+    blocks = jnp.transpose(expand, (1, 2, 0, 3))
 
     def whole(small, qkv, out, expand, down):
         return (
@@ -1022,13 +1071,18 @@
             down,
         )
 
-    weights0 = whole(small0, qkv0, out0, expand0, down0)
-    weights1 = whole(small1, qkv1, out1, expand1, down1)
-
-    result0, kept0 = layer_forward(x, weights0, tables)
+    weights0 = whole(small0, qkv0, out0, None, down0)
+
+    result0, kept0, expand0, down_moved, (qkv1, out1) = layer_forward(
+        x, weights0, tables, (blocks,), down_moved, (qkv1, out1)
+    )
+    weights0 = weights0[:5] + (expand0, down0)
+    weights1 = whole(small1, qkv1, out1, (expand0[0], 1), down1)
     x1 = tensor_gather(result0)
-    result1, kept1 = layer_forward(x1, weights1, tables)
-    out1_all = tensor_gather(result1)
+    seeds, x1 = lax.optimization_barrier((plane_part(cotangent), x1))
+    seed_rows = gather_ctx(seeds.reshape(half * tokens, width), 0)
+    result1, kept1, *_ = layer_forward(x1, weights1, tables, (), (), ())
+    out1_all = tensor_pair(result1)
 
     def exchange(layer0, layer1):
         kept_here = jnp.where(first, layer0, layer1)
@@ -1038,9 +1092,7 @@
         both = jnp.concatenate([low, high], axis=0)
         return both.reshape(1, micro, tokens, width)
 
-    section_output = exchange(x1, out1_all)
-
-    seed = lax.dynamic_slice_in_dim(cotangent, section * half + tensor, 1, 0)[0].astype(F32)
+    seed = lax.dynamic_slice_in_dim(seeds, tensor, 1, 0)[0].astype(F32)
     def ctx_scatter(value):
         return lax.psum_scatter(
             value.astype(BF16), "ctx", scatter_dimension=0, tiled=True
@@ -1065,16 +1117,16 @@
         both = jnp.concatenate([mixed.astype(BF16), rows.astype(BF16)], axis=1)
         return both.reshape(ctx_size * (slice_width + 16), group)
 
-    grad1, d1, d_expand1, d_reduce1, _ = layer_backward(
-        seed, kept1, weights1, tables, [(0, 1)], ()
-    )
+    grad1, d1, d_expand1, d_reduce1, _, out1_all = layer_backward(
+        seed, seed_rows, kept1, weights1, tables, [(0, 1)], (), out1_all
+    )
+    section_output = exchange(x1, out1_all)
     slices1 = (ctx_scatter(with_vectors(d1)), ctx_scatter(d1[3]))
-    grad1_all = tensor_gather(grad1)
-    grad1, grad1_all = lax.optimization_barrier((grad1, grad1_all))
-    grad0, d0, d_expand0, d_reduce0, earlier = layer_backward(
-        grad1.astype(F32), kept0, weights0, tables, [(1, 0)], slices1 + (section_output,)
-    )
-    slices1, section_output = earlier[:2], earlier[2]
+    grad1_all = tensor_pair(grad1)
+    grad0, d0, d_expand0, d_reduce0, earlier, _ = layer_backward(
+        grad1.astype(F32), grad1, kept0, weights0, tables, [(1, 0)], slices1 + (section_output, grad1_all), ()
+    )
+    slices1, (section_output, grad1_all) = earlier[:2], earlier[2:]
 
     def to_owner(part0, part1):
         received0 = lax.ppermute(part0.astype(BF16), "section", [(1, 0)])
@@ -1087,11 +1139,12 @@
         return own + received
 
     blocks = (2, ctx_size, slice_width, units)
-    grad0_all = tensor_gather(grad0)
+    grad0_all = tensor_pair(grad0)
     grad0_all, d_expand0 = lax.optimization_barrier((grad0_all, d_expand0))
     input_grad = exchange(grad0_all, grad1_all)
     total = collect(d_expand0.reshape(blocks), d_expand1.reshape(blocks), first)
-    d_expand = jnp.transpose(total, (2, 0, 1, 3)).reshape(1, slice_width, 2, ctx_size * units)
+    d_expand = lax.optimization_barrier(jnp.transpose(total, (2, 0, 1, 3)))
+    d_expand = lax.optimization_barrier(d_expand.reshape(1, slice_width, 2, ctx_size * units))
     d_expand = d_expand.astype(F32)
     d_reduce = of_owner(d_reduce0, d_reduce1)
 

time: 1120 us -> 1050 us (0.938)
  blocking collectives: 101 us -> 46.9 us
  other arithmetic: 63.5 us -> 78.4 us
  waiting for transfers between devices: 59.7 us -> 45.1 us
    all_gather x6 -> x3, blocking collectives: 56.5 us -> 28.2 us  [tensor_gather(): return lax.all_gather(rows, 'tensor', axis=0, tiled=True)]
    pallas_call x3 -> x2, Pallas kernels: 173 us -> 145 us  [attend(): pl.pallas_call(functools.partial(attend_kernel, planes, heads, len(blocks...]
    all_gather x1, blocking collectives: 44.2 us -> 18.7 us  [gather_ctx(): return lax.all_gather(value, 'ctx', axis=axis, tiled=True)]
    ppermute x6, waiting for transfers between devices: 29.5 us -> 9.94 us  [swap(): return lax.ppermute(value, 'section', SWAP)]
    unnamed x159 -> x163, local copies, waits for them, and re-layouts: 39 us -> 23.8 us
  transfers between devices with their start and end apart: 25 -> 29, of which waited for: 10 -> 8; matrix products, arithmetic and copies ran while one was open for 13% -> 14% of each run, Pallas kernels for 49% -> 62%
where the time goes in v3:
time: 1050 us
  Pallas kernels  729 us (69%)
  other arithmetic  78.4 us (7%)
  local copies, waits for them, and re-layouts  73.5 us (7%)
  blocking collectives  46.9 us (4%)
  waiting for transfers between devices  45.1 us (4%)
  matrix products  30.8 us (3%)
  starting transfers between devices  29.3 us (3%)
  between operations  15.4 us (1%)
    pallas_call x4, Pallas kernels, spread(): pl.pallas_call(functools.partial(spread_kernel, chunk, piece, layer, plan...  402 us
    pallas_call x2, Pallas kernels, attend(): pl.pallas_call(functools.partial(attend_kernel, planes, heads, len(blocks...  145 us
    pallas_call x1, Pallas kernels, collect(): pl.pallas_call(functools.partial(collect_kernel, size), out_shape=jax.Sha...  112 us
    pallas_call x2, Pallas kernels, attend_backward(): pl.pallas_call(functools.partial(attend_back_kernel, planes, heads), out_...  70.5 us
    dot_general x12, matrix products, dot(): return lax.dot_general(a, b, dims, preferred_element_type=F32)  30.8 us
    all_gather x3, blocking collectives, tensor_gather(): return lax.all_gather(rows, 'tensor', axis=0, tiled=True)  28.2 us
    unnamed x163, local copies, waits for them, and re-layouts  23.8 us
    ppermute x4, waiting for transfers between devices, tensor_scatter(): return own + lax.ppermute(other.astype(BF16), 'tensor', SWAP).astype(F32)  23 us
  transfers between devices with their start and end apart: 29, of which 8 were waited for; matrix products, arithmetic and copies ran while one was open for 14% of the time, Pallas kernels for 62%

profile of v3, /device:TPU:9, one launch (start us, length us, event | category | flops | bytes accessed | tf_op | source)
XLA Modules:
  0.0 1048.2 jit_solution(4252658790587076754)
XLA Ops:
  8.5 9.0 collective-permute-done.1
  31.1 10.9 %reshape.415 = bf16[192,2,8,560]{3,2,1,0:T(8,128)(2,1)} reshape(bf16[1,192,2,4480]{3,2,1,0:T(2,128)(2,1)} %param.18) | data formatting | bytes 6881280 | tf_op jit(solution)/shard_map/reshape;squeeze | solution.py:1060
  42.0 5.1 copy.78
  47.2 18.7 %all-gather.1 = bf16[8,1,1536]{2,1,0:T(2,128)(2,1)S(1)} all-gather(bf16[1,1,1536]{2,1,0:T(2,128)(2,1)S(1)} %reshape.411), channel_id=2, replica_groups=mesh['section'=2,'tensor'=2,'ctx'=8] {'ctx'}, dimensions={0}, use_global_device_ids=true | all-gather | bytes 27648 | tf_op jit(solution)/shard_map/all_gather | solution.py:66
  85.3 95.1 %attend.2 = (f32[256,768]{1,0:T(8,128)S(1)}, bf16[256,768]{1,0:T(8,128)(2,1)S(1)}, f32[256,128]{1,0:T(8,128)S(1)}, bf16[2,1024,256]{2,1,0:T(8,128)(2,1)S(1)}, bf16[2,2,8,192,560]{4,3,2,1,0:T(8,128)(2,1)}) custom-call(bf16[256,768]{1,0:T(8,128)(2,1)S(1)} %add_convert_fusion.7.refs_0_.q_ref, bf16[2,128,256]{2,1,0:T(8,128)(2,1)S(1)} %bitcast.122, ...), custom_call_target="tpu_custom_call" | custom-call | flops 262144 | bytes 256 | tf_op jit(solution)/shard_map/attend/pallas_call | solution.py:829
  188.2 5.5 collective-permute-done.4
  199.1 3.9 broadcast_select_fusion
  203.1 122.2 %mlp_forward.2 = (bf16[2048,1536]{1,0:T(8,128)(2,1)}, f32[128,1536]{1,0:T(8,128)}, bf16[2048,560]{1,0:T(8,128)(2,1)}, bf16[2048,560]{1,0:T(8,128)(2,1)}, bf16[2048,560]{1,0:T(8,128)(2,1)}) custom-call(bf16[128,1536]{1,0:T(8,128)(2,1)} %multiply_convert_fusion.3.own_ref, bf16[2,2,1536,560]{3,2,1,0:T(8,128)(2,1)} %bitcast.134, ...), custom_call_target="tpu_custom_call" | custom-call | flops 3145728 | bytes 2048 | tf_op jit(solution)/shard_map/mlp_forward/pallas_call | solution.py:492
  326.5 7.3 all_gather.30
  345.5 50.1 %attend.3 = (f32[256,768]{1,0:T(8,128)S(1)}, bf16[256,768]{1,0:T(8,128)(2,1)S(1)}, f32[256,128]{1,0:T(8,128)S(1)}, bf16[2,1024,256]{2,1,0:T(8,128)(2,1)S(1)}) custom-call(bf16[256,768]{1,0:T(8,128)(2,1)S(1)} %add_convert_fusion.5.refs_0_.q_ref, bf16[2,128,256]{2,1,0:T(8,128)(2,1)S(1)} %bitcast.123, s32[2,128,1]{2,1,0:T(8,128)S(1)} %copy-done.5, ...), custom_call_target="tpu_custom_call" | custom-call | flops 262144 | bytes 256 | tf_op jit(solution)/shard_map/attend/pallas_call | solution.py:829
  402.9 9.1 collective-permute-done.5
  415.1 96.0 %mlp_forward.3 = (bf16[2048,1536]{1,0:T(8,128)(2,1)}, f32[128,1536]{1,0:T(8,128)}, bf16[2048,560]{1,0:T(8,128)(2,1)}, bf16[2048,560]{1,0:T(8,128)(2,1)}, bf16[2048,560]{1,0:T(8,128)(2,1)}) custom-call(bf16[128,1536]{1,0:T(8,128)(2,1)} %multiply_convert_fusion.2.own_ref, bf16[2,2,1536,560]{3,2,1,0:T(8,128)(2,1)} %bitcast.135, ...), custom_call_target="tpu_custom_call" | custom-call | flops 3145728 | bytes 2048 | tf_op jit(solution)/shard_map/mlp_forward/pallas_call | solution.py:492
  511.1 74.8 %mlp_backward.2 = (bf16[16,1536]{1,0:T(8,128)(2,1)}, f32[128,1536]{1,0:T(8,128)}, bf16[2,1536,560]{2,1,0:T(8,128)(2,1)}, bf16[560,1536]{1,0:T(8,128)(2,1)}) custom-call(bf16[2048,1536]{1,0:T(8,128)(2,1)} %all-gather.16.cloned.1.call-done.own_ref, bf16[2,2,1536,560]{3,2,1,0:T(8,128)(2,1)} %bitcast.136, bf16[560,1536]{1,0:T(8,128)(2,1)} %get-tuple-element.140.refs_1_, ...), custom_call_target="tpu_custom_call" | custom-call | flops 3145728 | bytes 2048 | tf_op jit(solution)/shard_map/mlp_backward/pallas_call | solution.py:492
  590.3 10.3 all_gather.34
  600.6 4.2 collective-permute-start.6
  612.7 32.3 %attend_backward.2 = (f32[256,768]{1,0:T(8,128)S(1)}, f32[2,128,256]{2,1,0:T(8,128)S(1)}) custom-call(bf16[256,768]{1,0:T(8,128)(2,1)S(1)} %add_convert_fusion.5.refs_0_.q_ref, bf16[2,1024,256]{2,1,0:T(8,128)(2,1)S(1)} %copy-done.11, s32[2,128,1]{2,1,0:T(8,128)S(1)} %copy-done.5, s32[2,1,1024]{2,1,0:T(1,128)S(1)} %bitcast.132, ...), custom_call_target="tpu_custom_call" | custom-call | flops 262144 | bytes 256 | tf_op jit(solution)/shard_map/attend_backward/pallas_call | solution.py:882
  655.6 3.9 convolution_convert_fusion
  659.5 5.4 collective-permute-done.8
  666.5 4.1 fusion.2
  676.2 108.7 %mlp_backward.3 = (bf16[16,1536]{1,0:T(8,128)(2,1)}, f32[128,1536]{1,0:T(8,128)}, bf16[2,1536,560]{2,1,0:T(8,128)(2,1)}, bf16[560,1536]{1,0:T(8,128)(2,1)}) custom-call(bf16[128,1536]{1,0:T(8,128)(2,1)} %add_convert_fusion.2.own_ref, bf16[2,2,1536,560]{3,2,1,0:T(8,128)(2,1)} %bitcast.137, bf16[560,1536]{1,0:T(8,128)(2,1)} %get-tuple-element.141.refs_1_, ...), custom_call_target="tpu_custom_call" | custom-call | flops 3145728 | bytes 2048 | tf_op jit(solution)/shard_map/mlp_backward/pallas_call | solution.py:492
  793.1 10.6 %all_gather.35 = bf16[256,1536]{1,0:T(8,128)(2,1)S(1)} all-gather(bf16[128,1536]{1,0:T(8,128)(2,1)S(1)} %fusion.24), channel_id=1, replica_groups=mesh['section'=2,'tensor'=2,'ctx'=8] {'tensor'}, dimensions={0}, use_global_device_ids=true | all-gather | bytes 1179648 | tf_op jit(solution)/shard_map/all_gather | solution.py:78
  810.5 38.2 %attend_backward.3 = (f32[256,768]{1,0:T(8,128)S(1)}, f32[2,128,256]{2,1,0:T(8,128)S(1)}) custom-call(bf16[256,768]{1,0:T(8,128)(2,1)S(1)} %add_convert_fusion.7.refs_0_.q_ref, bf16[2,1024,256]{2,1,0:T(8,128)(2,1)S(1)} %copy-done.9, s32[2,128,1]{2,1,0:T(8,128)S(1)} %copy-done.5, s32[2,1,1024]{2,1,0:T(1,128)S(1)} %bitcast.133, ...), custom_call_target="tpu_custom_call" | custom-call | flops 262144 | bytes 256 | tf_op jit(solution)/shard_map/attend_backward/pallas_call | solution.py:882
  857.8 4.0 convolution_convert_fusion.3
  865.7 4.1 fusion.3
  873.5 5.5 collective-permute-start.19
  884.9 4.2 add_bitcast_fusion
  890.0 111.7 %collect.1 = bf16[2,8,192,560]{3,2,1,0:T(8,128)(2,1)S(1)} custom-call(bf16[2,8,192,560]{3,2,1,0:T(8,128)(2,1)S(1)} %bitcast.121, bf16[2,8,192,560]{3,2,1,0:T(8,128)(2,1)S(1)} %bitcast.120), custom_call_target="tpu_custom_call" | custom-call | flops 1720320 | bytes 1024 | tf_op jit(solution)/shard_map/collect/pallas_call | solution.py:230
  1001.6 4.2 copy.69
  1005.8 6.1 reshape.399
  1012.0 6.4 copy.71
  1023.8 5.7 collective-permute-done.18
  1030.5 5.7 collective-permute-done.15
  (365 shorter events, 149.9 us)
Async XLA Ops:
  7.2 191.0 %copy-start = (bf16[4,128,1536]{2,1,0:T(8,128)(2,1)S(1)}, bf16[4,128,1536]{2,1,0:T(8,128)(2,1)}, u32[]{:S(2)}) copy-start(bf16[4,128,1536]{2,1,0:T(8,128)(2,1)} %param.12) | copy-start | bytes 4718596
  7.2 62.0 %all-gather.8.cloned.1.call-start = ((), (), s32[]{:S(2)}) async-start(), calls=%async_computation.4 | async-start | bytes 3538944 | tf_op jit(solution)/shard_map/all_gather | solution.py:66
  7.3 10.3 collective-permute-start.1
  19.5 162.6 %all-gather.10.cloned.1.call-start = ((), (), s32[]{:S(2)}) async-start(), calls=%async_computation.5 | async-start | bytes 2654208 | tf_op jit(solution)/shard_map/all_gather | solution.py:66
  19.5 7.2 collective-permute-start.3
  22.9 24.2 %collective-permute-start = (bf16[512]{0:T(512)(128)(2,1)S(1)}, bf16[512]{0:T(512)(128)(2,1)S(1)}, u32[]{:S(2)}, u32[]{:S(2)}) collective-permute-start(bf16[512]{0:T(512)(128)(2,1)S(1)} %pad_maximum_fusion.13), channel_id=1, source_target_pairs={{0,16},{16,0},{1,17},{17,1},{2,18},{18,2},{3,19},{19,3},{4,20},{20... | collective-permute-start | bytes 3080 | tf_op jit(solution)/shard_map/ppermute | solution.py:62
  23.2 51.0 %collective-permute-start.2 = (bf16[560,1536]{1,0:T(8,128)(2,1)}, bf16[560,1536]{1,0:T(8,128)(2,1)}, u32[]{:S(2)}, u32[]{:S(2)}) collective-permute-start(bf16[560,1536]{1,0:T(8,128)(2,1)} %bitcast.157), channel_id=1, source_target_pairs={{0,16},{16,0},{1,17},{17,1},{2,18},{18,2},{3,19},{19,3},{4,20},{20... | collective-permute-start | bytes 5160968 | tf_op jit(solution)/shard_map/ppermute | solution.py:62
  27.6 306.5 %all-gather.12.cloned.1.call-start = ((), (), s32[]{:S(2)}) async-start(), calls=%async_computation.6 | async-start | bytes 3538944 | tf_op jit(solution)/shard_map/all_gather | solution.py:66
  186.8 6.9 collective-permute-start.4
  197.3 200.8 %all-gather.14.cloned.1.call-start = ((), (), s32[]{:S(2)}) async-start(), calls=%async_computation.7 | async-start | bytes 2654208 | tf_op jit(solution)/shard_map/all_gather | solution.py:66
  197.9 313.2 %all-gather.16.cloned.1.call-start = ((), (), s32[]{:S(2)}) async-start(), calls=%async_computation.8 | async-start | bytes 7077888 | tf_op jit(solution)/shard_map/all_gather | solution.py:66
  203.1 122.2 %copy-start.21 = (f32[128,1536]{1,0:T(8,128)S(1)}, f32[128,1536]{1,0:T(8,128)}, u32[]{:S(2)}) copy-start(f32[128,1536]{1,0:T(8,128)} %copy-done.20) | copy-start | bytes 2359300
  333.8 457.1 %reduce-scatter.7.cloned.1.call-start = ((), (), s32[]{:S(2)}) async-start(), calls=%async_computation.10 | async-start | bytes 2654208 | tf_op jit(solution)/shard_map/reduce_scatter | solution.py:1097
  401.7 10.3 collective-permute-start.5
  413.1 174.5 %copy-start.67 = (f32[128]{0:T(128)}, f32[128]{0:T(128)S(1)}, u32[]{:S(2)}) copy-start(f32[128]{0:T(128)S(1)} %add_rsqrt_fusion.2) | copy-start | bytes 1540
  600.6 46.6 %collective-permute-start.6 = (bf16[560,1536]{1,0:T(8,128)(2,1)}, bf16[560,1536]{1,0:T(8,128)(2,1)}, u32[]{:S(2)}, u32[]{:S(2)}) collective-permute-start(bf16[560,1536]{1,0:T(8,128)(2,1)} %get-tuple-element.79), channel_id=1, source_target_pairs={{0,16},{1,17},{2,18},{3,19},{4,20},{5,21},{6,22},{7,23},{8,24},{9,... | collective-permute-start | bytes 5160968 | tf_op jit(solution)/shard_map/ppermute | solution.py:991
  607.1 183.8 %reduce-scatter.5.cloned.1.call-start = ((), (), s32[]{:S(2)}) async-start(), calls=%async_computation.9 | async-start | bytes 3833856 | tf_op jit(solution)/shard_map/reduce_scatter | solution.py:1097
  607.1 37.9 %collective-permute-start.7 = (bf16[128,1536]{1,0:T(8,128)(2,1)}, bf16[128,1536]{1,0:T(8,128)(2,1)}, u32[]{:S(2)}, u32[]{:S(2)}) collective-permute-start(bf16[128,1536]{1,0:T(8,128)(2,1)} %get-tuple-element.160), channel_id=1, source_target_pairs={{0,8},{8,0},{1,9},{9,1},{2,10},{10,2},{3,11},{11,3},{4,12},{12,4},... | collective-permute-start | bytes 1179656 | tf_op jit(solution)/shard_map/ppermute | solution.py:82
  654.4 10.6 %collective-permute-start.8 = (bf16[128,1536]{1,0:T(8,128)(2,1)}, bf16[128,1536]{1,0:T(8,128)(2,1)}, u32[]{:S(2)}, u32[]{:S(2)}) collective-permute-start(bf16[128,1536]{1,0:T(8,128)(2,1)} %dynamic-slice_convert_fusion.1), channel_id=1, source_target_pairs={{0,8},{8,0},{1,9},{9,1},{2,10},{10,2},{3,11},{11,3},{4,12},{12,4},... | collective-permute-start | bytes 1179656 | tf_op jit(solution)/shard_map/ppermute | solution.py:92
  670.6 347.8 %reduce-scatter.11.cloned.1.call-start = ((), (), s32[]{:S(2)}) async-start(), calls=%async_computation.12 | async-start | bytes 2654208 | tf_op jit(solution)/shard_map/reduce_scatter | solution.py:1097
  674.3 112.0 %collective-permute-start.10 = (bf16[128,1536]{1,0:T(8,128)(2,1)}, bf16[128,1536]{1,0:T(8,128)(2,1)S(1)}, u32[]{:S(2)}, u32[]{:S(2)}) collective-permute-start(bf16[128,1536]{1,0:T(8,128)(2,1)} %add_convert_fusion.2.own_ref), channel_id=1, source_target_pairs={{0,8},{8,0},{1,9},{9,1},{2,10},{10,2},{3,11},{11,3},{4,12},{12,4},... | collective-permute-start | bytes 1179656 | tf_op jit(solution)/shard_map/ppermute | solution.py:82
  676.2 112.1 %collective-permute-start.9 = (bf16[256,1536]{1,0:T(8,128)(2,1)}, bf16[256,1536]{1,0:T(8,128)(2,1)}, u32[]{:S(2)}, u32[]{:S(2)}) collective-permute-start(bf16[256,1536]{1,0:T(8,128)(2,1)} %broadcast_select_fusion.8), channel_id=1, source_target_pairs={{0,16},{16,0},{1,17},{17,1},{2,18},{18,2},{3,19},{19,3},{4,20},{20... | collective-permute-start | bytes 2359304 | tf_op jit(solution)/shard_map/ppermute | solution.py:62
  784.9 63.8 %collective-permute-start.11 = (bf16[560,1536]{1,0:T(8,128)(2,1)}, bf16[560,1536]{1,0:T(8,128)(2,1)}, u32[]{:S(2)}, u32[]{:S(2)}) collective-permute-start(bf16[560,1536]{1,0:T(8,128)(2,1)} %get-tuple-element.96), channel_id=1, source_target_pairs={{16,0},{17,1},{18,2},{19,3},{20,4},{21,5},{22,6},{23,7},{24,8},{25... | collective-permute-start | bytes 5160968 | tf_op jit(solution)/shard_map/ppermute | solution.py:991
  806.9 215.6 %reduce-scatter.9.cloned.1.call-start = ((), (), s32[]{:S(2)}) async-start(), calls=%async_computation.11 | async-start | bytes 3833856 | tf_op jit(solution)/shard_map/reduce_scatter | solution.py:1097
  855.7 8.9 collective-permute-start.12
  873.0 8.0 collective-permute-start.13
  873.5 150.3 %collective-permute-start.19 = (bf16[96,1536]{1,0:T(8,128)(2,1)}, bf16[96,1536]{1,0:T(8,128)(2,1)}, u32[]{:S(2)}, u32[]{:S(2)}) collective-permute-start(bf16[96,1536]{1,0:T(8,128)(2,1)} %reduce-scatter.7.cloned.1.call-done), channel_id=1, source_target_pairs={{0,16},{1,17},{2,18},{3,19},{4,20},{5,21},{6,22},{7,23},{8,24},{9,... | collective-permute-start | bytes 884744 | tf_op jit(solution)/shard_map/ppermute | solution.py:1133
  878.9 151.5 %collective-permute-start.16 = (bf16[208,1024]{1,0:T(8,128)(2,1)}, bf16[208,1024]{1,0:T(8,128)(2,1)}, u32[]{:S(2)}, u32[]{:S(2)}) collective-permute-start(bf16[208,1024]{1,0:T(8,128)(2,1)} %reduce-scatter.5.cloned.1.call-done), channel_id=1, source_target_pairs={{0,16},{1,17},{2,18},{3,19},{4,20},{5,21},{6,22},{7,23},{8,24},{9,... | collective-permute-start | bytes 1277960 | tf_op jit(solution)/shard_map/ppermute | solution.py:1133
  882.3 137.4 %collective-permute-start.14 = (bf16[256,1536]{1,0:T(8,128)(2,1)}, bf16[256,1536]{1,0:T(8,128)(2,1)}, u32[]{:S(2)}, u32[]{:S(2)}) collective-permute-start(bf16[256,1536]{1,0:T(8,128)(2,1)} %broadcast_select_fusion.4), channel_id=1, source_target_pairs={{0,16},{16,0},{1,17},{17,1},{2,18},{18,2},{3,19},{19,3},{4,20},{20... | collective-permute-start | bytes 2359304 | tf_op jit(solution)/shard_map/ppermute | solution.py:62
  1018.4 11.1 %collective-permute-start.18 = (bf16[96,1536]{1,0:T(8,128)(2,1)}, bf16[96,1536]{1,0:T(8,128)(2,1)S(1)}, u32[]{:S(2)}, u32[]{:S(2)}) collective-permute-start(bf16[96,1536]{1,0:T(8,128)(2,1)} %reduce-scatter.11.cloned.1.call-done), channel_id=1, source_target_pairs={{16,0},{17,1},{18,2},{19,3},{20,4},{21,5},{22,6},{23,7},{24,8},{25... | collective-permute-start | bytes 884744 | tf_op jit(solution)/shard_map/ppermute | solution.py:1132
  1022.5 13.7 %collective-permute-start.15 = (bf16[208,1024]{1,0:T(8,128)(2,1)}, bf16[208,1024]{1,0:T(8,128)(2,1)S(1)}, u32[]{:S(2)}, u32[]{:S(2)}) collective-permute-start(bf16[208,1024]{1,0:T(8,128)(2,1)} %reduce-scatter.9.cloned.1.call-done), channel_id=1, source_target_pairs={{16,0},{17,1},{18,2},{19,3},{20,4},{21,5},{22,6},{23,7},{24,8},{25... | collective-permute-start | bytes 1277960 | tf_op jit(solution)/shard_map/ppermute | solution.py:1132
  1038.1 2.7 collective-permute-start.17
  (76 other events, 495.1 us)
Sparse Core Ops, SparseCore 0:
  19.6 39.8 all-gather.7
  61.2 31.3 all-gather.9
  197.4 64.5 all-gather.11
  263.5 36.0 all-gather.13
  333.9 83.9 all-gather.15
  607.2 45.9 reduce-scatter.6
  670.7 56.8 reduce-scatter.4
  807.0 55.0 reduce-scatter.10
  870.0 43.5 reduce-scatter.8

commit v4 on v3

--- a/solution.py
+++ b/solution.py
@@ -248,7 +248,9 @@
     )
 
 
-def spread_kernel(chunk, piece, layer, planes, gathered, ins, outs, extra, own_ref, *refs):
+def spread_kernel(
+    chunk, piece, layer, planes, gathered, reduced, ins, outs, extra, own_ref, *refs
+):
     in_refs, refs = refs[:ins], refs[ins:]
     all_ref, sum_ref = refs[:2]
     out_refs, refs = refs[2 : 2 + outs], refs[2 + outs :]
@@ -387,9 +389,14 @@
             if piece is None:
                 save(at).start()
             theirs = pl.multiple_of((at * 2 + 1 - core) * 2 * rows, 2 * rows)
+            mine = pl.multiple_of((at * 2 + core) * 2 * rows, 2 * rows)
+            if not reduced:
+                for start in (theirs, mine):
+                    part = chunk(land, start, 2 * rows, in_refs, out_refs, work_refs)
+                    sum_ref[pl.ds(start, 2 * rows)] = part.astype(BF16)
+                return
             core_out[at] = chunk(land, theirs, 2 * rows, in_refs, out_refs, work_refs).astype(BF16)
             reduce_core(at).start()
-            mine = pl.multiple_of((at * 2 + core) * 2 * rows, 2 * rows)
             both[...] = chunk(land, mine, 2 * rows, in_refs, out_refs, work_refs)
             reduce_core(at).wait_recv()
             both[...] += core_in[at].astype(F32)
@@ -408,36 +415,37 @@
     load.wait()
     lax.fori_loop(0, 2 * planes - 1, step, 0)
 
-    reduce_y(plane).start()
-
-    def collect(index, count):
-        if gathered:
-            index = 2 * planes - 3 - index
-        at = side_plane((index + 2) // 2, index % 2)
-
-        @pl.when(inside(at))
-        def _():
-            if piece is not None:
-                piece(land, count, planes, in_refs, out_refs, work_refs)
-            reduce_y(at).wait_recv()
-            z_out[at] = (kept[at] + y_in[at].astype(F32)).astype(BF16)
-            reduce_z(at).start()
-
-        return count + inside(at).astype(jnp.int32)
-
-    count = lax.fori_loop(0, 2 * planes - 2, collect, 0)
-    if piece is not None:
-        piece(land, count, planes, in_refs, out_refs, work_refs)
-    reduce_y(plane).wait_recv()
-    sum_ref[...] = kept[plane] + y_in[plane].astype(F32)
-
-    def finish(index, carry):
-        at = (plane + 1 + index) % planes
-        reduced_z(at).wait_recv()
-        sum_ref[...] += z_in[at].astype(F32)
-        return carry
-
-    lax.fori_loop(0, planes - 1, finish, 0)
+    if reduced:
+        reduce_y(plane).start()
+
+        def collect(index, count):
+            if gathered:
+                index = 2 * planes - 3 - index
+            at = side_plane((index + 2) // 2, index % 2)
+
+            @pl.when(inside(at))
+            def _():
+                if piece is not None:
+                    piece(land, count, planes, in_refs, out_refs, work_refs)
+                reduce_y(at).wait_recv()
+                z_out[at] = (kept[at] + y_in[at].astype(F32)).astype(BF16)
+                reduce_z(at).start()
+
+            return count + inside(at).astype(jnp.int32)
+
+        count = lax.fori_loop(0, 2 * planes - 2, collect, 0)
+        if piece is not None:
+            piece(land, count, planes, in_refs, out_refs, work_refs)
+        reduce_y(plane).wait_recv()
+        sum_ref[...] = kept[plane] + y_in[plane].astype(F32)
+
+        def finish(index, carry):
+            at = (plane + 1 + index) % planes
+            reduced_z(at).wait_recv()
+            sum_ref[...] += z_in[at].astype(F32)
+            return carry
+
+        lax.fori_loop(0, planes - 1, finish, 0)
 
     if not gathered:
         @pl.when(plane < planes - 1)
@@ -467,19 +475,20 @@
                 beside(at, core, 1 - tensor, 1).wait_send()
             if piece is None:
                 save(at).wait()
-            reduce_core(at).wait_send()
-            reduce_y(at).wait_send()
-
-            @pl.when(index > 0)
-            def _():
-                reduce_z(at).wait_send()
+            if reduced:
+                reduce_core(at).wait_send()
+                reduce_y(at).wait_send()
+
+                @pl.when(index > 0)
+                def _():
+                    reduce_z(at).wait_send()
 
         return carry
 
     lax.fori_loop(0, 2 * planes - 1, drain, 0)
 
 
-def spread(chunk, piece, own, inputs, layer, outputs, work, planes, ident, name):
+def spread(chunk, piece, own, inputs, layer, outputs, work, planes, ident, name, reduced=True):
     rows, width = own.shape
     gathered = rows == inputs[2].shape[0] if len(inputs) > 2 else False
     if gathered:
@@ -488,10 +497,12 @@
     dma = pltpu.SemaphoreType.DMA
     shape = jax.ShapeDtypeStruct
     saved = (count, width) if piece is None else (16, width)
-    outs = [shape(saved, BF16), shape((rows, width), F32)] + list(outputs)
+    total = shape((rows, width), F32) if reduced else shape((count, width), BF16)
+    outs = [shape(saved, BF16), total] + list(outputs)
+    held = planes if reduced else 1
     return pl.pallas_call(
         functools.partial(
-            spread_kernel, chunk, piece, layer, planes, gathered, len(inputs), len(outputs), len(work)
+            spread_kernel, chunk, piece, layer, planes, gathered, reduced, len(inputs), len(outputs), len(work)
         ),
         out_shape=outs,
         in_specs=[HBM if gathered else VMEM, HBM] + [VMEM] * (len(inputs) - 1),
@@ -501,14 +512,14 @@
             pltpu.VMEM(inputs[0].shape[1:], BF16),
             pltpu.SemaphoreType.DMA,
             pltpu.VMEM((count, width), BF16),
-            pltpu.VMEM((planes, 2 * rows, width), BF16),
-            pltpu.VMEM((planes, 2 * rows, width), BF16),
-            pltpu.VMEM((planes, rows, width), BF16),
-            pltpu.VMEM((planes, rows, width), BF16),
-            pltpu.VMEM((planes, rows, width), BF16),
-            pltpu.VMEM((planes, rows, width), BF16),
+            pltpu.VMEM((held, 2 * rows, width), BF16),
+            pltpu.VMEM((held, 2 * rows, width), BF16),
+            pltpu.VMEM((held, rows, width), BF16),
+            pltpu.VMEM((held, rows, width), BF16),
+            pltpu.VMEM((held, rows, width), BF16),
+            pltpu.VMEM((held, rows, width), BF16),
             pltpu.VMEM((2 * rows, width), F32),
-            pltpu.VMEM((planes, rows, width), F32),
+            pltpu.VMEM((held, rows, width), F32),
             dma((planes, 2)), dma((planes,)), dma((planes,)), dma((planes,)), dma((planes, 2)), dma((planes, 2)),
             dma((planes,)), dma((planes,)), dma((planes,)), dma((planes,)), dma((planes,)), dma((planes,)), dma((planes,)),
         ],
@@ -574,6 +585,7 @@
         planes,
         1,
         "mlp_forward",
+        layer == 0,
     )
 
 
@@ -598,7 +610,8 @@
 def feed_forward(own, expand_layer, down_w):
     planes = lax.axis_size("ctx") // 2
     if planes == 4:
-        return mlp_forward(own, *expand_layer, down_w, planes)
+        rows, total, *kept = mlp_forward(own, *expand_layer, down_w, planes)
+        return rows, total if expand_layer[1] == 0 else scatter_tokens(total), *kept
     expand = expand_layer[0][expand_layer[1]]
     rows = gather_tokens(own)
     gate, up = dot(rows, expand[0]), dot(rows, expand[1])
@@ -643,17 +656,18 @@
 
 
 def attend_kernel(planes, heads, with_job, *refs):
-    q_ref, kv_ref, qpos_ref, kpos_ref = refs[:4]
+    mixed_ref, cosine_ref, sine_ref, qpos_ref, kpos_ref = refs[:5]
     if with_job:
-        out_ref, low_ref, log_ref, all_ref = refs[5:9]
-        zs, zr, cs, cr = refs[10:14]
-        start, stage, finish = share_job(2 * planes, refs[4], refs[9], *refs[14:])
+        out_ref, low_ref, log_ref, all_ref, q_ref = refs[6:11]
+        zs, zr, cs, cr = refs[12:16]
+        start, stage, finish = share_job(2 * planes, refs[5], refs[11], *refs[16:])
     else:
-        out_ref, low_ref, log_ref, all_ref, zs, zr, cs, cr = refs[4:]
+        out_ref, low_ref, log_ref, all_ref, q_ref, zs, zr, cs, cr = refs[5:]
     ctx = lax.axis_index("ctx")
     plane, core = ctx // 2, ctx % 2
-    batch, tokens, pair = kv_ref.shape
-    head_dim = pair // 2
+    batch, tokens = qpos_ref.shape[:2]
+    head_dim = cosine_ref.shape[1]
+    query_width = heads * head_dim
     factor = 1.0 / math.sqrt(head_dim)
     if with_job:
         greet_all(2 * planes, ctx)
@@ -672,7 +686,16 @@
         ref = block(source * 2 + which)
         return remote(ref, ref, cs.at[source], cr.at[source], core_peer)
 
-    all_ref[:, pl.ds(pl.multiple_of(ctx * tokens, tokens), tokens)] = kv_ref[...]
+    def turned(rows, span):
+        values = mixed_ref[rows, span]
+        return values * cosine_ref[rows] + pltpu.roll(values, head_dim // 2, 1) * sine_ref[rows]
+
+    own = pl.ds(pl.multiple_of(ctx * tokens, tokens), tokens)
+    for index in range(batch):
+        rows = slice(index * tokens, (index + 1) * tokens)
+        keys = turned(rows, slice(query_width, query_width + head_dim))
+        all_ref[index, own, :head_dim] = keys.astype(BF16)
+        all_ref[index, own, head_dim:] = mixed_ref[rows, query_width + head_dim :].astype(BF16)
     for step in range(1, planes):
         along((plane + step) % planes, plane).start()
     beside(plane, core).start()
@@ -694,7 +717,9 @@
         logs = jnp.zeros((tokens, head_dim), F32)
         for head in range(heads):
             span = slice(head * head_dim, (head + 1) * head_dim)
-            scores = dot(q_ref[rows, span], keys, LAST)
+            queries = turned(rows, span).astype(BF16)
+            q_ref[rows, span] = queries
+            scores = dot(queries, keys, LAST)
             scores = jnp.where(allowed, scores * factor, -1e30)
             top = jnp.max(scores, axis=1, keepdims=True)
             weights = jnp.exp(scores - top)
@@ -723,8 +748,8 @@
 
 
 def attend_back_kernel(
-    planes, heads, q_ref, kv_ref, qpos_ref, kpos_ref, grad_ref, out_ref, log_ref, dq_ref, dkv_ref,
-    whole, core_out, core_in, z_out, z_in, cs, cr, zs, zr,
+    planes, heads, q_ref, kv_ref, qpos_ref, kpos_ref, grad_ref, out_ref, log_ref, cosine_ref,
+    sine_ref, mixed_ref, dkv_ref, whole, core_out, core_in, z_out, z_in, cs, cr, zs, zr,
 ):
     ctx = lax.axis_index("ctx")
     plane, core = ctx // 2, ctx % 2
@@ -734,6 +759,10 @@
     factor = 1.0 / math.sqrt(head_dim)
     greet_line(planes, plane, core)
     core_peer = {"ctx": plane * 2 + 1 - core}
+
+    def turned_back(grads, rows):
+        rolled = pltpu.roll(grads, head_dim // 2, 1)
+        return (grads * cosine_ref[rows] - rolled * sine_ref[rows]).astype(BF16)
 
     def to_core(index):
         return remote(core_out.at[index], core_in.at[index], cs.at[index], cr.at[index], core_peer)
@@ -761,7 +790,7 @@
             scores = jnp.where(allowed, dot(queries, keys, LAST) * factor, -1e30)
             weights = jnp.exp(scores - logs[:, head : head + 1])
             grad_scores = (weights * (dot(grads, values, LAST) - delta) * factor).astype(BF16)
-            dq_ref[rows, span] = dot(grad_scores, keys)
+            mixed_ref[rows, span] = turned_back(dot(grad_scores, keys), rows)
             grad_keys = dot(grad_scores, queries, ROWS)
             grad_values = dot(weights.astype(BF16), grads, ROWS)
             if head == 0:
@@ -795,20 +824,34 @@
             source = (plane + step) % planes
             to_plane(index, source, source).wait_recv()
             dkv_ref[index] += z_in[index, source].astype(F32)
+        rows = slice(index * tokens, (index + 1) * tokens)
+        width = heads * head_dim
+        mixed_ref[rows, width : width + head_dim] = turned_back(dkv_ref[index, :, :head_dim], rows)
+        mixed_ref[rows, width + head_dim :] = dkv_ref[index, :, head_dim:].astype(BF16)
     for index in range(batch):
         to_core(index).wait_send()
         for step in range(1, planes):
             to_plane(index, (plane + step) % planes, plane).wait_send()
 
 
-def attend(queries, kv, query_pos, key_pos, blocks):
-    batch, tokens, pair = kv.shape
-    head_dim = pair // 2
-    heads = queries.shape[1] // head_dim
+def attend(mixed, tables, heads, blocks):
+    cosine, sine, query_pos, key_pos, _ = tables
+    batch, tokens = query_pos.shape
+    head_dim = cosine.shape[1]
+    query_width = heads * head_dim
+    pair = 2 * head_dim
     planes = lax.axis_size("ctx") // 2
     keys = key_pos.shape[1]
+    rows = batch * tokens
     if planes != 4:
-        kv_all = gather_ctx(kv, 1)
+        queries = rotate(
+            mixed[:, :query_width].reshape(rows, heads, head_dim),
+            cosine[:, None, :],
+            sine[:, None, :],
+        ).astype(BF16).reshape(rows, query_width)
+        own_keys = rotate(mixed[:, query_width : query_width + head_dim], cosine, sine)
+        kv = jnp.concatenate([own_keys, mixed[:, query_width + head_dim :]], axis=1).astype(BF16)
+        kv_all = gather_ctx(kv.reshape(batch, tokens, pair), 1)
         split = queries.reshape(batch, tokens, heads, head_dim)
         scores = jnp.einsum(
             "bqhd,bkd->bqhk", split, kv_all[..., :head_dim], preferred_element_type=F32
@@ -821,22 +864,22 @@
             "bqhk,bkd->bqhd", probs, kv_all[..., head_dim:], preferred_element_type=F32
         ).reshape(queries.shape)
         shared = [share(part) for part in blocks]
-        return out, out.astype(BF16), logs, kv_all, *shared
+        return out, out.astype(BF16), logs, kv_all, queries, *shared
     size = 2 * planes
     shape = jax.ShapeDtypeStruct
     dma = pltpu.SemaphoreType.DMA
-    rows = batch * tokens
     return pl.pallas_call(
         functools.partial(attend_kernel, planes, heads, len(blocks) > 0),
         out_shape=[
-            shape(queries.shape, F32),
-            shape(queries.shape, BF16),
+            shape((rows, query_width), F32),
+            shape((rows, query_width), BF16),
             shape((rows, head_dim), F32),
             shape((batch, keys, pair), BF16),
+            shape((rows, query_width), BF16),
         ]
         + [shape((2,) + part.shape, part.dtype) for part in blocks],
-        in_specs=[VMEM] * 4 + [HBM] * len(blocks),
-        out_specs=[VMEM] * 4 + [HBM] * len(blocks),
+        in_specs=[VMEM] * 5 + [HBM] * len(blocks),
+        out_specs=[VMEM] * 5 + [HBM] * len(blocks),
         scratch_shapes=[dma((planes,)), dma((planes,)), dma((planes,)), dma((planes,))]
         + ([dma((size,))] * 4 + [dma]) * len(blocks),
         compiler_params=pltpu.CompilerParams(
@@ -846,10 +889,16 @@
             flops=rows * keys, bytes_accessed=rows, transcendentals=0
         ),
         name="attend",
-    )(queries, kv, query_pos[:, :, None], key_pos[:, None, :], *blocks)
-
-
-def attend_backward(queries, kv_all, query_pos, key_pos, grads, out, logs):
+    )(mixed, cosine, signed(sine), query_pos[:, :, None], key_pos[:, None, :], *blocks)
+
+
+def signed(sine):
+    half = sine.shape[1] // 2
+    return jnp.concatenate([-sine[:, :half], sine[:, half:]], axis=1)
+
+
+def attend_backward(queries, kv_all, tables, grads, out, logs):
+    cosine, sine, query_pos, key_pos, _ = tables
     batch, keys, pair = kv_all.shape
     head_dim = pair // 2
     heads = queries.shape[1] // head_dim
@@ -876,15 +925,20 @@
         dkv = lax.psum_scatter(
             jnp.concatenate([dk, dv], axis=-1).astype(BF16), "ctx", scatter_dimension=1, tiled=True
         )
-        return dq.reshape(queries.shape), dkv.astype(F32)
+        dkv = dkv.astype(F32).reshape(rows, pair)
+        dq = unrotate(dq.reshape(rows, heads, head_dim), cosine[:, None, :], sine[:, None, :])
+        dk = unrotate(dkv[:, :head_dim], cosine, sine)
+        parts = [dq.reshape(queries.shape), dk, dkv[:, head_dim:]]
+        return jnp.concatenate(parts, axis=1).astype(BF16)
     shape = jax.ShapeDtypeStruct
     dma = pltpu.SemaphoreType.DMA
     return pl.pallas_call(
         functools.partial(attend_back_kernel, planes, heads),
-        out_shape=[shape(queries.shape, F32), shape((batch, tokens, pair), F32)],
-        in_specs=[VMEM] * 7,
-        out_specs=[VMEM] * 2,
+        out_shape=shape((rows, queries.shape[1] + pair), BF16),
+        in_specs=[VMEM] * 9,
+        out_specs=VMEM,
         scratch_shapes=[
+            pltpu.VMEM((batch, tokens, pair), F32),
             pltpu.VMEM((batch, keys, pair), F32),
             pltpu.VMEM((batch, planes, tokens, pair), BF16),
             pltpu.VMEM((batch, planes, tokens, pair), BF16),
@@ -899,7 +953,17 @@
             flops=rows * keys, bytes_accessed=rows, transcendentals=0
         ),
         name="attend_backward",
-    )(queries, kv_all, query_pos[:, :, None], key_pos[:, None, :], grads, out, logs)
+    )(
+        queries,
+        kv_all,
+        query_pos[:, :, None],
+        key_pos[:, None, :],
+        grads,
+        out,
+        logs,
+        cosine,
+        signed(sine),
+    )
 
 
 def layer_forward(x_low, weights, tables, blocks, sooner, later):
@@ -915,16 +979,9 @@
     root_attn = inverse_root(x)
     normed = (x * root_attn * gain_attn).astype(BF16)
     mixed = dot(normed, w_mixed) + bias
-    queries = rotate(
-        mixed[:, :query_width].reshape(count, heads, head_dim),
-        cosine[:, None, :],
-        sine[:, None, :],
-    ).astype(BF16).reshape(count, query_width)
-    keys = rotate(mixed[:, query_width : query_width + head_dim], cosine, sine)
-    kv = jnp.concatenate([keys, mixed[:, query_width + head_dim :]], axis=1).astype(BF16)
-    kv, sooner = lax.optimization_barrier((kv, sooner))
-    attended_full, attended, log_total, kv, *shared = attend(
-        queries, kv.reshape(batch, tokens, 2 * head_dim), query_pos, key_pos, blocks
+    mixed, sooner = lax.optimization_barrier((mixed, sooner))
+    attended_full, attended, log_total, kv, queries, *shared = attend(
+        mixed, tables, heads, blocks
     )
     if shared:
         w_expand = (shared[0].reshape((2, 2, width, -1)), 0)
@@ -991,23 +1048,15 @@
     moved_reduce = lax.ppermute(d_reduce, "section", route)
     grad_middle, d_gain_mlp = norm_backward(middle, root_mlp, gain_mlp, grad_normed_mlp)
     grad_middle = grad_middle + grad_out
-    grad_branch = tensor_gather(grad_middle.astype(BF16))
+    grad_branch = tensor_pair(grad_middle.astype(BF16))
     d_project = dot(attended, grad_branch, ROWS)
     grad_attended = dot(grad_branch, w_project, LAST).astype(BF16)
-    grad_q, grad_kv = attend_backward(
-        queries, kv, query_pos, key_pos, grad_attended, attended_full, log_total
-    )
-    grad_q, grad_kv, moved_reduce, pinned = lax.optimization_barrier(
-        (grad_q, grad_kv, moved_reduce, pinned)
-    )
-    grad_kv = grad_kv.reshape(count, 2 * head_dim)
-    grad_q = unrotate(
-        grad_q.reshape(count, heads, head_dim), cosine[:, None, :], sine[:, None, :]
-    )
-    grad_k = unrotate(grad_kv[:, :head_dim], cosine, sine)
-    grad_mixed = jnp.concatenate(
-        [grad_q.reshape(count, heads * head_dim), grad_k, grad_kv[:, head_dim:]], axis=1
-    ).astype(BF16)
+    grad_mixed = attend_backward(
+        queries, kv, tables, grad_attended, attended_full, log_total
+    )
+    grad_mixed, moved_reduce, pinned = lax.optimization_barrier(
+        (grad_mixed, moved_reduce, pinned)
+    )
     d_mixed = dot(normed, grad_mixed, ROWS)
     d_bias = jnp.sum(grad_mixed.astype(F32), axis=0)
     grad_normed = tensor_scatter(dot(grad_mixed, w_mixed, LAST))
@@ -1078,7 +1127,7 @@
     )
     weights0 = weights0[:5] + (expand0, down0)
     weights1 = whole(small1, qkv1, out1, (expand0[0], 1), down1)
-    x1 = tensor_gather(result0)
+    x1 = tensor_pair(result0)
     seeds, x1 = lax.optimization_barrier((plane_part(cotangent), x1))
     seed_rows = gather_ctx(seeds.reshape(half * tokens, width), 0)
     result1, kept1, *_ = layer_forward(x1, weights1, tables, (), (), ())

time: 1050 us -> 1030 us (0.981)
  waiting for transfers between devices: 45.1 us -> 89.2 us
  blocking collectives: 46.9 us -> 17.5 us
  other arithmetic: 78.4 us -> 53.2 us
    all_gather x3 -> x0, blocking collectives: 28.2 us -> none  [tensor_gather(): return lax.all_gather(rows, 'tensor', axis=0, tiled=True)]
    ppermute x3 -> x6, waiting for transfers between devices: 0.04 us -> 27.2 us  [tensor_pair(): received = lax.ppermute(rows, 'tensor', SWAP)]
    unnamed x163 -> x165, local copies, waits for them, and re-layouts: 23.8 us -> 27.6 us
  transfers between devices with their start and end apart: 29 -> 33, of which waited for: 8 -> 13; matrix products, arithmetic and copies ran while one was open for 14% -> 11% of each run, Pallas kernels for 62% -> 71%
where the time goes in v4:
time: 1030 us; the launch traced here: 1020 us
  Pallas kernels  725 us (70%)
  waiting for transfers between devices  89.2 us (9%)
  local copies, waits for them, and re-layouts  63.7 us (6%)
  other arithmetic  53.2 us (5%)
  starting transfers between devices  29.6 us (3%)
  matrix products  29.4 us (3%)
  blocking collectives  17.5 us (2%)
  between operations  15.8 us (2%)
    pallas_call x4, Pallas kernels, spread(): pl.pallas_call(functools.partial(spread_kernel, chunk, piece, layer, plan...  396 us
    pallas_call x2, Pallas kernels, attend(): pl.pallas_call(functools.partial(attend_kernel, planes, heads, len(blocks...  146 us
    pallas_call x1, Pallas kernels, collect(): pl.pallas_call(functools.partial(collect_kernel, size), out_shape=jax.Sha...  115 us
    pallas_call x2, Pallas kernels, attend_backward(): pl.pallas_call(functools.partial(attend_back_kernel, planes, heads), out_...  69.1 us
    dot_general x12, matrix products, dot(): return lax.dot_general(a, b, dims, preferred_element_type=F32)  29.4 us
    unnamed x165, local copies, waits for them, and re-layouts  27.6 us
    ppermute x6, waiting for transfers between devices, tensor_pair(): received = lax.ppermute(rows, 'tensor', SWAP)  27.2 us
    ppermute x4, waiting for transfers between devices, tensor_scatter(): return own + lax.ppermute(other.astype(BF16), 'tensor', SWAP).astype(F32)  22.3 us
  transfers between devices with their start and end apart: 33, of which 13 were waited for; matrix products, arithmetic and copies ran while one was open for 11% of the time, Pallas kernels for 71%

profile of v4, /device:TPU:9, one launch (start us, length us, event | category | flops | bytes accessed | tf_op | source)
XLA Modules:
  0.0 1023.4 jit_solution(11716973638857436515)
XLA Ops:
  8.5 9.0 collective-permute-done.1
  20.8 6.0 collective-permute-done.3
  32.9 11.3 %reshape.317 = bf16[192,2,8,560]{3,2,1,0:T(8,128)(2,1)} reshape(bf16[1,192,2,4480]{3,2,1,0:T(2,128)(2,1)} %param.18) | data formatting | bytes 6881280 | tf_op jit(solution)/shard_map/reshape;squeeze | solution.py:1109
  44.2 5.1 copy.50
  50.0 17.5 %all-gather.1 = bf16[8,1,1536]{2,1,0:T(2,128)(2,1)S(1)} all-gather(bf16[1,1,1536]{2,1,0:T(2,128)(2,1)S(1)} %reshape.313), channel_id=2, replica_groups=mesh['section'=2,'tensor'=2,'ctx'=8] {'ctx'}, dimensions={0}, use_global_device_ids=true | all-gather | bytes 27648 | tf_op jit(solution)/shard_map/all_gather | solution.py:66
  75.2 105.9 %attend.2 = (f32[256,768]{1,0:T(8,128)S(1)}, bf16[256,768]{1,0:T(8,128)(2,1)S(1)}, f32[256,128]{1,0:T(8,128)S(1)}, bf16[2,1024,256]{2,1,0:T(8,128)(2,1)S(1)}, bf...) custom-call(f32[256,1024]{1,0:T(8,128)S(1)} %convolution_add_fusion.1.refs_0_, ...), custom_call_target="tpu_custom_call" | custom-call | flops 262144 | bytes 256 | tf_op jit(solution)/shard_map/attend/pallas_call | solution.py:871
  189.8 5.1 collective-permute-done.4
  199.1 4.0 broadcast_select_fusion
  203.1 128.6 %mlp_forward.2 = (bf16[2048,1536]{1,0:T(8,128)(2,1)}, f32[128,1536]{1,0:T(8,128)}, bf16[2048,560]{1,0:T(8,128)(2,1)}, bf16[2048,560]{1,0:T(8,128)(2,1)}, bf16[2048,560]{1,0:T(8,128)(2,1)}) custom-call(bf16[128,1536]{1,0:T(8,128)(2,1)} %multiply_convert_fusion.3.own_ref, bf16[2,2,1536,560]{3,2,1,0:T(8,128)(2,1)} %bitcast.112, ...), custom_call_target="tpu_custom_call" | custom-call | flops 3145728 | bytes 2048 | tf_op jit(solution)/shard_map/mlp_forward/pallas_call | solution.py:503
  335.6 7.6 collective-permute-done.5
  346.9 39.7 %attend.3 = (f32[256,768]{1,0:T(8,128)S(1)}, bf16[256,768]{1,0:T(8,128)(2,1)S(1)}, f32[256,128]{1,0:T(8,128)S(1)}, bf16[2,1024,256]{2,1,0:T(8,128)(2,1)S(1)}, bf16[256,768]{1,0:T(8,128)(2,1)S(1)}) custom-call(f32[256,1024]{1,0:T(8,128)S(1)} %convolution_add_fusion.refs_0_, f32[256,128]{1,0:T(8,128)S(1)} %get-tuple-element.159.refs_1_.cosine_ref, ...), custom_call_target="tpu_custom_call" | custom-call | flops 262144 | bytes 256 | tf_op jit(solution)/shard_map/attend/pallas_call | solution.py:871
  394.6 7.8 collective-permute-done.6
  404.4 56.6 %mlp_forward.3 = (bf16[2048,1536]{1,0:T(8,128)(2,1)}, bf16[2048,1536]{1,0:T(8,128)(2,1)}, bf16[2048,560]{1,0:T(8,128)(2,1)}, bf16[2048,560]{1,0:T(8,128)(2,1)}, bf16[2048,560]{1,0:T(8,128)(2,1)}) custom-call(bf16[128,1536]{1,0:T(8,128)(2,1)} %multiply_convert_fusion.2.own_ref, bf16[2,2,1536,560]{3,2,1,0:T(8,128)(2,1)} %bitcast.113, ...), custom_call_target="tpu_custom_call" | custom-call | flops 3145728 | bytes 2048 | tf_op jit(solution)/shard_map/mlp_forward/pallas_call | solution.py:503
  461.4 98.5 %mlp_backward.2 = (bf16[16,1536]{1,0:T(8,128)(2,1)}, f32[128,1536]{1,0:T(8,128)}, bf16[2,1536,560]{2,1,0:T(8,128)(2,1)}, bf16[560,1536]{1,0:T(8,128)(2,1)}) custom-call(bf16[2048,1536]{1,0:T(8,128)(2,1)} %all-gather.16.cloned.1.call-done.own_ref, bf16[2,2,1536,560]{3,2,1,0:T(8,128)(2,1)} %bitcast.114, bf16[560,1536]{1,0:T(8,128)(2,1)} %get-tuple-element.132.refs_1_, ...), custom_call_target="tpu_custom_call" | custom-call | flops 3145728 | bytes 2048 | tf_op jit(solution)/shard_map/mlp_backward/pallas_call | solution.py:503
  561.8 10.1 reduce-scatter.6.cloned.1.call-done
  575.9 8.0 collective-permute-done.7
  587.0 3.7 collective-permute-start.8
  595.1 30.7 %attend_backward.2 = bf16[256,1024]{1,0:T(8,128)(2,1)S(1)} custom-call(bf16[256,768]{1,0:T(8,128)(2,1)S(1)} %copy-done.15, bf16[2,1024,256]{2,1,0:T(8,128)(2,1)S(1)} %get-tuple-element.63.kv_ref, s32[2,128,1]{2,1,0:T(8,128)S(1)} %copy.34.refs_3_.qpos_ref, s32[2,1,1024]{2,1,0:T(1,128)S(1)} %bitcast.110, ...), custom_call_target="tpu_custom_call" | custom-call | flops 262144 | bytes 256 | tf_op jit(solution)/shard_map/attend_backward/pallas_call | solution.py:935
  633.8 6.3 collective-permute-done.10
  640.6 4.1 fusion.2
  648.3 111.9 %mlp_backward.3 = (bf16[16,1536]{1,0:T(8,128)(2,1)}, f32[128,1536]{1,0:T(8,128)}, bf16[2,1536,560]{2,1,0:T(8,128)(2,1)}, bf16[560,1536]{1,0:T(8,128)(2,1)}) custom-call(bf16[128,1536]{1,0:T(8,128)(2,1)} %copy-done.28, bf16[2,2,1536,560]{3,2,1,0:T(8,128)(2,1)} %bitcast.115, bf16[560,1536]{1,0:T(8,128)(2,1)} %get-tuple-element.133.refs_1_, ...), custom_call_target="tpu_custom_call" | custom-call | flops 3145728 | bytes 2048 | tf_op jit(solution)/shard_map/mlp_backward/pallas_call | solution.py:503
  767.2 9.0 collective-permute-done.13
  782.8 38.4 %attend_backward.3 = bf16[256,1024]{1,0:T(8,128)(2,1)S(1)} custom-call(bf16[256,768]{1,0:T(8,128)(2,1)S(1)} %copy-done.13, bf16[2,1024,256]{2,1,0:T(8,128)(2,1)S(1)} %copy-done.7, s32[2,128,1]{2,1,0:T(8,128)S(1)} %copy.34.refs_3_.qpos_ref, s32[2,1,1024]{2,1,0:T(1,128)S(1)} %bitcast.111, bf16[256,768]{1,0:T(8,128)(2,1)S(1)} %convolution_convert_fusion.4.grad_ref, ...), custom_call_target="tpu_custom_call" | custom-call | flops 262144 | bytes 256 | tf_op jit(solution)/shard_map/attend_backward/pallas_call | solution.py:935
  826.8 3.9 convolution_convert_fusion.3
  834.9 4.1 fusion.3
  842.4 3.6 collective-permute-start.19
  857.4 114.6 %collect.1 = bf16[2,8,192,560]{3,2,1,0:T(8,128)(2,1)S(1)} custom-call(bf16[2,8,192,560]{3,2,1,0:T(8,128)(2,1)S(1)} %bitcast.107, bf16[2,8,192,560]{3,2,1,0:T(8,128)(2,1)S(1)} %bitcast.106), custom_call_target="tpu_custom_call" | custom-call | flops 1720320 | bytes 1024 | tf_op jit(solution)/shard_map/collect/pallas_call | solution.py:230
  972.0 4.2 copy.41
  976.2 7.5 reshape.301
  983.7 8.4 copy.43
  996.2 7.1 collective-permute-done.21
  1004.3 6.8 collective-permute-done.18
  (336 shorter events, 122.6 us)
Async XLA Ops:
  7.2 64.9 %all-gather.8.cloned.1.call-start = ((), (), s32[]{:S(2)}) async-start(), calls=%async_computation.5 | async-start | bytes 3538944 | tf_op jit(solution)/shard_map/all_gather | solution.py:66
  7.2 10.3 %collective-permute-start.1 = (bf16[192,1024]{1,0:T(8,128)(2,1)}, bf16[192,1024]{1,0:T(8,128)(2,1)S(1)}, u32[]{:S(2)}, u32[]{:S(2)}) collective-permute-start(bf16[192,1024]{1,0:T(8,128)(2,1)} %bitcast.129), channel_id=1, source_target_pairs={{0,16},{16,0},{1,17},{17,1},{2,18},{18,2},{3,19},{19,3},{4,20},{20... | collective-permute-start | bytes 1179656 | tf_op jit(solution)/shard_map/ppermute | solution.py:62
  19.5 165.0 %all-gather.10.cloned.1.call-start = ((), (), s32[]{:S(2)}) async-start(), calls=%async_computation.6 | async-start | bytes 2654208 | tf_op jit(solution)/shard_map/all_gather | solution.py:66
  19.5 7.2 collective-permute-start.3
  28.6 315.4 %all-gather.12.cloned.1.call-start = ((), (), s32[]{:S(2)}) async-start(), calls=%async_computation.7 | async-start | bytes 3538944 | tf_op jit(solution)/shard_map/all_gather | solution.py:66
  29.3 19.9 %collective-permute-start = (bf16[512]{0:T(512)(128)(2,1)}, bf16[512]{0:T(512)(128)(2,1)}, u32[]{:S(2)}, u32[]{:S(2)}) collective-permute-start(bf16[512]{0:T(512)(128)(2,1)} %pad_maximum_fusion.15), channel_id=1, source_target_pairs={{0,16},{16,0},{1,17},{17,1},{2,18},{18,2},{3,19},{19,3},{4,20},{20... | collective-permute-start | bytes 3080 | tf_op jit(solution)/shard_map/ppermute | solution.py:62
  30.5 44.7 %collective-permute-start.2 = (bf16[560,1536]{1,0:T(8,128)(2,1)}, bf16[560,1536]{1,0:T(8,128)(2,1)}, u32[]{:S(2)}, u32[]{:S(2)}) collective-permute-start(bf16[560,1536]{1,0:T(8,128)(2,1)} %bitcast.126), channel_id=1, source_target_pairs={{0,16},{16,0},{1,17},{17,1},{2,18},{18,2},{3,19},{19,3},{4,20},{20... | collective-permute-start | bytes 5160968 | tf_op jit(solution)/shard_map/ppermute | solution.py:62
  188.2 6.6 collective-permute-start.4
  198.3 189.9 %all-gather.14.cloned.1.call-start = ((), (), s32[]{:S(2)}) async-start(), calls=%async_computation.8 | async-start | bytes 2654208 | tf_op jit(solution)/shard_map/all_gather | solution.py:66
  198.8 262.6 %all-gather.16.cloned.1.call-start = ((), (), s32[]{:S(2)}) async-start(), calls=%async_computation.9 | async-start | bytes 7077888 | tf_op jit(solution)/shard_map/all_gather | solution.py:66
  333.1 10.1 collective-permute-start.5
  343.3 228.6 %reduce-scatter.6.cloned.1.call-start = ((), (), s32[]{:S(2)}) async-start(), calls=%async_computation.10 | async-start | bytes 6684672 | tf_op jit(solution)/shard_map/reduce_scatter | solution.py:74
  391.9 10.6 %collective-permute-start.6 = (bf16[128,1536]{1,0:T(8,128)(2,1)S(1)}, bf16[128,1536]{1,0:T(8,128)(2,1)S(1)}, u32[]{:S(2)}, u32[]{:S(2)}) collective-permute-start(bf16[128,1536]{1,0:T(8,128)(2,1)S(1)} %dynamic-slice_convert_fusion.2), channel_id=1, source_target_pairs={{0,8},{8,0},{1,9},{9,1},{2,10},{10,2},{3,11},{11,3},{4,12},{12,4},... | collective-permute-start | bytes 1179656 | tf_op jit(solution)/shard_map/ppermute | solution.py:92
  461.1 304.0 %reduce-scatter.10.cloned.1.call-start = ((), (), s32[]{:S(2)}) async-start(), calls=%async_computation.12 | async-start | bytes 2654208 | tf_op jit(solution)/shard_map/reduce_scatter | solution.py:1146
  574.3 9.5 collective-permute-start.7
  586.9 178.1 %reduce-scatter.8.cloned.1.call-start = ((), (), s32[]{:S(2)}) async-start(), calls=%async_computation.11 | async-start | bytes 3833856 | tf_op jit(solution)/shard_map/reduce_scatter | solution.py:1146
  587.0 41.1 %collective-permute-start.8 = (bf16[560,1536]{1,0:T(8,128)(2,1)}, bf16[560,1536]{1,0:T(8,128)(2,1)S(1)}, u32[]{:S(2)}, u32[]{:S(2)}) collective-permute-start(bf16[560,1536]{1,0:T(8,128)(2,1)} %get-tuple-element.74), channel_id=1, source_target_pairs={{0,16},{1,17},{2,18},{3,19},{4,20},{5,21},{6,22},{7,23},{8,24},{9,... | collective-permute-start | bytes 5160968 | tf_op jit(solution)/shard_map/ppermute | solution.py:1048
  590.7 35.2 %collective-permute-start.9 = (bf16[128,1536]{1,0:T(8,128)(2,1)}, bf16[128,1536]{1,0:T(8,128)(2,1)S(1)}, u32[]{:S(2)}, u32[]{:S(2)}) collective-permute-start(bf16[128,1536]{1,0:T(8,128)(2,1)} %get-tuple-element.146), channel_id=1, source_target_pairs={{0,8},{8,0},{1,9},{9,1},{2,10},{10,2},{3,11},{11,3},{4,12},{12,4},... | collective-permute-start | bytes 1179656 | tf_op jit(solution)/shard_map/ppermute | solution.py:82
  630.4 9.7 collective-permute-start.10
  644.7 347.4 %reduce-scatter.14.cloned.1.call-start = ((), (), s32[]{:S(2)}) async-start(), calls=%async_computation.14 | async-start | bytes 2654208 | tf_op jit(solution)/shard_map/reduce_scatter | solution.py:1146
  647.3 113.0 %collective-permute-start.12 = (bf16[128,1536]{1,0:T(8,128)(2,1)S(1)}, bf16[128,1536]{1,0:T(8,128)(2,1)}, u32[]{:S(2)}, u32[]{:S(2)}) collective-permute-start(bf16[128,1536]{1,0:T(8,128)(2,1)S(1)} %add_convert_fusion.1.own_ref), channel_id=1, source_target_pairs={{0,8},{8,0},{1,9},{9,1},{2,10},{10,2},{3,11},{11,3},{4,12},{12,4},... | collective-permute-start | bytes 1179656 | tf_op jit(solution)/shard_map/ppermute | solution.py:82
  648.3 114.1 %collective-permute-start.11 = (bf16[256,1536]{1,0:T(8,128)(2,1)}, bf16[256,1536]{1,0:T(8,128)(2,1)}, u32[]{:S(2)}, u32[]{:S(2)}) collective-permute-start(bf16[256,1536]{1,0:T(8,128)(2,1)} %broadcast_select_fusion.8), channel_id=1, source_target_pairs={{0,16},{16,0},{1,17},{17,1},{2,18},{18,2},{3,19},{19,3},{4,20},{20... | collective-permute-start | bytes 2359304 | tf_op jit(solution)/shard_map/ppermute | solution.py:62
  766.3 9.9 collective-permute-start.13
  778.6 216.2 %reduce-scatter.12.cloned.1.call-start = ((), (), s32[]{:S(2)}) async-start(), calls=%async_computation.13 | async-start | bytes 3833856 | tf_op jit(solution)/shard_map/reduce_scatter | solution.py:1146
  778.7 42.6 %collective-permute-start.14 = (bf16[560,1536]{1,0:T(8,128)(2,1)}, bf16[560,1536]{1,0:T(8,128)(2,1)S(1)}, u32[]{:S(2)}, u32[]{:S(2)}) collective-permute-start(bf16[560,1536]{1,0:T(8,128)(2,1)} %get-tuple-element.89), channel_id=1, source_target_pairs={{16,0},{17,1},{18,2},{19,3},{20,4},{21,5},{22,6},{23,7},{24,8},{25... | collective-permute-start | bytes 5160968 | tf_op jit(solution)/shard_map/ppermute | solution.py:1048
  824.4 9.5 collective-permute-start.15
  842.2 8.4 collective-permute-start.16
  842.4 161.9 %collective-permute-start.19 = (bf16[208,1024]{1,0:T(8,128)(2,1)}, bf16[208,1024]{1,0:T(8,128)(2,1)}, u32[]{:S(2)}, u32[]{:S(2)}) collective-permute-start(bf16[208,1024]{1,0:T(8,128)(2,1)} %reduce-scatter.8.cloned.1.call-done), channel_id=1, source_target_pairs={{0,16},{1,17},{2,18},{3,19},{4,20},{5,21},{6,22},{7,23},{8,24},{9,... | collective-permute-start | bytes 1277960 | tf_op jit(solution)/shard_map/ppermute | solution.py:1182
  846.0 150.2 %collective-permute-start.22 = (bf16[96,1536]{1,0:T(8,128)(2,1)}, bf16[96,1536]{1,0:T(8,128)(2,1)}, u32[]{:S(2)}, u32[]{:S(2)}) collective-permute-start(bf16[96,1536]{1,0:T(8,128)(2,1)} %reduce-scatter.10.cloned.1.call-done), channel_id=1, source_target_pairs={{0,16},{1,17},{2,18},{3,19},{4,20},{5,21},{6,22},{7,23},{8,24},{9,... | collective-permute-start | bytes 884744 | tf_op jit(solution)/shard_map/ppermute | solution.py:1182
  850.9 142.5 %collective-permute-start.17 = (bf16[256,1536]{1,0:T(8,128)(2,1)S(1)}, bf16[256,1536]{1,0:T(8,128)(2,1)S(1)}, u32[]{:S(2)}, u32[]{:S(2)}) collective-permute-start(bf16[256,1536]{1,0:T(8,128)(2,1)S(1)} %broadcast_select_fusion.4), channel_id=1, source_target_pairs={{0,16},{16,0},{1,17},{17,1},{2,18},{18,2},{3,19},{19,3},{4,20},{20... | collective-permute-start | bytes 2359304 | tf_op jit(solution)/shard_map/ppermute | solution.py:62
  992.1 11.2 %collective-permute-start.21 = (bf16[96,1536]{1,0:T(8,128)(2,1)}, bf16[96,1536]{1,0:T(8,128)(2,1)S(1)}, u32[]{:S(2)}, u32[]{:S(2)}) collective-permute-start(bf16[96,1536]{1,0:T(8,128)(2,1)} %reduce-scatter.14.cloned.1.call-done), channel_id=1, source_target_pairs={{16,0},{17,1},{18,2},{19,3},{20,4},{21,5},{22,6},{23,7},{24,8},{25... | collective-permute-start | bytes 884744 | tf_op jit(solution)/shard_map/ppermute | solution.py:1181
  994.8 16.3 %collective-permute-start.18 = (bf16[208,1024]{1,0:T(8,128)(2,1)}, bf16[208,1024]{1,0:T(8,128)(2,1)S(1)}, u32[]{:S(2)}, u32[]{:S(2)}) collective-permute-start(bf16[208,1024]{1,0:T(8,128)(2,1)} %reduce-scatter.12.cloned.1.call-done), channel_id=1, source_target_pairs={{16,0},{17,1},{18,2},{19,3},{20,4},{21,5},{22,6},{23,7},{24,8},{25... | collective-permute-start | bytes 1277960 | tf_op jit(solution)/shard_map/ppermute | solution.py:1181
  (81 other events, 948.4 us)
Sparse Core Ops, SparseCore 0:
  19.6 39.7 all-gather.7
  61.6 41.7 all-gather.9
  198.4 63.3 all-gather.11
  263.8 35.8 all-gather.13
  343.4 75.9 all-gather.15
  461.2 110.6 reduce-scatter.5
  587.0 45.9 reduce-scatter.9
  644.8 59.3 reduce-scatter.7
  778.7 54.0 reduce-scatter.13
  839.2 50.2 reduce-scatter.11

commit v5 on v4

--- a/solution.py
+++ b/solution.py
@@ -1049,14 +1049,17 @@
     grad_middle, d_gain_mlp = norm_backward(middle, root_mlp, gain_mlp, grad_normed_mlp)
     grad_middle = grad_middle + grad_out
     grad_branch = tensor_pair(grad_middle.astype(BF16))
-    d_project = dot(attended, grad_branch, ROWS)
     grad_attended = dot(grad_branch, w_project, LAST).astype(BF16)
     grad_mixed = attend_backward(
         queries, kv, tables, grad_attended, attended_full, log_total
     )
-    grad_mixed, moved_reduce, pinned = lax.optimization_barrier(
-        (grad_mixed, moved_reduce, pinned)
-    )
+    if earlier:
+        d_project = dot(attended, grad_branch, ROWS)
+    grad_mixed, moved_reduce, pinned, late_branch = lax.optimization_barrier(
+        (grad_mixed, moved_reduce, pinned, grad_branch)
+    )
+    if not earlier:
+        d_project = dot(attended, late_branch, ROWS)
     d_mixed = dot(normed, grad_mixed, ROWS)
     d_bias = jnp.sum(grad_mixed.astype(F32), axis=0)
     grad_normed = tensor_scatter(dot(grad_mixed, w_mixed, LAST))

time: 1030 us -> 1010 us (0.981)
  Pallas kernels: 725 us -> 709 us
    pallas_call x4, Pallas kernels: 396 us -> 385 us  [spread(): pl.pallas_call(functools.partial(spread_kernel, chunk, piece, layer, plan...]
    unnamed x165 -> x159, local copies, waits for them, and re-layouts: 27.6 us -> 27 us
  transfers between devices with their start and end apart: 33 -> 33, of which waited for: 13 -> 14; matrix products, arithmetic and copies ran while one was open for 11% -> 11% of each run, Pallas kernels for 71% -> 71%
where the time goes in v5:
time: 1010 us; the launch traced here: 1000 us
  Pallas kernels  709 us (70%)
  waiting for transfers between devices  86.7 us (9%)
  local copies, waits for them, and re-layouts  63 us (6%)
  other arithmetic  51.5 us (5%)
  starting transfers between devices  31.4 us (3%)
  matrix products  29.6 us (3%)
  blocking collectives  17.5 us (2%)
  between operations  15.8 us (2%)
    pallas_call x4, Pallas kernels, spread(): pl.pallas_call(functools.partial(spread_kernel, chunk, piece, layer, plan...  385 us
    pallas_call x2, Pallas kernels, attend(): pl.pallas_call(functools.partial(attend_kernel, planes, heads, len(blocks...  146 us
    pallas_call x1, Pallas kernels, collect(): pl.pallas_call(functools.partial(collect_kernel, size), out_shape=jax.Sha...  117 us
    pallas_call x2, Pallas kernels, attend_backward(): pl.pallas_call(functools.partial(attend_back_kernel, planes, heads), out_...  61.4 us
    dot_general x12, matrix products, dot(): return lax.dot_general(a, b, dims, preferred_element_type=F32)  29.6 us
    unnamed x159, local copies, waits for them, and re-layouts  27 us
    ppermute x6, waiting for transfers between devices, tensor_pair(): received = lax.ppermute(rows, 'tensor', SWAP)  21.7 us
  transfers between devices with their start and end apart: 33, of which 14 were waited for; matrix products, arithmetic and copies ran while one was open for 11% of the time, Pallas kernels for 71%

profile of v5, /device:TPU:9, one launch (start us, length us, event | category | flops | bytes accessed | tf_op | source)
XLA Modules:
  0.0 1004.4 jit_solution(2729426395609251891)
XLA Ops:
  8.5 9.0 collective-permute-done.1
  20.8 6.0 collective-permute-done.3
  32.9 11.3 %reshape.317 = bf16[192,2,8,560]{3,2,1,0:T(8,128)(2,1)} reshape(bf16[1,192,2,4480]{3,2,1,0:T(2,128)(2,1)} %param.18) | data formatting | bytes 6881280 | tf_op jit(solution)/shard_map/reshape;squeeze | solution.py:1112
  44.2 5.1 copy.50
  50.0 17.5 %all-gather.1 = bf16[8,1,1536]{2,1,0:T(2,128)(2,1)S(1)} all-gather(bf16[1,1,1536]{2,1,0:T(2,128)(2,1)S(1)} %reshape.313), channel_id=2, replica_groups=mesh['section'=2,'tensor'=2,'ctx'=8] {'ctx'}, dimensions={0}, use_global_device_ids=true | all-gather | bytes 27648 | tf_op jit(solution)/shard_map/all_gather | solution.py:66
  75.2 106.0 %attend.2 = (f32[256,768]{1,0:T(8,128)S(1)}, bf16[256,768]{1,0:T(8,128)(2,1)S(1)}, f32[256,128]{1,0:T(8,128)S(1)}, bf16[2,1024,256]{2,1,0:T(8,128)(2,1)S(1)}, bf...) custom-call(f32[256,1024]{1,0:T(8,128)S(1)} %convolution_add_fusion.1.refs_0_, ...), custom_call_target="tpu_custom_call" | custom-call | flops 262144 | bytes 256 | tf_op jit(solution)/shard_map/attend/pallas_call | solution.py:871
  189.8 5.1 collective-permute-done.4
  199.1 4.0 broadcast_select_fusion
  203.1 128.5 %mlp_forward.2 = (bf16[2048,1536]{1,0:T(8,128)(2,1)}, f32[128,1536]{1,0:T(8,128)}, bf16[2048,560]{1,0:T(8,128)(2,1)}, bf16[2048,560]{1,0:T(8,128)(2,1)}, bf16[2048,560]{1,0:T(8,128)(2,1)}) custom-call(bf16[128,1536]{1,0:T(8,128)(2,1)} %multiply_convert_fusion.3.own_ref, bf16[2,2,1536,560]{3,2,1,0:T(8,128)(2,1)} %bitcast.113, ...), custom_call_target="tpu_custom_call" | custom-call | flops 3145728 | bytes 2048 | tf_op jit(solution)/shard_map/mlp_forward/pallas_call | solution.py:503
  335.6 7.6 collective-permute-done.5
  347.0 39.6 %attend.3 = (f32[256,768]{1,0:T(8,128)S(1)}, bf16[256,768]{1,0:T(8,128)(2,1)S(1)}, f32[256,128]{1,0:T(8,128)S(1)}, bf16[2,1024,256]{2,1,0:T(8,128)(2,1)S(1)}, bf16[256,768]{1,0:T(8,128)(2,1)S(1)}) custom-call(f32[256,1024]{1,0:T(8,128)S(1)} %convolution_add_fusion.refs_0_, f32[256,128]{1,0:T(8,128)S(1)} %get-tuple-element.161.refs_1_.cosine_ref, ...), custom_call_target="tpu_custom_call" | custom-call | flops 262144 | bytes 256 | tf_op jit(solution)/shard_map/attend/pallas_call | solution.py:871
  394.7 7.8 collective-permute-done.6
  404.5 56.6 %mlp_forward.3 = (bf16[2048,1536]{1,0:T(8,128)(2,1)}, bf16[2048,1536]{1,0:T(8,128)(2,1)}, bf16[2048,560]{1,0:T(8,128)(2,1)}, bf16[2048,560]{1,0:T(8,128)(2,1)}, bf16[2048,560]{1,0:T(8,128)(2,1)}) custom-call(bf16[128,1536]{1,0:T(8,128)(2,1)} %multiply_convert_fusion.2.own_ref, bf16[2,2,1536,560]{3,2,1,0:T(8,128)(2,1)} %bitcast.114, ...), custom_call_target="tpu_custom_call" | custom-call | flops 3145728 | bytes 2048 | tf_op jit(solution)/shard_map/mlp_forward/pallas_call | solution.py:503
  461.5 98.5 %mlp_backward.2 = (bf16[16,1536]{1,0:T(8,128)(2,1)}, f32[128,1536]{1,0:T(8,128)}, bf16[2,1536,560]{2,1,0:T(8,128)(2,1)}, bf16[560,1536]{1,0:T(8,128)(2,1)}) custom-call(bf16[2048,1536]{1,0:T(8,128)(2,1)} %all-gather.16.cloned.1.call-done.own_ref, bf16[2,2,1536,560]{3,2,1,0:T(8,128)(2,1)} %bitcast.115, bf16[560,1536]{1,0:T(8,128)(2,1)} %get-tuple-element.134.refs_1_, ...), custom_call_target="tpu_custom_call" | custom-call | flops 3145728 | bytes 2048 | tf_op jit(solution)/shard_map/mlp_backward/pallas_call | solution.py:503
  561.9 10.2 %reduce-scatter.6.cloned.1.call-done = bf16[128,1536]{1,0:T(8,128)(2,1)} async-done(((bf16[2048,1536]{1,0:T(8,128)(2,1)}), bf16[128,1536]{1,0:T(8,128)(2,1)}) %reduce-scatter.6.cloned.1.call-update) | async-done | bytes 393232 | tf_op jit(solution)/shard_map/reduce_scatter | solution.py:74
  575.5 4.7 collective-permute-start.8
  580.3 3.2 collective-permute-done.7
  584.8 23.7 %attend_backward.2 = bf16[256,1024]{1,0:T(8,128)(2,1)S(1)} custom-call(bf16[256,768]{1,0:T(8,128)(2,1)S(1)} %copy-done.15, bf16[2,1024,256]{2,1,0:T(8,128)(2,1)S(1)} %get-tuple-element.64.kv_ref, s32[2,128,1]{2,1,0:T(8,128)S(1)} %copy.34.refs_3_.qpos_ref, s32[2,1,1024]{2,1,0:T(1,128)S(1)} %bitcast.111, ...), custom_call_target="tpu_custom_call" | custom-call | flops 262144 | bytes 256 | tf_op jit(solution)/shard_map/attend_backward/pallas_call | solution.py:935
  609.6 5.0 collective-permute-done.8
  624.5 5.3 collective-permute-done.10
  630.2 4.1 fusion.2
  640.3 101.5 %mlp_backward.3 = (bf16[16,1536]{1,0:T(8,128)(2,1)}, f32[128,1536]{1,0:T(8,128)}, bf16[2,1536,560]{2,1,0:T(8,128)(2,1)}, bf16[560,1536]{1,0:T(8,128)(2,1)}) custom-call(bf16[128,1536]{1,0:T(8,128)(2,1)} %copy-done.28, bf16[2,2,1536,560]{3,2,1,0:T(8,128)(2,1)} %bitcast.116, bf16[560,1536]{1,0:T(8,128)(2,1)} %get-tuple-element.135.refs_1_, ...), custom_call_target="tpu_custom_call" | custom-call | flops 3145728 | bytes 2048 | tf_op jit(solution)/shard_map/mlp_backward/pallas_call | solution.py:503
  748.0 9.8 collective-permute-done.13
  764.4 37.7 %attend_backward.3 = bf16[256,1024]{1,0:T(8,128)(2,1)S(1)} custom-call(bf16[256,768]{1,0:T(8,128)(2,1)S(1)} %copy-done.13, bf16[2,1024,256]{2,1,0:T(8,128)(2,1)S(1)} %copy-done.7, s32[2,128,1]{2,1,0:T(8,128)S(1)} %copy.34.refs_3_.qpos_ref, s32[2,1,1024]{2,1,0:T(1,128)S(1)} %bitcast.112, bf16[256,768]{1,0:T(8,128)(2,1)S(1)} %convolution_convert_fusion.4.grad_ref, ...), custom_call_target="tpu_custom_call" | custom-call | flops 262144 | bytes 256 | tf_op jit(solution)/shard_map/attend_backward/pallas_call | solution.py:935
  807.7 3.9 convolution_convert_fusion.3
  814.6 4.1 fusion.3
  836.9 116.6 %collect.1 = bf16[2,8,192,560]{3,2,1,0:T(8,128)(2,1)S(1)} custom-call(bf16[2,8,192,560]{3,2,1,0:T(8,128)(2,1)S(1)} %bitcast.108, bf16[2,8,192,560]{3,2,1,0:T(8,128)(2,1)S(1)} %bitcast.107), custom_call_target="tpu_custom_call" | custom-call | flops 1720320 | bytes 1024 | tf_op jit(solution)/shard_map/collect/pallas_call | solution.py:230
  953.5 4.2 copy.41
  957.7 7.5 reshape.301
  965.2 8.4 copy.43
  977.8 7.1 collective-permute-done.21
  985.8 7.0 collective-permute-done.18
  (330 shorter events, 122.1 us)
Async XLA Ops:
  7.2 64.9 %all-gather.8.cloned.1.call-start = ((), (), s32[]{:S(2)}) async-start(), calls=%async_computation.5 | async-start | bytes 3538944 | tf_op jit(solution)/shard_map/all_gather | solution.py:66
  7.2 10.3 %collective-permute-start.1 = (bf16[192,1024]{1,0:T(8,128)(2,1)}, bf16[192,1024]{1,0:T(8,128)(2,1)S(1)}, u32[]{:S(2)}, u32[]{:S(2)}) collective-permute-start(bf16[192,1024]{1,0:T(8,128)(2,1)} %bitcast.130), channel_id=1, source_target_pairs={{0,16},{16,0},{1,17},{17,1},{2,18},{18,2},{3,19},{19,3},{4,20},{20... | collective-permute-start | bytes 1179656 | tf_op jit(solution)/shard_map/ppermute | solution.py:62
  19.5 165.1 %all-gather.10.cloned.1.call-start = ((), (), s32[]{:S(2)}) async-start(), calls=%async_computation.6 | async-start | bytes 2654208 | tf_op jit(solution)/shard_map/all_gather | solution.py:66
  19.5 7.2 collective-permute-start.3
  28.6 315.4 %all-gather.12.cloned.1.call-start = ((), (), s32[]{:S(2)}) async-start(), calls=%async_computation.7 | async-start | bytes 3538944 | tf_op jit(solution)/shard_map/all_gather | solution.py:66
  29.3 19.9 %collective-permute-start = (bf16[512]{0:T(512)(128)(2,1)}, bf16[512]{0:T(512)(128)(2,1)}, u32[]{:S(2)}, u32[]{:S(2)}) collective-permute-start(bf16[512]{0:T(512)(128)(2,1)} %pad_maximum_fusion.11), channel_id=1, source_target_pairs={{0,16},{16,0},{1,17},{17,1},{2,18},{18,2},{3,19},{19,3},{4,20},{20... | collective-permute-start | bytes 3080 | tf_op jit(solution)/shard_map/ppermute | solution.py:62
  30.5 44.6 %collective-permute-start.2 = (bf16[560,1536]{1,0:T(8,128)(2,1)}, bf16[560,1536]{1,0:T(8,128)(2,1)}, u32[]{:S(2)}, u32[]{:S(2)}) collective-permute-start(bf16[560,1536]{1,0:T(8,128)(2,1)} %bitcast.127), channel_id=1, source_target_pairs={{0,16},{16,0},{1,17},{17,1},{2,18},{18,2},{3,19},{19,3},{4,20},{20... | collective-permute-start | bytes 5160968 | tf_op jit(solution)/shard_map/ppermute | solution.py:62
  188.3 6.6 collective-permute-start.4
  198.3 190.0 %all-gather.14.cloned.1.call-start = ((), (), s32[]{:S(2)}) async-start(), calls=%async_computation.8 | async-start | bytes 2654208 | tf_op jit(solution)/shard_map/all_gather | solution.py:66
  198.9 262.6 %all-gather.16.cloned.1.call-start = ((), (), s32[]{:S(2)}) async-start(), calls=%async_computation.9 | async-start | bytes 7077888 | tf_op jit(solution)/shard_map/all_gather | solution.py:66
  333.1 10.1 %collective-permute-start.5 = (bf16[128,1536]{1,0:T(8,128)(2,1)S(1)}, bf16[128,1536]{1,0:T(8,128)(2,1)S(1)}, u32[]{:S(2)}, u32[]{:S(2)}) collective-permute-start(bf16[128,1536]{1,0:T(8,128)(2,1)S(1)} %add_convert_fusion.3), channel_id=1, source_target_pairs={{0,8},{8,0},{1,9},{9,1},{2,10},{10,2},{3,11},{11,3},{4,12},{12,4},... | collective-permute-start | bytes 1179656 | tf_op jit(solution)/shard_map/ppermute | solution.py:82
  343.4 228.7 %reduce-scatter.6.cloned.1.call-start = ((), (), s32[]{:S(2)}) async-start(), calls=%async_computation.10 | async-start | bytes 6684672 | tf_op jit(solution)/shard_map/reduce_scatter | solution.py:74
  391.9 10.6 %collective-permute-start.6 = (bf16[128,1536]{1,0:T(8,128)(2,1)S(1)}, bf16[128,1536]{1,0:T(8,128)(2,1)S(1)}, u32[]{:S(2)}, u32[]{:S(2)}) collective-permute-start(bf16[128,1536]{1,0:T(8,128)(2,1)S(1)} %dynamic-slice_convert_fusion.2), channel_id=1, source_target_pairs={{0,8},{8,0},{1,9},{9,1},{2,10},{10,2},{3,11},{11,3},{4,12},{12,4},... | collective-permute-start | bytes 1179656 | tf_op jit(solution)/shard_map/ppermute | solution.py:92
  461.2 285.4 %reduce-scatter.10.cloned.1.call-start = ((), (), s32[]{:S(2)}) async-start(), calls=%async_computation.12 | async-start | bytes 2654208 | tf_op jit(solution)/shard_map/reduce_scatter | solution.py:1149
  573.9 9.6 collective-permute-start.7
  575.5 39.1 %collective-permute-start.8 = (bf16[560,1536]{1,0:T(8,128)(2,1)}, bf16[560,1536]{1,0:T(8,128)(2,1)}, u32[]{:S(2)}, u32[]{:S(2)}) collective-permute-start(bf16[560,1536]{1,0:T(8,128)(2,1)} %get-tuple-element.75), channel_id=1, source_target_pairs={{0,16},{1,17},{2,18},{3,19},{4,20},{5,21},{6,22},{7,23},{8,24},{9,... | collective-permute-start | bytes 5160968 | tf_op jit(solution)/shard_map/ppermute | solution.py:1048
  580.2 28.3 %collective-permute-start.9 = (bf16[128,1536]{1,0:T(8,128)(2,1)S(1)}, bf16[128,1536]{1,0:T(8,128)(2,1)S(1)}, u32[]{:S(2)}, u32[]{:S(2)}) collective-permute-start(bf16[128,1536]{1,0:T(8,128)(2,1)S(1)} %get-tuple-element.148), channel_id=1, source_target_pairs={{0,8},{8,0},{1,9},{9,1},{2,10},{10,2},{3,11},{11,3},{4,12},{12,4},... | collective-permute-start | bytes 1179656 | tf_op jit(solution)/shard_map/ppermute | solution.py:82
  616.9 129.7 %reduce-scatter.8.cloned.1.call-start = ((), (), s32[]{:S(2)}) async-start(), calls=%async_computation.11 | async-start | bytes 3833856 | tf_op jit(solution)/shard_map/reduce_scatter | solution.py:1149
  621.1 8.6 collective-permute-start.10
  634.4 339.3 %reduce-scatter.14.cloned.1.call-start = ((), (), s32[]{:S(2)}) async-start(), calls=%async_computation.14 | async-start | bytes 2654208 | tf_op jit(solution)/shard_map/reduce_scatter | solution.py:1149
  637.0 104.9 %collective-permute-start.12 = (bf16[128,1536]{1,0:T(8,128)(2,1)S(1)}, bf16[128,1536]{1,0:T(8,128)(2,1)}, u32[]{:S(2)}, u32[]{:S(2)}) collective-permute-start(bf16[128,1536]{1,0:T(8,128)(2,1)S(1)} %add_convert_fusion.1.own_ref), channel_id=1, source_target_pairs={{0,8},{8,0},{1,9},{9,1},{2,10},{10,2},{3,11},{11,3},{4,12},{12,4},... | collective-permute-start | bytes 1179656 | tf_op jit(solution)/shard_map/ppermute | solution.py:82
  638.0 106.0 %collective-permute-start.11 = (bf16[256,1536]{1,0:T(8,128)(2,1)}, bf16[256,1536]{1,0:T(8,128)(2,1)}, u32[]{:S(2)}, u32[]{:S(2)}) collective-permute-start(bf16[256,1536]{1,0:T(8,128)(2,1)} %broadcast_select_fusion.8), channel_id=1, source_target_pairs={{0,16},{16,0},{1,17},{17,1},{2,18},{18,2},{3,19},{19,3},{4,20},{20... | collective-permute-start | bytes 2359304 | tf_op jit(solution)/shard_map/ppermute | solution.py:62
  747.9 9.9 collective-permute-start.13
  760.1 216.2 %reduce-scatter.12.cloned.1.call-start = ((), (), s32[]{:S(2)}) async-start(), calls=%async_computation.13 | async-start | bytes 3833856 | tf_op jit(solution)/shard_map/reduce_scatter | solution.py:1149
  760.2 41.9 %collective-permute-start.14 = (bf16[560,1536]{1,0:T(8,128)(2,1)}, bf16[560,1536]{1,0:T(8,128)(2,1)S(1)}, u32[]{:S(2)}, u32[]{:S(2)}) collective-permute-start(bf16[560,1536]{1,0:T(8,128)(2,1)} %get-tuple-element.91), channel_id=1, source_target_pairs={{16,0},{17,1},{18,2},{19,3},{20,4},{21,5},{22,6},{23,7},{24,8},{25... | collective-permute-start | bytes 5160968 | tf_op jit(solution)/shard_map/ppermute | solution.py:1048
  805.2 8.3 collective-permute-start.15
  821.9 8.4 collective-permute-start.16
  824.0 161.8 %collective-permute-start.19 = (bf16[208,1024]{1,0:T(8,128)(2,1)}, bf16[208,1024]{1,0:T(8,128)(2,1)}, u32[]{:S(2)}, u32[]{:S(2)}) collective-permute-start(bf16[208,1024]{1,0:T(8,128)(2,1)} %reduce-scatter.8.cloned.1.call-done), channel_id=1, source_target_pairs={{0,16},{1,17},{2,18},{3,19},{4,20},{5,21},{6,22},{7,23},{8,24},{9,... | collective-permute-start | bytes 1277960 | tf_op jit(solution)/shard_map/ppermute | solution.py:1185
  827.0 150.7 %collective-permute-start.22 = (bf16[96,1536]{1,0:T(8,128)(2,1)}, bf16[96,1536]{1,0:T(8,128)(2,1)}, u32[]{:S(2)}, u32[]{:S(2)}) collective-permute-start(bf16[96,1536]{1,0:T(8,128)(2,1)} %reduce-scatter.10.cloned.1.call-done), channel_id=1, source_target_pairs={{0,16},{1,17},{2,18},{3,19},{4,20},{5,21},{6,22},{7,23},{8,24},{9,... | collective-permute-start | bytes 884744 | tf_op jit(solution)/shard_map/ppermute | solution.py:1185
  830.5 144.4 %collective-permute-start.17 = (bf16[256,1536]{1,0:T(8,128)(2,1)S(1)}, bf16[256,1536]{1,0:T(8,128)(2,1)S(1)}, u32[]{:S(2)}, u32[]{:S(2)}) collective-permute-start(bf16[256,1536]{1,0:T(8,128)(2,1)S(1)} %broadcast_select_fusion.4), channel_id=1, source_target_pairs={{0,16},{16,0},{1,17},{17,1},{2,18},{18,2},{3,19},{19,3},{4,20},{20... | collective-permute-start | bytes 2359304 | tf_op jit(solution)/shard_map/ppermute | solution.py:62
  973.6 11.2 %collective-permute-start.21 = (bf16[96,1536]{1,0:T(8,128)(2,1)}, bf16[96,1536]{1,0:T(8,128)(2,1)S(1)}, u32[]{:S(2)}, u32[]{:S(2)}) collective-permute-start(bf16[96,1536]{1,0:T(8,128)(2,1)} %reduce-scatter.14.cloned.1.call-done), channel_id=1, source_target_pairs={{16,0},{17,1},{18,2},{19,3},{20,4},{21,5},{22,6},{23,7},{24,8},{25... | collective-permute-start | bytes 884744 | tf_op jit(solution)/shard_map/ppermute | solution.py:1184
  976.3 16.4 %collective-permute-start.18 = (bf16[208,1024]{1,0:T(8,128)(2,1)}, bf16[208,1024]{1,0:T(8,128)(2,1)S(1)}, u32[]{:S(2)}, u32[]{:S(2)}) collective-permute-start(bf16[208,1024]{1,0:T(8,128)(2,1)} %reduce-scatter.12.cloned.1.call-done), channel_id=1, source_target_pairs={{16,0},{17,1},{18,2},{19,3},{20,4},{21,5},{22,6},{23,7},{24,8},{25... | collective-permute-start | bytes 1277960 | tf_op jit(solution)/shard_map/ppermute | solution.py:1184
  (78 other events, 935.1 us)
Sparse Core Ops, SparseCore 0:
  19.6 39.7 all-gather.7
  61.6 41.9 all-gather.9
  198.5 63.3 all-gather.11
  263.9 36.2 all-gather.13
  343.5 75.9 all-gather.15
  461.3 110.6 reduce-scatter.5
  617.0 32.8 reduce-scatter.9
  652.9 60.4 reduce-scatter.7
  760.2 52.9 reduce-scatter.13
  818.8 51.3 reduce-scatter.11

commit v6 on v5

--- a/solution.py
+++ b/solution.py
@@ -240,6 +240,56 @@
         cost_estimate=pl.CostEstimate(flops=first.size, bytes_accessed=1024, transcendentals=0),
         name="collect",
     )(first, second)
+
+
+def join_kernel(blocks_ref, out_ref):
+    parts, size = blocks_ref.shape[:2]
+    for part in range(parts):
+        pieces = [blocks_ref[part, index].astype(F32) for index in range(size)]
+        out_ref[:, part, :] = jnp.concatenate(pieces, axis=1)
+
+
+def join(blocks):
+    parts, size, rows, columns = blocks.shape
+    if size != 8:
+        joined = jnp.transpose(blocks, (2, 0, 1, 3))
+        return joined.reshape(rows, parts, size * columns).astype(F32)
+    tile = 32
+    return pl.pallas_call(
+        join_kernel,
+        grid=(rows // tile,),
+        out_shape=jax.ShapeDtypeStruct((rows, parts, size * columns), F32),
+        in_specs=[pl.BlockSpec((parts, size, tile, columns), lambda index: (0, 0, index, 0))],
+        out_specs=pl.BlockSpec((tile, parts, size * columns), lambda index: (index, 0, 0)),
+        compiler_params=pltpu.CompilerParams(vmem_limit_bytes=32 << 20),
+        name="join",
+    )(blocks)
+
+
+def cut_kernel(rows_ref, out_ref):
+    parts, size = out_ref.shape[:2]
+    columns = out_ref.shape[3]
+    for part in range(parts):
+        values = rows_ref[:, part, :]
+        for index in range(size):
+            out_ref[part, index] = values[:, index * columns : (index + 1) * columns]
+
+
+def cut(values, size):
+    rows, parts, columns = values.shape
+    columns //= size
+    if size != 8:
+        return jnp.transpose(values.reshape(rows, parts, size, columns), (1, 2, 0, 3))
+    tile = 32
+    return pl.pallas_call(
+        cut_kernel,
+        grid=(rows // tile,),
+        out_shape=jax.ShapeDtypeStruct((parts, size, rows, columns), values.dtype),
+        in_specs=[pl.BlockSpec((tile, parts, size * columns), lambda index: (index, 0, 0))],
+        out_specs=pl.BlockSpec((parts, size, tile, columns), lambda index: (0, 0, index, 0)),
+        compiler_params=pltpu.CompilerParams(vmem_limit_bytes=32 << 20),
+        name="cut",
+    )(values)
 
 
 def remote(src, dst, send, recv, device):
@@ -1109,8 +1159,7 @@
     out0, out1 = layers(out, swap(out))
     down_moved = swap(w_down[0])
     down0, down1 = layers(w_down[0], down_moved)
-    expand = w_gate_up[0].reshape(slice_width, 2, ctx_size, units)
-    blocks = jnp.transpose(expand, (1, 2, 0, 3))
+    blocks = cut(w_gate_up[0], ctx_size)
 
     def whole(small, qkv, out, expand, down):
         return (
@@ -1195,9 +1244,7 @@
     grad0_all, d_expand0 = lax.optimization_barrier((grad0_all, d_expand0))
     input_grad = exchange(grad0_all, grad1_all)
     total = collect(d_expand0.reshape(blocks), d_expand1.reshape(blocks), first)
-    d_expand = lax.optimization_barrier(jnp.transpose(total, (2, 0, 1, 3)))
-    d_expand = lax.optimization_barrier(d_expand.reshape(1, slice_width, 2, ctx_size * units))
-    d_expand = d_expand.astype(F32)
+    d_expand = join(total)[None]
     d_reduce = of_owner(d_reduce0, d_reduce1)
 
     d_mixed = to_owner(ctx_scatter(with_vectors(d0)), slices1[0])

time: 1010 us -> 998 us (0.988)
  local copies, waits for them, and re-layouts: 63 us -> 31 us
  Pallas kernels: 709 us -> 726 us
    pallas_call x0 -> x2, Pallas kernels: none -> 16.5 us  [the longest x1 11.8 us: cut(): pl.pallas_call(cut_kernel, grid=(rows // tile,), out_shape=jax.ShapeDtype...]
    another operation x3 -> x1, local copies, waits for them, and re-layouts: 16.4 us -> 0.08 us  [the longest x2 16.3 us: shards(): expand = w_gate_up[0].reshape(slice_width, 2, ctx_size, units)]
    unnamed x159 -> x162, local copies, waits for them, and re-layouts: 27 us -> 23 us
  transfers between devices with their start and end apart: 33 -> 33, of which waited for: 14 -> 14; matrix products, arithmetic and copies ran while one was open for 11% -> 8% of each run, Pallas kernels for 71% -> 73%
where the time goes in v6:
time: 998 us; the launch traced here: 989 us
  Pallas kernels  726 us (73%)
  waiting for transfers between devices  86.7 us (9%)
  other arithmetic  51.6 us (5%)
  local copies, waits for them, and re-layouts  31 us (3%)
  starting transfers between devices  30.8 us (3%)
  matrix products  29.5 us (3%)
  blocking collectives  17.1 us (2%)
  between operations  15.8 us (2%)
    pallas_call x4, Pallas kernels, spread(): pl.pallas_call(functools.partial(spread_kernel, chunk, piece, layer, plan...  385 us
    pallas_call x2, Pallas kernels, attend(): pl.pallas_call(functools.partial(attend_kernel, planes, heads, len(blocks...  146 us
    pallas_call x1, Pallas kernels, collect(): pl.pallas_call(functools.partial(collect_kernel, size), out_shape=jax.Sha...  117 us
    pallas_call x2, Pallas kernels, attend_backward(): pl.pallas_call(functools.partial(attend_back_kernel, planes, heads), out_...  61.2 us
    dot_general x12, matrix products, dot(): return lax.dot_general(a, b, dims, preferred_element_type=F32)  29.5 us
    unnamed x162, local copies, waits for them, and re-layouts  23 us
    ppermute x6, waiting for transfers between devices, tensor_pair(): received = lax.ppermute(rows, 'tensor', SWAP)  21.3 us
    ppermute x4, waiting for transfers between devices, tensor_scatter(): return own + lax.ppermute(other.astype(BF16), 'tensor', SWAP).astype(F32)  20.8 us
  transfers between devices with their start and end apart: 33, of which 14 were waited for; matrix products, arithmetic and copies ran while one was open for 8% of the time, Pallas kernels for 73%

profile of v6, /device:TPU:9, one launch (start us, length us, event | category | flops | bytes accessed | tf_op | source)
XLA Modules:
  0.0 988.7 jit_solution(16820059422644846722)
XLA Ops:
  8.5 9.0 collective-permute-done.1
  20.8 6.0 collective-permute-done.3
  35.3 11.8 %cut.1.refs_5_ = bf16[2,8,192,560]{3,2,1,0:T(8,128)(2,1)S(1)} custom-call(bf16[192,2,4480]{2,1,0:T(2,128)(2,1)S(1)} %bitcast.102), custom_call_target="tpu_custom_call" | custom-call | tf_op jit(solution)/shard_map/cut/pallas_call | solution.py:284
  49.9 17.1 %all-gather.1 = bf16[8,1,1536]{2,1,0:T(2,128)(2,1)S(1)} all-gather(bf16[1,1,1536]{2,1,0:T(2,128)(2,1)S(1)} %reshape.309), channel_id=2, replica_groups=mesh['section'=2,'tensor'=2,'ctx'=8] {'ctx'}, dimensions={0}, use_global_device_ids=true | all-gather | bytes 27648 | tf_op jit(solution)/shard_map/all_gather | solution.py:66
  71.5 3.1 convolution_add_fusion.1.refs_0_
  74.6 106.7 %attend.2 = (f32[256,768]{1,0:T(8,128)S(1)}, bf16[256,768]{1,0:T(8,128)(2,1)S(1)}, f32[256,128]{1,0:T(8,128)S(1)}, bf16[2,1024,256]{2,1,0:T(8,128)(2,1)S(1)}, bf...) custom-call(f32[256,1024]{1,0:T(8,128)S(1)} %convolution_add_fusion.1.refs_0_, ...), custom_call_target="tpu_custom_call" | custom-call | flops 262144 | bytes 256 | tf_op jit(solution)/shard_map/attend/pallas_call | solution.py:921
  189.8 5.1 collective-permute-done.4
  199.2 4.0 broadcast_select_fusion
  203.2 128.5 %mlp_forward.2 = (bf16[2048,1536]{1,0:T(8,128)(2,1)}, f32[128,1536]{1,0:T(8,128)}, bf16[2048,560]{1,0:T(8,128)(2,1)}, bf16[2048,560]{1,0:T(8,128)(2,1)}, bf16[2048,560]{1,0:T(8,128)(2,1)}) custom-call(bf16[128,1536]{1,0:T(8,128)(2,1)} %multiply_convert_fusion.3.own_ref, bf16[2,2,1536,560]{3,2,1,0:T(8,128)(2,1)} %bitcast.107, ...), custom_call_target="tpu_custom_call" | custom-call | flops 3145728 | bytes 2048 | tf_op jit(solution)/shard_map/mlp_forward/pallas_call | solution.py:553
  335.7 7.5 collective-permute-done.5
  346.9 39.7 %attend.3 = (f32[256,768]{1,0:T(8,128)S(1)}, bf16[256,768]{1,0:T(8,128)(2,1)S(1)}, f32[256,128]{1,0:T(8,128)S(1)}, bf16[2,1024,256]{2,1,0:T(8,128)(2,1)S(1)}, bf16[256,768]{1,0:T(8,128)(2,1)S(1)}) custom-call(f32[256,1024]{1,0:T(8,128)S(1)} %convolution_add_fusion.refs_0_, f32[256,128]{1,0:T(8,128)S(1)} %get-tuple-element.151.refs_1_.cosine_ref, ...), custom_call_target="tpu_custom_call" | custom-call | flops 262144 | bytes 256 | tf_op jit(solution)/shard_map/attend/pallas_call | solution.py:921
  394.6 7.8 collective-permute-done.6
  404.4 56.7 %mlp_forward.3 = (bf16[2048,1536]{1,0:T(8,128)(2,1)}, bf16[2048,1536]{1,0:T(8,128)(2,1)}, bf16[2048,560]{1,0:T(8,128)(2,1)}, bf16[2048,560]{1,0:T(8,128)(2,1)}, bf16[2048,560]{1,0:T(8,128)(2,1)}) custom-call(bf16[128,1536]{1,0:T(8,128)(2,1)} %multiply_convert_fusion.2.own_ref, bf16[2,2,1536,560]{3,2,1,0:T(8,128)(2,1)} %bitcast.108, ...), custom_call_target="tpu_custom_call" | custom-call | flops 3145728 | bytes 2048 | tf_op jit(solution)/shard_map/mlp_forward/pallas_call | solution.py:553
  461.6 98.6 %mlp_backward.2 = (bf16[16,1536]{1,0:T(8,128)(2,1)}, f32[128,1536]{1,0:T(8,128)}, bf16[2,1536,560]{2,1,0:T(8,128)(2,1)}, bf16[560,1536]{1,0:T(8,128)(2,1)}) custom-call(bf16[2048,1536]{1,0:T(8,128)(2,1)} %all-gather.16.cloned.1.call-done.own_ref, bf16[2,2,1536,560]{3,2,1,0:T(8,128)(2,1)} %bitcast.109, bf16[560,1536]{1,0:T(8,128)(2,1)} %get-tuple-element.124.refs_1_, ...), custom_call_target="tpu_custom_call" | custom-call | flops 3145728 | bytes 2048 | tf_op jit(solution)/shard_map/mlp_backward/pallas_call | solution.py:553
  562.0 10.1 %reduce-scatter.6.cloned.1.call-done = bf16[128,1536]{1,0:T(8,128)(2,1)} async-done(((bf16[2048,1536]{1,0:T(8,128)(2,1)}), bf16[128,1536]{1,0:T(8,128)(2,1)}) %reduce-scatter.6.cloned.1.call-update) | async-done | bytes 393232 | tf_op jit(solution)/shard_map/reduce_scatter | solution.py:74
  575.5 4.4 collective-permute-start.8
  580.1 3.5 collective-permute-done.7
  584.8 23.6 %attend_backward.2 = bf16[256,1024]{1,0:T(8,128)(2,1)S(1)} custom-call(bf16[256,768]{1,0:T(8,128)(2,1)S(1)} %copy-done.17, bf16[2,1024,256]{2,1,0:T(8,128)(2,1)S(1)} %get-tuple-element.64.kv_ref, s32[2,128,1]{2,1,0:T(8,128)S(1)} %copy.28.refs_3_.qpos_ref, s32[2,1,1024]{2,1,0:T(1,128)S(1)} %bitcast.105, ...), custom_call_target="tpu_custom_call" | custom-call | flops 262144 | bytes 256 | tf_op jit(solution)/shard_map/attend_backward/pallas_call | solution.py:985
  609.5 5.2 collective-permute-done.8
  617.0 3.0 fusion.19
  624.5 5.4 collective-permute-done.10
  630.4 4.1 fusion.2
  640.4 101.4 %mlp_backward.3 = (bf16[16,1536]{1,0:T(8,128)(2,1)}, f32[128,1536]{1,0:T(8,128)}, bf16[2,1536,560]{2,1,0:T(8,128)(2,1)}, bf16[560,1536]{1,0:T(8,128)(2,1)}) custom-call(bf16[128,1536]{1,0:T(8,128)(2,1)} %copy-done.30, bf16[2,2,1536,560]{3,2,1,0:T(8,128)(2,1)} %bitcast.110, bf16[560,1536]{1,0:T(8,128)(2,1)} %get-tuple-element.125.refs_1_, ...), custom_call_target="tpu_custom_call" | custom-call | flops 3145728 | bytes 2048 | tf_op jit(solution)/shard_map/mlp_backward/pallas_call | solution.py:553
  748.0 9.8 collective-permute-done.13
  764.5 37.6 %attend_backward.3 = bf16[256,1024]{1,0:T(8,128)(2,1)S(1)} custom-call(bf16[256,768]{1,0:T(8,128)(2,1)S(1)} %copy-done.15, bf16[2,1024,256]{2,1,0:T(8,128)(2,1)S(1)} %copy-done.9, s32[2,128,1]{2,1,0:T(8,128)S(1)} %copy.28.refs_3_.qpos_ref, s32[2,1,1024]{2,1,0:T(1,128)S(1)} %bitcast.106, bf16[256,768]{1,0:T(8,128)(2,1)S(1)} %convolution_convert_fusion.4.grad_ref, ...), custom_call_target="tpu_custom_call" | custom-call | flops 262144 | bytes 256 | tf_op jit(solution)/shard_map/attend_backward/pallas_call | solution.py:985
  807.4 3.9 convolution_convert_fusion.3
  814.8 4.1 fusion.3
  823.5 3.5 collective-permute-start.19
  836.2 117.0 %collect.1.blocks_ref = bf16[2,8,192,560]{3,2,1,0:T(8,128)(2,1)S(1)} custom-call(bf16[2,8,192,560]{3,2,1,0:T(8,128)(2,1)S(1)} %bitcast.101, bf16[2,8,192,560]{3,2,1,0:T(8,128)(2,1)S(1)} %bitcast.100), custom_call_target="tpu_custom_call" | custom-call | flops 1720320 | bytes 1024 | tf_op jit(solution)/shard_map/collect/pallas_call | solution.py:230
  953.1 4.7 join.1
  962.0 7.1 collective-permute-done.21
  970.0 6.6 collective-permute-done.18
  (331 shorter events, 116.5 us)
Async XLA Ops:
  7.2 64.3 %all-gather.8.cloned.1.call-start = ((), (), s32[]{:S(2)}) async-start(), calls=%async_computation.5 | async-start | bytes 3538944 | tf_op jit(solution)/shard_map/all_gather | solution.py:66
  7.2 10.3 %collective-permute-start.1 = (bf16[192,1024]{1,0:T(8,128)(2,1)}, bf16[192,1024]{1,0:T(8,128)(2,1)S(1)}, u32[]{:S(2)}, u32[]{:S(2)}) collective-permute-start(bf16[192,1024]{1,0:T(8,128)(2,1)} %bitcast.124), channel_id=1, source_target_pairs={{0,16},{16,0},{1,17},{17,1},{2,18},{18,2},{3,19},{19,3},{4,20},{20... | collective-permute-start | bytes 1179656 | tf_op jit(solution)/shard_map/ppermute | solution.py:62
  19.5 165.1 %all-gather.10.cloned.1.call-start = ((), (), s32[]{:S(2)}) async-start(), calls=%async_computation.6 | async-start | bytes 2654208 | tf_op jit(solution)/shard_map/all_gather | solution.py:66
  19.5 7.2 collective-permute-start.3
  28.6 315.2 %all-gather.12.cloned.1.call-start = ((), (), s32[]{:S(2)}) async-start(), calls=%async_computation.7 | async-start | bytes 3538944 | tf_op jit(solution)/shard_map/all_gather | solution.py:66
  29.3 19.7 %collective-permute-start = (bf16[512]{0:T(512)(128)(2,1)}, bf16[512]{0:T(512)(128)(2,1)}, u32[]{:S(2)}, u32[]{:S(2)}) collective-permute-start(bf16[512]{0:T(512)(128)(2,1)} %pad_maximum_fusion.11), channel_id=1, source_target_pairs={{0,16},{16,0},{1,17},{17,1},{2,18},{18,2},{3,19},{19,3},{4,20},{20... | collective-permute-start | bytes 3080 | tf_op jit(solution)/shard_map/ppermute | solution.py:62
  30.5 44.0 %collective-permute-start.2 = (bf16[560,1536]{1,0:T(8,128)(2,1)}, bf16[560,1536]{1,0:T(8,128)(2,1)}, u32[]{:S(2)}, u32[]{:S(2)}) collective-permute-start(bf16[560,1536]{1,0:T(8,128)(2,1)} %bitcast.121), channel_id=1, source_target_pairs={{0,16},{16,0},{1,17},{17,1},{2,18},{18,2},{3,19},{19,3},{4,20},{20... | collective-permute-start | bytes 5160968 | tf_op jit(solution)/shard_map/ppermute | solution.py:62
  188.3 6.6 collective-permute-start.4
  198.4 189.8 %all-gather.14.cloned.1.call-start = ((), (), s32[]{:S(2)}) async-start(), calls=%async_computation.8 | async-start | bytes 2654208 | tf_op jit(solution)/shard_map/all_gather | solution.py:66
  198.9 262.6 %all-gather.16.cloned.1.call-start = ((), (), s32[]{:S(2)}) async-start(), calls=%async_computation.9 | async-start | bytes 7077888 | tf_op jit(solution)/shard_map/all_gather | solution.py:66
  333.2 10.0 %collective-permute-start.5 = (bf16[128,1536]{1,0:T(8,128)(2,1)S(1)}, bf16[128,1536]{1,0:T(8,128)(2,1)S(1)}, u32[]{:S(2)}, u32[]{:S(2)}) collective-permute-start(bf16[128,1536]{1,0:T(8,128)(2,1)S(1)} %add_convert_fusion.3), channel_id=1, source_target_pairs={{0,8},{8,0},{1,9},{9,1},{2,10},{10,2},{3,11},{11,3},{4,12},{12,4},... | collective-permute-start | bytes 1179656 | tf_op jit(solution)/shard_map/ppermute | solution.py:82
  343.4 228.7 %reduce-scatter.6.cloned.1.call-start = ((), (), s32[]{:S(2)}) async-start(), calls=%async_computation.10 | async-start | bytes 6684672 | tf_op jit(solution)/shard_map/reduce_scatter | solution.py:74
  391.9 10.6 %collective-permute-start.6 = (bf16[128,1536]{1,0:T(8,128)(2,1)S(1)}, bf16[128,1536]{1,0:T(8,128)(2,1)S(1)}, u32[]{:S(2)}, u32[]{:S(2)}) collective-permute-start(bf16[128,1536]{1,0:T(8,128)(2,1)S(1)} %dynamic-slice_convert_fusion.2), channel_id=1, source_target_pairs={{0,8},{8,0},{1,9},{9,1},{2,10},{10,2},{3,11},{11,3},{4,12},{12,4},... | collective-permute-start | bytes 1179656 | tf_op jit(solution)/shard_map/ppermute | solution.py:92
  461.1 285.6 %reduce-scatter.10.cloned.1.call-start = ((), (), s32[]{:S(2)}) async-start(), calls=%async_computation.12 | async-start | bytes 2654208 | tf_op jit(solution)/shard_map/reduce_scatter | solution.py:1198
  573.9 9.6 collective-permute-start.7
  575.5 39.1 %collective-permute-start.8 = (bf16[560,1536]{1,0:T(8,128)(2,1)}, bf16[560,1536]{1,0:T(8,128)(2,1)}, u32[]{:S(2)}, u32[]{:S(2)}) collective-permute-start(bf16[560,1536]{1,0:T(8,128)(2,1)} %get-tuple-element.75), channel_id=1, source_target_pairs={{0,16},{1,17},{2,18},{3,19},{4,20},{5,21},{6,22},{7,23},{8,24},{9,... | collective-permute-start | bytes 5160968 | tf_op jit(solution)/shard_map/ppermute | solution.py:1098
  580.0 28.5 %collective-permute-start.9 = (bf16[128,1536]{1,0:T(8,128)(2,1)S(1)}, bf16[128,1536]{1,0:T(8,128)(2,1)S(1)}, u32[]{:S(2)}, u32[]{:S(2)}) collective-permute-start(bf16[128,1536]{1,0:T(8,128)(2,1)S(1)} %get-tuple-element.138), channel_id=1, source_target_pairs={{0,8},{8,0},{1,9},{9,1},{2,10},{10,2},{3,11},{11,3},{4,12},{12,4},... | collective-permute-start | bytes 1179656 | tf_op jit(solution)/shard_map/ppermute | solution.py:82
  616.9 129.8 %reduce-scatter.8.cloned.1.call-start = ((), (), s32[]{:S(2)}) async-start(), calls=%async_computation.11 | async-start | bytes 3833856 | tf_op jit(solution)/shard_map/reduce_scatter | solution.py:1198
  621.2 8.8 collective-permute-start.10
  634.6 323.2 %reduce-scatter.14.cloned.1.call-start = ((), (), s32[]{:S(2)}) async-start(), calls=%async_computation.14 | async-start | bytes 2654208 | tf_op jit(solution)/shard_map/reduce_scatter | solution.py:1198
  637.2 104.7 %collective-permute-start.12 = (bf16[128,1536]{1,0:T(8,128)(2,1)S(1)}, bf16[128,1536]{1,0:T(8,128)(2,1)}, u32[]{:S(2)}, u32[]{:S(2)}) collective-permute-start(bf16[128,1536]{1,0:T(8,128)(2,1)S(1)} %add_convert_fusion.1.own_ref), channel_id=1, source_target_pairs={{0,8},{8,0},{1,9},{9,1},{2,10},{10,2},{3,11},{11,3},{4,12},{12,4},... | collective-permute-start | bytes 1179656 | tf_op jit(solution)/shard_map/ppermute | solution.py:82
  638.2 105.8 %collective-permute-start.11 = (bf16[256,1536]{1,0:T(8,128)(2,1)}, bf16[256,1536]{1,0:T(8,128)(2,1)}, u32[]{:S(2)}, u32[]{:S(2)}) collective-permute-start(bf16[256,1536]{1,0:T(8,128)(2,1)} %broadcast_select_fusion.8), channel_id=1, source_target_pairs={{0,16},{16,0},{1,17},{17,1},{2,18},{18,2},{3,19},{19,3},{4,20},{20... | collective-permute-start | bytes 2359304 | tf_op jit(solution)/shard_map/ppermute | solution.py:62
  748.0 9.9 collective-permute-start.13
  760.2 200.3 %reduce-scatter.12.cloned.1.call-start = ((), (), s32[]{:S(2)}) async-start(), calls=%async_computation.13 | async-start | bytes 3833856 | tf_op jit(solution)/shard_map/reduce_scatter | solution.py:1198
  760.3 41.9 %collective-permute-start.14 = (bf16[560,1536]{1,0:T(8,128)(2,1)}, bf16[560,1536]{1,0:T(8,128)(2,1)S(1)}, u32[]{:S(2)}, u32[]{:S(2)}) collective-permute-start(bf16[560,1536]{1,0:T(8,128)(2,1)} %get-tuple-element.91), channel_id=1, source_target_pairs={{16,0},{17,1},{18,2},{19,3},{20,4},{21,5},{22,6},{23,7},{24,8},{25... | collective-permute-start | bytes 5160968 | tf_op jit(solution)/shard_map/ppermute | solution.py:1098
  805.3 8.5 collective-permute-start.15
  822.1 7.4 collective-permute-start.16
  823.5 146.6 %collective-permute-start.19 = (bf16[208,1024]{1,0:T(8,128)(2,1)}, bf16[208,1024]{1,0:T(8,128)(2,1)}, u32[]{:S(2)}, u32[]{:S(2)}) collective-permute-start(bf16[208,1024]{1,0:T(8,128)(2,1)} %reduce-scatter.8.cloned.1.call-done), channel_id=1, source_target_pairs={{0,16},{1,17},{2,18},{3,19},{4,20},{5,21},{6,22},{7,23},{8,24},{9,... | collective-permute-start | bytes 1277960 | tf_op jit(solution)/shard_map/ppermute | solution.py:1234
  827.0 135.0 %collective-permute-start.22 = (bf16[96,1536]{1,0:T(8,128)(2,1)}, bf16[96,1536]{1,0:T(8,128)(2,1)}, u32[]{:S(2)}, u32[]{:S(2)}) collective-permute-start(bf16[96,1536]{1,0:T(8,128)(2,1)} %reduce-scatter.10.cloned.1.call-done), channel_id=1, source_target_pairs={{0,16},{1,17},{2,18},{3,19},{4,20},{5,21},{6,22},{7,23},{8,24},{9,... | collective-permute-start | bytes 884744 | tf_op jit(solution)/shard_map/ppermute | solution.py:1234
  829.8 129.4 %collective-permute-start.17 = (bf16[256,1536]{1,0:T(8,128)(2,1)S(1)}, bf16[256,1536]{1,0:T(8,128)(2,1)S(1)}, u32[]{:S(2)}, u32[]{:S(2)}) collective-permute-start(bf16[256,1536]{1,0:T(8,128)(2,1)S(1)} %broadcast_select_fusion.4), channel_id=1, source_target_pairs={{0,16},{16,0},{1,17},{17,1},{2,18},{18,2},{3,19},{19,3},{4,20},{20... | collective-permute-start | bytes 2359304 | tf_op jit(solution)/shard_map/ppermute | solution.py:62
  957.8 11.3 %collective-permute-start.21 = (bf16[96,1536]{1,0:T(8,128)(2,1)}, bf16[96,1536]{1,0:T(8,128)(2,1)S(1)}, u32[]{:S(2)}, u32[]{:S(2)}) collective-permute-start(bf16[96,1536]{1,0:T(8,128)(2,1)} %reduce-scatter.14.cloned.1.call-done), channel_id=1, source_target_pairs={{16,0},{17,1},{18,2},{19,3},{20,4},{21,5},{22,6},{23,7},{24,8},{25... | collective-permute-start | bytes 884744 | tf_op jit(solution)/shard_map/ppermute | solution.py:1233
  960.5 16.2 %collective-permute-start.18 = (bf16[208,1024]{1,0:T(8,128)(2,1)}, bf16[208,1024]{1,0:T(8,128)(2,1)S(1)}, u32[]{:S(2)}, u32[]{:S(2)}) collective-permute-start(bf16[208,1024]{1,0:T(8,128)(2,1)} %reduce-scatter.12.cloned.1.call-done), channel_id=1, source_target_pairs={{16,0},{17,1},{18,2},{19,3},{20,4},{21,5},{22,6},{23,7},{24,8},{25... | collective-permute-start | bytes 1277960 | tf_op jit(solution)/shard_map/ppermute | solution.py:1233
  (80 other events, 952.5 us)
Sparse Core Ops, SparseCore 0:
  19.6 39.8 all-gather.7
  61.6 42.4 all-gather.9
  198.5 63.3 all-gather.11
  263.9 36.2 all-gather.13
  343.5 75.9 all-gather.15
  461.2 110.7 reduce-scatter.5
  617.0 32.9 reduce-scatter.9
  653.0 59.4 reduce-scatter.7
  760.3 52.7 reduce-scatter.13
  819.1 51.0 reduce-scatter.11

commit v7 on v6

--- a/solution.py
+++ b/solution.py
@@ -1095,6 +1095,8 @@
         hidden,
     )
     grad_normed_mlp, earlier = lax.optimization_barrier((grad_normed_mlp, earlier))
+    if earlier:
+        pinned = tuple(lax.ppermute(part, "section", SWAP[:1]) for part in earlier[:2])
     moved_reduce = lax.ppermute(d_reduce, "section", route)
     grad_middle, d_gain_mlp = norm_backward(middle, root_mlp, gain_mlp, grad_normed_mlp)
     grad_middle = grad_middle + grad_out
@@ -1224,14 +1226,13 @@
     section_output = exchange(x1, out1_all)
     slices1 = (ctx_scatter(with_vectors(d1)), ctx_scatter(d1[3]))
     grad1_all = tensor_pair(grad1)
-    grad0, d0, d_expand0, d_reduce0, earlier, _ = layer_backward(
+    grad0, d0, d_expand0, d_reduce0, earlier, moved1 = layer_backward(
         grad1.astype(F32), grad1, kept0, weights0, tables, [(1, 0)], slices1 + (section_output, grad1_all), ()
     )
     slices1, (section_output, grad1_all) = earlier[:2], earlier[2:]
 
-    def to_owner(part0, part1):
+    def to_owner(part0, part1, received1):
         received0 = lax.ppermute(part0.astype(BF16), "section", [(1, 0)])
-        received1 = lax.ppermute(part1.astype(BF16), "section", [(0, 1)])
         own = jnp.where(first, part0, part1).astype(F32)
         return own + jnp.where(first, received0, received1).astype(F32)
 
@@ -1247,8 +1248,8 @@
     d_expand = join(total)[None]
     d_reduce = of_owner(d_reduce0, d_reduce1)
 
-    d_mixed = to_owner(ctx_scatter(with_vectors(d0)), slices1[0])
-    d_project = to_owner(ctx_scatter(d0[3]), slices1[1])
+    d_mixed = to_owner(ctx_scatter(with_vectors(d0)), slices1[0], moved1[0])
+    d_project = to_owner(ctx_scatter(d0[3]), slices1[1], moved1[1])
     vectors = d_mixed[slice_width]
     d_mixed = d_mixed[:slice_width]
     count_qk, count_v = split_at // ctx_size, head_dim // ctx_size

time: 998 us -> 999 us (level)
    unnamed x162 -> x178, local copies, waits for them, and re-layouts: 23 us -> 22.2 us
where the time goes in v7:
time: 999 us; the launch traced here: 990 us
  Pallas kernels  722 us (72%)
  waiting for transfers between devices  92.2 us (9%)
  other arithmetic  51.5 us (5%)
  starting transfers between devices  31.8 us (3%)
  local copies, waits for them, and re-layouts  30.3 us (3%)
  matrix products  29.5 us (3%)
  blocking collectives  17.1 us (2%)
  between operations  15.9 us (2%)
    pallas_call x4, Pallas kernels, spread(): pl.pallas_call(functools.partial(spread_kernel, chunk, piece, layer, plan...  385 us
    pallas_call x2, Pallas kernels, attend(): pl.pallas_call(functools.partial(attend_kernel, planes, heads, len(blocks...  146 us
    pallas_call x1, Pallas kernels, collect(): pl.pallas_call(functools.partial(collect_kernel, size), out_shape=jax.Sha...  111 us
    pallas_call x2, Pallas kernels, attend_backward(): pl.pallas_call(functools.partial(attend_back_kernel, planes, heads), out_...  61.9 us
    dot_general x12, matrix products, dot(): return lax.dot_general(a, b, dims, preferred_element_type=F32)  29.5 us
    ppermute x6, waiting for transfers between devices, tensor_pair(): received = lax.ppermute(rows, 'tensor', SWAP)  27 us
    unnamed x178, local copies, waits for them, and re-layouts  22.2 us
    ppermute x4, waiting for transfers between devices, tensor_scatter(): return own + lax.ppermute(other.astype(BF16), 'tensor', SWAP).astype(F32)  20.5 us
  transfers between devices with their start and end apart: 33, of which 14 were waited for; matrix products, arithmetic and copies ran while one was open for 8% of the time, Pallas kernels for 73%

profile of v7, /device:TPU:9, one launch (start us, length us, event | category | flops | bytes accessed | tf_op | source)
XLA Modules:
  0.0 989.8 jit_solution(14977872613002147476)
XLA Ops:
  8.5 9.0 collective-permute-done.1
  20.8 6.0 collective-permute-done.3
  35.3 11.8 %cut.1.refs_5_ = bf16[2,8,192,560]{3,2,1,0:T(8,128)(2,1)S(1)} custom-call(bf16[192,2,4480]{2,1,0:T(2,128)(2,1)S(1)} %bitcast.102), custom_call_target="tpu_custom_call" | custom-call | tf_op jit(solution)/shard_map/cut/pallas_call | solution.py:284
  49.8 17.1 %all-gather.1 = bf16[8,1,1536]{2,1,0:T(2,128)(2,1)S(1)} all-gather(bf16[1,1,1536]{2,1,0:T(2,128)(2,1)S(1)} %reshape.309), channel_id=2, replica_groups=mesh['section'=2,'tensor'=2,'ctx'=8] {'ctx'}, dimensions={0}, use_global_device_ids=true | all-gather | bytes 27648 | tf_op jit(solution)/shard_map/all_gather | solution.py:66
  71.4 3.1 convolution_add_fusion.1.refs_0_
  74.5 106.8 %attend.2 = (f32[256,768]{1,0:T(8,128)S(1)}, bf16[256,768]{1,0:T(8,128)(2,1)S(1)}, f32[256,128]{1,0:T(8,128)S(1)}, bf16[2,1024,256]{2,1,0:T(8,128)(2,1)S(1)}, bf...) custom-call(f32[256,1024]{1,0:T(8,128)S(1)} %convolution_add_fusion.1.refs_0_, ...), custom_call_target="tpu_custom_call" | custom-call | flops 262144 | bytes 256 | tf_op jit(solution)/shard_map/attend/pallas_call | solution.py:921
  189.9 5.1 collective-permute-done.4
  199.2 4.0 broadcast_select_fusion
  203.2 128.5 %mlp_forward.2 = (bf16[2048,1536]{1,0:T(8,128)(2,1)}, f32[128,1536]{1,0:T(8,128)}, bf16[2048,560]{1,0:T(8,128)(2,1)}, bf16[2048,560]{1,0:T(8,128)(2,1)}, bf16[2048,560]{1,0:T(8,128)(2,1)}) custom-call(bf16[128,1536]{1,0:T(8,128)(2,1)} %multiply_convert_fusion.3.own_ref, bf16[2,2,1536,560]{3,2,1,0:T(8,128)(2,1)} %bitcast.107, ...), custom_call_target="tpu_custom_call" | custom-call | flops 3145728 | bytes 2048 | tf_op jit(solution)/shard_map/mlp_forward/pallas_call | solution.py:553
  335.7 7.5 collective-permute-done.5
  346.9 39.7 %attend.3 = (f32[256,768]{1,0:T(8,128)S(1)}, bf16[256,768]{1,0:T(8,128)(2,1)S(1)}, f32[256,128]{1,0:T(8,128)S(1)}, bf16[2,1024,256]{2,1,0:T(8,128)(2,1)S(1)}, bf16[256,768]{1,0:T(8,128)(2,1)S(1)}) custom-call(f32[256,1024]{1,0:T(8,128)S(1)} %convolution_add_fusion.refs_0_, f32[256,128]{1,0:T(8,128)S(1)} %get-tuple-element.155.refs_1_.cosine_ref, ...), custom_call_target="tpu_custom_call" | custom-call | flops 262144 | bytes 256 | tf_op jit(solution)/shard_map/attend/pallas_call | solution.py:921
  394.7 7.8 collective-permute-done.6
  404.5 56.7 %mlp_forward.3 = (bf16[2048,1536]{1,0:T(8,128)(2,1)}, bf16[2048,1536]{1,0:T(8,128)(2,1)}, bf16[2048,560]{1,0:T(8,128)(2,1)}, bf16[2048,560]{1,0:T(8,128)(2,1)}, bf16[2048,560]{1,0:T(8,128)(2,1)}) custom-call(bf16[128,1536]{1,0:T(8,128)(2,1)} %multiply_convert_fusion.2.own_ref, bf16[2,2,1536,560]{3,2,1,0:T(8,128)(2,1)} %bitcast.108, ...), custom_call_target="tpu_custom_call" | custom-call | flops 3145728 | bytes 2048 | tf_op jit(solution)/shard_map/mlp_forward/pallas_call | solution.py:553
  461.7 98.7 %mlp_backward.2 = (bf16[16,1536]{1,0:T(8,128)(2,1)}, f32[128,1536]{1,0:T(8,128)}, bf16[2,1536,560]{2,1,0:T(8,128)(2,1)}, bf16[560,1536]{1,0:T(8,128)(2,1)}) custom-call(bf16[2048,1536]{1,0:T(8,128)(2,1)} %all-gather.16.cloned.1.call-done.own_ref, bf16[2,2,1536,560]{3,2,1,0:T(8,128)(2,1)} %bitcast.109, bf16[560,1536]{1,0:T(8,128)(2,1)} %get-tuple-element.128.refs_1_, ...), custom_call_target="tpu_custom_call" | custom-call | flops 3145728 | bytes 2048 | tf_op jit(solution)/shard_map/mlp_backward/pallas_call | solution.py:553
  562.2 10.1 %reduce-scatter.6.cloned.1.call-done = bf16[128,1536]{1,0:T(8,128)(2,1)} async-done(((bf16[2048,1536]{1,0:T(8,128)(2,1)}), bf16[128,1536]{1,0:T(8,128)(2,1)}) %reduce-scatter.6.cloned.1.call-update) | async-done | bytes 393232 | tf_op jit(solution)/shard_map/reduce_scatter | solution.py:74
  575.7 4.4 collective-permute-start.8
  580.3 3.5 collective-permute-done.7
  585.0 23.7 %attend_backward.2 = bf16[256,1024]{1,0:T(8,128)(2,1)S(1)} custom-call(bf16[256,768]{1,0:T(8,128)(2,1)S(1)} %copy-done.17, bf16[2,1024,256]{2,1,0:T(8,128)(2,1)S(1)} %get-tuple-element.66.kv_ref, s32[2,128,1]{2,1,0:T(8,128)S(1)} %copy.28.refs_3_.qpos_ref, s32[2,1,1024]{2,1,0:T(1,128)S(1)} %bitcast.105, ...), custom_call_target="tpu_custom_call" | custom-call | flops 262144 | bytes 256 | tf_op jit(solution)/shard_map/attend_backward/pallas_call | solution.py:985
  609.9 5.0 collective-permute-done.8
  624.7 5.4 collective-permute-done.10
  630.6 4.1 fusion.2
  640.6 101.5 %mlp_backward.3 = (bf16[16,1536]{1,0:T(8,128)(2,1)}, f32[128,1536]{1,0:T(8,128)}, bf16[2,1536,560]{2,1,0:T(8,128)(2,1)}, bf16[560,1536]{1,0:T(8,128)(2,1)}) custom-call(bf16[128,1536]{1,0:T(8,128)(2,1)} %copy-done.30, bf16[2,2,1536,560]{3,2,1,0:T(8,128)(2,1)} %bitcast.110, bf16[560,1536]{1,0:T(8,128)(2,1)} %get-tuple-element.129.refs_1_, ...), custom_call_target="tpu_custom_call" | custom-call | flops 3145728 | bytes 2048 | tf_op jit(solution)/shard_map/mlp_backward/pallas_call | solution.py:553
  748.2 9.8 collective-permute-done.13
  762.1 4.1 collective-permute-start.15
  770.3 38.2 %attend_backward.3 = bf16[256,1024]{1,0:T(8,128)(2,1)S(1)} custom-call(bf16[256,768]{1,0:T(8,128)(2,1)S(1)} %copy-done.15, bf16[2,1024,256]{2,1,0:T(8,128)(2,1)S(1)} %copy-done.9, s32[2,128,1]{2,1,0:T(8,128)S(1)} %copy.28.refs_3_.qpos_ref, s32[2,1,1024]{2,1,0:T(1,128)S(1)} %bitcast.106, bf16[256,768]{1,0:T(8,128)(2,1)S(1)} %convolution_convert_fusion.4.grad_ref, ...), custom_call_target="tpu_custom_call" | custom-call | flops 262144 | bytes 256 | tf_op jit(solution)/shard_map/attend_backward/pallas_call | solution.py:985
  813.9 3.9 convolution_convert_fusion.3
  821.1 4.1 fusion.3
  829.2 6.3 collective-permute-done.18
  842.2 111.4 %collect.1.blocks_ref = bf16[2,8,192,560]{3,2,1,0:T(8,128)(2,1)S(1)} custom-call(bf16[2,8,192,560]{3,2,1,0:T(8,128)(2,1)S(1)} %bitcast.101, bf16[2,8,192,560]{3,2,1,0:T(8,128)(2,1)S(1)} %bitcast.100), custom_call_target="tpu_custom_call" | custom-call | flops 1720320 | bytes 1024 | tf_op jit(solution)/shard_map/collect/pallas_call | solution.py:230
  953.6 4.7 join.1
  962.5 6.9 collective-permute-done.22
  970.4 7.0 collective-permute-done.20
  (347 shorter events, 118.2 us)
Async XLA Ops:
  7.2 64.2 %all-gather.8.cloned.1.call-start = ((), (), s32[]{:S(2)}) async-start(), calls=%async_computation.5 | async-start | bytes 3538944 | tf_op jit(solution)/shard_map/all_gather | solution.py:66
  7.2 10.3 %collective-permute-start.1 = (bf16[192,1024]{1,0:T(8,128)(2,1)}, bf16[192,1024]{1,0:T(8,128)(2,1)S(1)}, u32[]{:S(2)}, u32[]{:S(2)}) collective-permute-start(bf16[192,1024]{1,0:T(8,128)(2,1)} %bitcast.124), channel_id=1, source_target_pairs={{0,16},{16,0},{1,17},{17,1},{2,18},{18,2},{3,19},{19,3},{4,20},{20... | collective-permute-start | bytes 1179656 | tf_op jit(solution)/shard_map/ppermute | solution.py:62
  19.5 165.1 %all-gather.10.cloned.1.call-start = ((), (), s32[]{:S(2)}) async-start(), calls=%async_computation.6 | async-start | bytes 2654208 | tf_op jit(solution)/shard_map/all_gather | solution.py:66
  19.5 7.2 collective-permute-start.3
  28.6 315.2 %all-gather.12.cloned.1.call-start = ((), (), s32[]{:S(2)}) async-start(), calls=%async_computation.7 | async-start | bytes 3538944 | tf_op jit(solution)/shard_map/all_gather | solution.py:66
  29.3 19.7 %collective-permute-start = (bf16[512]{0:T(512)(128)(2,1)}, bf16[512]{0:T(512)(128)(2,1)}, u32[]{:S(2)}, u32[]{:S(2)}) collective-permute-start(bf16[512]{0:T(512)(128)(2,1)} %pad_maximum_fusion.11), channel_id=1, source_target_pairs={{0,16},{16,0},{1,17},{17,1},{2,18},{18,2},{3,19},{19,3},{4,20},{20... | collective-permute-start | bytes 3080 | tf_op jit(solution)/shard_map/ppermute | solution.py:62
  30.5 43.9 %collective-permute-start.2 = (bf16[560,1536]{1,0:T(8,128)(2,1)}, bf16[560,1536]{1,0:T(8,128)(2,1)}, u32[]{:S(2)}, u32[]{:S(2)}) collective-permute-start(bf16[560,1536]{1,0:T(8,128)(2,1)} %bitcast.121), channel_id=1, source_target_pairs={{0,16},{16,0},{1,17},{17,1},{2,18},{18,2},{3,19},{19,3},{4,20},{20... | collective-permute-start | bytes 5160968 | tf_op jit(solution)/shard_map/ppermute | solution.py:62
  188.3 6.6 collective-permute-start.4
  198.4 189.9 %all-gather.14.cloned.1.call-start = ((), (), s32[]{:S(2)}) async-start(), calls=%async_computation.8 | async-start | bytes 2654208 | tf_op jit(solution)/shard_map/all_gather | solution.py:66
  199.0 262.7 %all-gather.16.cloned.1.call-start = ((), (), s32[]{:S(2)}) async-start(), calls=%async_computation.9 | async-start | bytes 7077888 | tf_op jit(solution)/shard_map/all_gather | solution.py:66
  333.2 10.0 %collective-permute-start.5 = (bf16[128,1536]{1,0:T(8,128)(2,1)S(1)}, bf16[128,1536]{1,0:T(8,128)(2,1)S(1)}, u32[]{:S(2)}, u32[]{:S(2)}) collective-permute-start(bf16[128,1536]{1,0:T(8,128)(2,1)S(1)} %add_convert_fusion.3), channel_id=1, source_target_pairs={{0,8},{8,0},{1,9},{9,1},{2,10},{10,2},{3,11},{11,3},{4,12},{12,4},... | collective-permute-start | bytes 1179656 | tf_op jit(solution)/shard_map/ppermute | solution.py:82
  343.3 228.9 %reduce-scatter.6.cloned.1.call-start = ((), (), s32[]{:S(2)}) async-start(), calls=%async_computation.10 | async-start | bytes 6684672 | tf_op jit(solution)/shard_map/reduce_scatter | solution.py:74
  391.9 10.6 %collective-permute-start.6 = (bf16[128,1536]{1,0:T(8,128)(2,1)S(1)}, bf16[128,1536]{1,0:T(8,128)(2,1)S(1)}, u32[]{:S(2)}, u32[]{:S(2)}) collective-permute-start(bf16[128,1536]{1,0:T(8,128)(2,1)S(1)} %dynamic-slice_convert_fusion.2), channel_id=1, source_target_pairs={{0,8},{8,0},{1,9},{9,1},{2,10},{10,2},{3,11},{11,3},{4,12},{12,4},... | collective-permute-start | bytes 1179656 | tf_op jit(solution)/shard_map/ppermute | solution.py:92
  461.3 285.7 %reduce-scatter.10.cloned.1.call-start = ((), (), s32[]{:S(2)}) async-start(), calls=%async_computation.12 | async-start | bytes 2654208 | tf_op jit(solution)/shard_map/reduce_scatter | solution.py:1200
  574.1 9.6 collective-permute-start.7
  575.7 39.1 %collective-permute-start.8 = (bf16[560,1536]{1,0:T(8,128)(2,1)}, bf16[560,1536]{1,0:T(8,128)(2,1)}, u32[]{:S(2)}, u32[]{:S(2)}) collective-permute-start(bf16[560,1536]{1,0:T(8,128)(2,1)} %get-tuple-element.77), channel_id=1, source_target_pairs={{0,16},{1,17},{2,18},{3,19},{4,20},{5,21},{6,22},{7,23},{8,24},{9,... | collective-permute-start | bytes 5160968 | tf_op jit(solution)/shard_map/ppermute | solution.py:1100
  580.2 28.6 %collective-permute-start.9 = (bf16[128,1536]{1,0:T(8,128)(2,1)S(1)}, bf16[128,1536]{1,0:T(8,128)(2,1)S(1)}, u32[]{:S(2)}, u32[]{:S(2)}) collective-permute-start(bf16[128,1536]{1,0:T(8,128)(2,1)S(1)} %get-tuple-element.142), channel_id=1, source_target_pairs={{0,8},{8,0},{1,9},{9,1},{2,10},{10,2},{3,11},{11,3},{4,12},{12,4},... | collective-permute-start | bytes 1179656 | tf_op jit(solution)/shard_map/ppermute | solution.py:82
  617.1 129.8 %reduce-scatter.8.cloned.1.call-start = ((), (), s32[]{:S(2)}) async-start(), calls=%async_computation.11 | async-start | bytes 3833856 | tf_op jit(solution)/shard_map/reduce_scatter | solution.py:1200
  621.4 8.7 collective-permute-start.10
  634.7 323.6 %reduce-scatter.14.cloned.1.call-start = ((), (), s32[]{:S(2)}) async-start(), calls=%async_computation.14 | async-start | bytes 2654208 | tf_op jit(solution)/shard_map/reduce_scatter | solution.py:1200
  637.4 104.7 %collective-permute-start.12 = (bf16[128,1536]{1,0:T(8,128)(2,1)S(1)}, bf16[128,1536]{1,0:T(8,128)(2,1)}, u32[]{:S(2)}, u32[]{:S(2)}) collective-permute-start(bf16[128,1536]{1,0:T(8,128)(2,1)S(1)} %add_convert_fusion.1.own_ref), channel_id=1, source_target_pairs={{0,8},{8,0},{1,9},{9,1},{2,10},{10,2},{3,11},{11,3},{4,12},{12,4},... | collective-permute-start | bytes 1179656 | tf_op jit(solution)/shard_map/ppermute | solution.py:82
  638.4 105.9 %collective-permute-start.11 = (bf16[256,1536]{1,0:T(8,128)(2,1)}, bf16[256,1536]{1,0:T(8,128)(2,1)}, u32[]{:S(2)}, u32[]{:S(2)}) collective-permute-start(bf16[256,1536]{1,0:T(8,128)(2,1)} %broadcast_select_fusion.8), channel_id=1, source_target_pairs={{0,16},{16,0},{1,17},{17,1},{2,18},{18,2},{3,19},{19,3},{4,20},{20... | collective-permute-start | bytes 2359304 | tf_op jit(solution)/shard_map/ppermute | solution.py:62
  748.2 9.9 collective-permute-start.13
  760.4 200.7 %reduce-scatter.12.cloned.1.call-start = ((), (), s32[]{:S(2)}) async-start(), calls=%async_computation.13 | async-start | bytes 3833856 | tf_op jit(solution)/shard_map/reduce_scatter | solution.py:1200
  760.5 48.0 %collective-permute-start.14 = (bf16[560,1536]{1,0:T(8,128)(2,1)}, bf16[560,1536]{1,0:T(8,128)(2,1)S(1)}, u32[]{:S(2)}, u32[]{:S(2)}) collective-permute-start(bf16[560,1536]{1,0:T(8,128)(2,1)} %get-tuple-element.93), channel_id=1, source_target_pairs={{16,0},{17,1},{18,2},{19,3},{20,4},{21,5},{22,6},{23,7},{24,8},{25... | collective-permute-start | bytes 5160968 | tf_op jit(solution)/shard_map/ppermute | solution.py:1100
  762.1 46.5 %collective-permute-start.15 = (bf16[208,1024]{1,0:T(8,128)(2,1)S(1)}, bf16[208,1024]{1,0:T(8,128)(2,1)S(1)}, u32[]{:S(2)}, u32[]{:S(2)}) collective-permute-start(bf16[208,1024]{1,0:T(8,128)(2,1)S(1)} %copy-done.55), channel_id=1, source_target_pairs={{0,16},{1,17},{2,18},{3,19},{4,20},{5,21},{6,22},{7,23},{8,24},{9,... | collective-permute-start | bytes 1277960 | tf_op jit(solution)/shard_map/ppermute | solution.py:1099
  766.2 42.3 %collective-permute-start.16 = (bf16[96,1536]{1,0:T(8,128)(2,1)S(1)}, bf16[96,1536]{1,0:T(8,128)(2,1)S(1)}, u32[]{:S(2)}, u32[]{:S(2)}) collective-permute-start(bf16[96,1536]{1,0:T(8,128)(2,1)S(1)} %copy-done.60), channel_id=1, source_target_pairs={{0,16},{1,17},{2,18},{3,19},{4,20},{5,21},{6,22},{7,23},{8,24},{9,... | collective-permute-start | bytes 884744 | tf_op jit(solution)/shard_map/ppermute | solution.py:1099
  811.9 8.2 collective-permute-start.17
  828.4 7.1 collective-permute-start.18
  835.8 123.8 %collective-permute-start.19 = (bf16[256,1536]{1,0:T(8,128)(2,1)S(1)}, bf16[256,1536]{1,0:T(8,128)(2,1)S(1)}, u32[]{:S(2)}, u32[]{:S(2)}) collective-permute-start(bf16[256,1536]{1,0:T(8,128)(2,1)S(1)} %broadcast_select_fusion.4), channel_id=1, source_target_pairs={{0,16},{16,0},{1,17},{17,1},{2,18},{18,2},{3,19},{19,3},{4,20},{20... | collective-permute-start | bytes 2359304 | tf_op jit(solution)/shard_map/ppermute | solution.py:62
  958.3 11.1 %collective-permute-start.22 = (bf16[96,1536]{1,0:T(8,128)(2,1)}, bf16[96,1536]{1,0:T(8,128)(2,1)S(1)}, u32[]{:S(2)}, u32[]{:S(2)}) collective-permute-start(bf16[96,1536]{1,0:T(8,128)(2,1)} %reduce-scatter.14.cloned.1.call-done), channel_id=1, source_target_pairs={{16,0},{17,1},{18,2},{19,3},{20,4},{21,5},{22,6},{23,7},{24,8},{25... | collective-permute-start | bytes 884744 | tf_op jit(solution)/shard_map/ppermute | solution.py:1235
  961.1 16.3 %collective-permute-start.20 = (bf16[208,1024]{1,0:T(8,128)(2,1)}, bf16[208,1024]{1,0:T(8,128)(2,1)S(1)}, u32[]{:S(2)}, u32[]{:S(2)}) collective-permute-start(bf16[208,1024]{1,0:T(8,128)(2,1)} %reduce-scatter.12.cloned.1.call-done), channel_id=1, source_target_pairs={{16,0},{17,1},{18,2},{19,3},{20,4},{21,5},{22,6},{23,7},{24,8},{25... | collective-permute-start | bytes 1277960 | tf_op jit(solution)/shard_map/ppermute | solution.py:1235
  (88 other events, 1040.9 us)
Sparse Core Ops, SparseCore 0:
  19.6 39.8 all-gather.7
  61.6 42.5 all-gather.9
  198.5 63.3 all-gather.11
  264.0 35.8 all-gather.13
  343.5 76.0 all-gather.15
  461.4 110.8 reduce-scatter.5
  617.2 32.4 reduce-scatter.9
  652.7 61.1 reduce-scatter.7
  760.5 53.4 reduce-scatter.13
  825.4 71.8 reduce-scatter.11
